TPU v7x, 128 devices: a whole 4x4x4 slice. The times are simulated.
128 devices in a mesh: gx: 8 (over x, core), gy: 16 (over y, z).
Axes of the slice: x: 4, y: 4, z: 4, core: 2. Of those that a mesh axis runs over, the one named last changes fastest.
Arguments:
- features: bfloat16 [16, 32, 16, 512, 128], P('gx', 'gy'), may hold values from -6 to 6
- owner: int32 [16, 32, 16], P('gx', 'gy'), may hold values from -1 to 255, as said below
- norm_gain: float32 [8, 128], replicated, may hold values from 0.1 to 1.9
- time_shift: float32 [8, 512], replicated, may hold values from -4 to 4
- w_in: bfloat16 [8, 128, 512], replicated, may hold values from -0.5 to 0.5
- w_out: bfloat16 [8, 512, 128], replicated, may hold values from -0.25 to 0.25
- w_down: bfloat16 [2, 2, 2, 128, 128], replicated, may hold values from -0.1875 to 0.1875
- w_conv: bfloat16 [3, 3, 3, 128, 128], replicated, may hold values from -0.109375 to 0.109375
- w_up: bfloat16 [2, 2, 2, 128, 128], replicated, may hold values from -0.5 to 0.5
Outputs:
- denoised: bfloat16 [16, 32, 16, 512, 128], P('gx', 'gy')
Inputs may be any that keep to these rules, and one draw needn't show every extreme that they name: Within each gx index and gy group, every owner along gy gets exactly 16 bricks, one in each compute slot; at most 2 bricks of one device go to one owner, and some device sends 2 to some owner; a device holds at most 32 occupied bricks, and some device holds exactly that many.
All inputs are finite; a program needn't handle non-finite values.
Results may differ from a plain program's by a relative error of at most 0.029.
Values may be sent and summed in bfloat16 or wider, within the bound.
A program may use at most 192 MiB of HBM per device.

v0:
```python
import math

import jax
import jax.numpy as jnp
from jax import lax
from jax.sharding import PartitionSpec as P

LOAD = 16


def extended(cells, sides, width):
    for axis, dim in sides:
        count = lax.axis_size(axis)
        ends = count - 1
        head = lax.slice_in_dim(cells, 0, width, axis=dim)
        tail = lax.slice_in_dim(cells, cells.shape[dim] - width, cells.shape[dim], axis=dim)
        cells = jnp.concatenate(
            [
                lax.ppermute(tail, axis, [(i, (i + 1) % count) for i in range(ends)]),
                cells,
                lax.ppermute(head, axis, [((i + 1) % count, i) for i in range(ends)]),
            ],
            axis=dim,
        )
    return cells


def brick_down(bricks, live, norm_gain, time_shift, w_in, w_out, w_down):
    count, voxels, chan = bricks.shape
    stream = bricks.reshape(-1, chan)
    for layer in range(w_in.shape[0]):
        whole = stream.astype(jnp.float32)
        scale = lax.rsqrt(jnp.mean(whole * whole, axis=-1, keepdims=True) + 1e-06)
        normed = (whole * scale * norm_gain[layer]).astype(jnp.bfloat16)
        hidden = jax.nn.silu(
            jnp.dot(normed, w_in[layer], preferred_element_type=jnp.float32) + time_shift[layer]
        ).astype(jnp.bfloat16)
        stream = (whole + jnp.dot(hidden, w_out[layer], preferred_element_type=jnp.float32)).astype(
            jnp.bfloat16
        )
    cells = stream.reshape(count, 4, 2, 4, 2, 4, 2, chan)
    down = jnp.einsum("giajbkcd,abcde->gijke", cells, w_down, preferred_element_type=jnp.float32)
    return (jax.nn.silu(down).reshape(count, 64, chan) * live[:, None, None]).astype(jnp.bfloat16)


def brick_up(bricks, mixed, live, w_up):
    count, voxels, chan = bricks.shape
    coarse = mixed.reshape(count, 4, 4, 4, chan)
    upward = jnp.einsum(
        "gijkd,abcde->giajbkce", coarse, w_up, preferred_element_type=jnp.float32
    ).reshape(count, voxels, chan)
    return ((bricks.astype(jnp.float32) + upward) * live[:, None, None]).astype(jnp.bfloat16)


def blockwise(func, count, arrays):
    block = math.gcd(count, 8)
    shaped = tuple((a.reshape((count // block, block) + a.shape[1:]) for a in arrays))
    result = lax.map(lambda group: func(*group), shaped)
    return result.reshape((count,) + result.shape[2:])


def local(features, owner, norm_gain, time_shift, w_in, w_out, w_down, w_conv, w_up):
    cols_x, cols_y, zcap, voxels, chan = features.shape
    slots = cols_x * cols_y * zcap
    flat = features.reshape(slots, voxels, chan)
    code = owner.reshape(slots)
    alive = code >= 0
    live = alive.astype(jnp.float32)

    def reduce_bricks(bricks, marks):
        return brick_down(bricks, marks, norm_gain, time_shift, w_in, w_out, w_down)

    width = lax.axis_size("gy")
    cap = (2 * LOAD + width - 1) // width
    dest = jnp.where(alive, code // LOAD, -1)
    target = jnp.where(alive, code % LOAD, -1)
    order = jnp.arange(slots, dtype=jnp.int32)
    earlier = (dest[:, None] == dest[None, :]) & alive[None, :] & (order[None, :] < order[:, None])
    rank = jnp.sum(earlier.astype(jnp.int32), axis=1)
    position = jnp.where(alive, dest * cap + rank, -1)
    picker = position[None, :] == jnp.arange(width * cap, dtype=jnp.int32)[:, None]
    picker_bf = picker.astype(jnp.bfloat16)
    packed = jnp.dot(
        picker_bf, flat.reshape(slots, voxels * chan), preferred_element_type=jnp.float32
    ).astype(jnp.bfloat16)
    labels = jnp.max(jnp.where(picker, target[None, :], -1), axis=1).astype(jnp.bfloat16)
    arrived, arrived_labels = (
        lax.all_to_all(
            packed.reshape(width, cap, voxels * chan), "gy", split_axis=0, concat_axis=0, tiled=True
        ),
        lax.all_to_all(labels.reshape(width, cap), "gy", split_axis=0, concat_axis=0, tiled=True),
    )
    slot_of = arrived_labels.reshape(width * cap).astype(jnp.int32)
    placer = (slot_of[None, :] == jnp.arange(LOAD, dtype=jnp.int32)[:, None]).astype(jnp.bfloat16)
    compact = jnp.dot(
        placer, arrived.reshape(width * cap, voxels * chan), preferred_element_type=jnp.float32
    ).astype(jnp.bfloat16)
    made = blockwise(
        reduce_bricks, LOAD, (compact.reshape(LOAD, voxels, chan), jnp.ones((LOAD,), jnp.float32))
    )
    returned = jnp.dot(
        placer.T, made.reshape(LOAD, 64 * chan), preferred_element_type=jnp.float32
    ).astype(jnp.bfloat16)
    home = lax.all_to_all(
        returned.reshape(width, cap, 64 * chan), "gy", split_axis=0, concat_axis=0, tiled=True
    )
    coarse_slots = jnp.dot(
        picker_bf.T, home.reshape(width * cap, 64 * chan), preferred_element_type=jnp.float32
    ).astype(jnp.bfloat16)
    gsx, gsy, gsz = (cols_x * 4, cols_y * 4, zcap * 4)
    grid = (
        coarse_slots.reshape(cols_x, cols_y, zcap, 4, 4, 4, chan)
        .transpose(0, 3, 1, 4, 2, 5, 6)
        .reshape(gsx, gsy, gsz, chan)
    )
    rimmed = extended(grid, (("gx", 0), ("gy", 1)), 1)
    padded = jnp.pad(rimmed, ((0, 0), (0, 0), (1, 1), (0, 0)))
    total = grid.astype(jnp.float32)
    for d in range(3):
        for e in range(3):
            for f in range(3):
                moved = padded[d : d + gsx, e : e + gsy, f : f + gsz].reshape(-1, chan)
                total = total + jnp.dot(
                    moved, w_conv[d, e, f], preferred_element_type=jnp.float32
                ).reshape(total.shape)
    live_grid = jnp.broadcast_to(
        live.reshape(cols_x, 1, cols_y, 1, zcap, 1, 1), (cols_x, 4, cols_y, 4, zcap, 4, 1)
    ).reshape(gsx, gsy, gsz, 1)
    mixed = (total * live_grid).astype(jnp.bfloat16)
    mixed = (
        mixed.reshape(cols_x, 4, cols_y, 4, zcap, 4, chan)
        .transpose(0, 2, 4, 1, 3, 5, 6)
        .reshape(slots, 64, chan)
    )

    def lift_bricks(bricks, coarse, marks):
        return brick_up(bricks, coarse, marks, w_up)

    result = blockwise(lift_bricks, slots, (flat, mixed, live))
    return result.reshape(cols_x, cols_y, zcap, voxels, chan)


def solution(mesh):
    in_specs = (
        P("gx", "gy", None, None, None),
        P("gx", "gy", None),
        P(),
        P(),
        P(),
        P(),
        P(),
        P(),
        P(),
    )
    out_specs = P("gx", "gy", None, None, None)
    return jax.shard_map(local, mesh=mesh, in_specs=in_specs, out_specs=out_specs, check_vma=False)
```

profile of v0, /device:TPU:9, one launch (start us, length us, event | category | flops | bytes accessed | tf_op | source)
XLA Modules:
  0.0 358.0 jit_solution(11128736410081705150)
XLA Ops:
  1.8 7.8 %all-to-all-start = ((bf16[16,1,2]{2,1,0:T(2,128)(2,1)}), bf16[16,1,2]{2,1,0:T(2,128)(2,1)S(1)}, u32[]{:S(2)}, u32[]{:S(2)}) async-start(bf16[16,1,2]{2,1,0:T(2,128)(2,1)} %convert_element_type.204), calls=%async_computation | async-start | bytes 16384 | tf_op jit(solution)/shard_map/all_to_all | solution.py:91
  9.7 11.1 %convolution_convert_fusion = bf16[32,65536]{1,0:T(8,128)(2,1)} fusion(bf16[8,8,512,128]{3,2,1,0:T(8,128)(2,1)} %bitcast.448, s32[64]{0:T(128)S(1)} %get-tuple-element.208), kind=kOutput, calls=%fused_computation.132 | convolution fusion | flops 270534656 | bytes 12583168 | tf_op jit(solution)/shard_map/dot_general | solution.py:83
  20.8 5.9 %reshape.392 = bf16[16,2,65536]{2,1,0:T(2,128)(2,1)} reshape(bf16[32,65536]{1,0:T(8,128)(2,1)} %convolution_convert_fusion) | data formatting | bytes 8388608 | tf_op jit(solution)/shard_map/reshape | solution.py:89
  26.7 6.7 %all-to-all-start.1 = ((bf16[16,2,65536]{2,1,0:T(2,128)(2,1)}), bf16[16,2,65536]{2,1,0:T(2,128)(2,1)}, u32[]{:S(2)}, u32[]{:S(2)}) async-start(bf16[16,2,65536]{2,1,0:T(2,128)(2,1)} %reshape.392), calls=%async_computation.1 | async-start | bytes 8388608 | tf_op jit(solution)/shard_map/all_to_all | solution.py:88
  33.5 50.2 %all-to-all-done.1 = bf16[16,2,65536]{2,1,0:T(2,128)(2,1)} async-done(((bf16[16,2,65536]{2,1,0:T(2,128)(2,1)}), bf16[16,2,65536]{2,1,0:T(2,128)(2,1)}, u32[]{:S(2)}, u32[]{:S(2)}) %all-to-all-start.1) | async-done | bytes 4194336 | tf_op jit(solution)/shard_map/all_to_all | solution.py:88
  83.6 5.4 %reshape.393 = bf16[32,65536]{1,0:T(8,128)(2,1)} reshape(bf16[16,2,65536]{2,1,0:T(2,128)(2,1)} %all-to-all-done.1) | data formatting | bytes 8388608 | tf_op jit(solution)/shard_map/reshape | solution.py:96
  89.0 2.9 fusion.115
  92.0 122.4 %while.20 = (s32[]{:T(128)}, bf16[2,8,64,128]{3,1,2,0:T(8,128)(2,1)S(1)}, bf16[2,8,512,128]{3,1,2,0:T(8,128)(2,1)S(1)}, f32[8,128]{1,0:T(8,128)S(1)}, bf16[8,128...) while((s32[]{:T(128)}, ...), condition=%wide.region_11.12_spmd, body=%wide.region_2.11_spmd.sunk | while | flops 8859779072 | bytes 78835896 | solution.py:58
  112.8 5.7 %multiply_reduce_fusion.17 = (f32[4096]{0:T(1024)S(1)}, f32[4096,128]{1,0:T(8,128)}) fusion(f32[4096,128]{1,0:T(8,128)S(1)} %bitcast.446, bf16[8,512,128]{2,1,0:T(8,128)(2,1)} %get-tuple-element.379, bf16[4096,128]{1,0:T(8,128)(2,1)S(1)} %bitcast.447, f32[512]{0:T(512)S(1)} %bitcast.462, bf16[8,128,512]{2,1,0:T(8,128)(2,1)} %get-tuple-element.377), kind=kOutput, calls=%fused_computation.44.clone.1 | convolution fusion | flops 1088942080 | bytes 5523456 | tf_op jit(solution)/shard_map/while/body/eval_jaxpr/dot_general | solution.py:38
  118.5 5.9 %multiply_reduce_fusion.18 = (f32[4096]{0:T(1024)S(1)}, f32[4096,128]{1,0:T(8,128)S(1)}) fusion(f32[4096,128]{1,0:T(8,128)} %get-tuple-element.321, bf16[8,512,128]{2,1,0:T(8,128)(2,1)} %get-tuple-element.379, f32[512]{0:T(512)S(1)} %bitcast.461, f32[128]{0:T(128)S(1)} %get-tuple-element.323, f32[4096]{0:T(1024)S(1)} %add_rsqrt_fusion.17, ...), kind=kOutput, calls=%fused_computation.42.clone.1 | convolution fusion | flops 1090514944 | bytes 6588928 | tf_op jit(solution)/shard_map/while/body/eval_jaxpr/dot_general | solution.py:38
  124.5 5.8 %multiply_reduce_fusion.19 = (f32[4096]{0:T(1024)S(1)}, f32[4096,128]{1,0:T(8,128)}) fusion(f32[4096,128]{1,0:T(8,128)S(1)} %get-tuple-element.325, bf16[8,512,128]{2,1,0:T(8,128)(2,1)} %get-tuple-element.379, f32[512]{0:T(512)S(1)} %bitcast.460, f32[128]{0:T(128)S(1)} %get-tuple-element.327, f32[4096]{0:T(1024)S(1)} %add_rsqrt_fusion.18, ...), kind=kOutput, calls=%fused_computation.40.clone.1 | convolution fusion | flops 1090514944 | bytes 6588928 | tf_op jit(solution)/shard_map/while/body/eval_jaxpr/dot_general | solution.py:38
  130.3 5.9 %multiply_reduce_fusion.20 = (f32[4096]{0:T(1024)S(1)}, f32[4096,128]{1,0:T(8,128)S(1)}) fusion(f32[4096,128]{1,0:T(8,128)} %get-tuple-element.329, bf16[8,512,128]{2,1,0:T(8,128)(2,1)} %get-tuple-element.379, f32[512]{0:T(512)S(1)} %bitcast.459, f32[128]{0:T(128)S(1)} %get-tuple-element.331, f32[4096]{0:T(1024)S(1)} %add_rsqrt_fusion.19, ...), kind=kOutput, calls=%fused_computation.38.clone.1 | convolution fusion | flops 1090514944 | bytes 6588928 | tf_op jit(solution)/shard_map/while/body/eval_jaxpr/dot_general | solution.py:38
  136.2 5.8 %multiply_reduce_fusion.21 = (f32[4096]{0:T(1024)S(1)}, f32[4096,128]{1,0:T(8,128)}) fusion(f32[4096,128]{1,0:T(8,128)S(1)} %get-tuple-element.333, bf16[8,512,128]{2,1,0:T(8,128)(2,1)} %get-tuple-element.379, f32[512]{0:T(512)S(1)} %bitcast.458, f32[128]{0:T(128)S(1)} %get-tuple-element.335, f32[4096]{0:T(1024)S(1)} %add_rsqrt_fusion.20, ...), kind=kOutput, calls=%fused_computation.36.clone.1 | convolution fusion | flops 1090514944 | bytes 6588928 | tf_op jit(solution)/shard_map/while/body/eval_jaxpr/dot_general | solution.py:38
  142.0 5.9 %multiply_reduce_fusion.22 = (f32[4096]{0:T(1024)S(1)}, f32[4096,128]{1,0:T(8,128)S(1)}) fusion(f32[4096,128]{1,0:T(8,128)} %get-tuple-element.337, bf16[8,512,128]{2,1,0:T(8,128)(2,1)} %get-tuple-element.379, f32[512]{0:T(512)S(1)} %bitcast.457, f32[128]{0:T(128)S(1)} %get-tuple-element.339, f32[4096]{0:T(1024)S(1)} %add_rsqrt_fusion.21, ...), kind=kOutput, calls=%fused_computation.34.clone.1 | convolution fusion | flops 1090514944 | bytes 6588928 | tf_op jit(solution)/shard_map/while/body/eval_jaxpr/dot_general | solution.py:38
  148.0 5.8 %multiply_reduce_fusion.23 = (f32[4096]{0:T(1024)S(1)}, f32[4096,128]{1,0:T(8,128)}) fusion(f32[4096,128]{1,0:T(8,128)S(1)} %get-tuple-element.341, bf16[8,512,128]{2,1,0:T(8,128)(2,1)} %get-tuple-element.379, f32[512]{0:T(512)S(1)} %bitcast.456, f32[128]{0:T(128)S(1)} %get-tuple-element.343, f32[4096]{0:T(1024)S(1)} %add_rsqrt_fusion.22, ...), kind=kOutput, calls=%fused_computation.32.clone.1 | convolution fusion | flops 1090514944 | bytes 6588928 | tf_op jit(solution)/shard_map/while/body/eval_jaxpr/dot_general | solution.py:38
  153.8 6.6 %fusion.284 = bf16[4096,128]{1,0:T(8,128)(2,1)} fusion(f32[4096,128]{1,0:T(8,128)} %get-tuple-element.345, f32[512]{0:T(512)S(1)} %bitcast.455, f32[128]{0:T(128)S(1)} %get-tuple-element.347, f32[4096]{0:T(1024)S(1)} %add_rsqrt_fusion.23, bf16[8,512,128]{2,1,0:T(8,128)(2,1)} %get-tuple-element.379, bf16[8,128,512]{2,1,0:T(8,128)(2,1)} %get-tuple-element.377), kind=kOutput, calls=%fused_computation.30.clone.1 | convolution fusion | flops 1088946176 | bytes 5523968 | tf_op jit(solution)/shard_map/while/body/eval_jaxpr/dot_general | solution.py:38
  164.2 5.7 %multiply_reduce_fusion.17 = (f32[4096]{0:T(1024)S(1)}, f32[4096,128]{1,0:T(8,128)}) fusion(f32[4096,128]{1,0:T(8,128)S(1)} %bitcast.446, bf16[8,512,128]{2,1,0:T(8,128)(2,1)} %get-tuple-element.379, bf16[4096,128]{1,0:T(8,128)(2,1)S(1)} %bitcast.447, f32[512]{0:T(512)S(1)} %bitcast.462, bf16[8,128,512]{2,1,0:T(8,128)(2,1)} %get-tuple-element.377), kind=kOutput, calls=%fused_computation.44.clone.1 | convolution fusion | flops 1088942080 | bytes 5523456 | tf_op jit(solution)/shard_map/while/body/eval_jaxpr/dot_general | solution.py:38
  169.9 5.9 %multiply_reduce_fusion.18 = (f32[4096]{0:T(1024)S(1)}, f32[4096,128]{1,0:T(8,128)S(1)}) fusion(f32[4096,128]{1,0:T(8,128)} %get-tuple-element.321, bf16[8,512,128]{2,1,0:T(8,128)(2,1)} %get-tuple-element.379, f32[512]{0:T(512)S(1)} %bitcast.461, f32[128]{0:T(128)S(1)} %get-tuple-element.323, f32[4096]{0:T(1024)S(1)} %add_rsqrt_fusion.17, ...), kind=kOutput, calls=%fused_computation.42.clone.1 | convolution fusion | flops 1090514944 | bytes 6588928 | tf_op jit(solution)/shard_map/while/body/eval_jaxpr/dot_general | solution.py:38
  175.9 5.8 %multiply_reduce_fusion.19 = (f32[4096]{0:T(1024)S(1)}, f32[4096,128]{1,0:T(8,128)}) fusion(f32[4096,128]{1,0:T(8,128)S(1)} %get-tuple-element.325, bf16[8,512,128]{2,1,0:T(8,128)(2,1)} %get-tuple-element.379, f32[512]{0:T(512)S(1)} %bitcast.460, f32[128]{0:T(128)S(1)} %get-tuple-element.327, f32[4096]{0:T(1024)S(1)} %add_rsqrt_fusion.18, ...), kind=kOutput, calls=%fused_computation.40.clone.1 | convolution fusion | flops 1090514944 | bytes 6588928 | tf_op jit(solution)/shard_map/while/body/eval_jaxpr/dot_general | solution.py:38
  181.7 5.9 %multiply_reduce_fusion.20 = (f32[4096]{0:T(1024)S(1)}, f32[4096,128]{1,0:T(8,128)S(1)}) fusion(f32[4096,128]{1,0:T(8,128)} %get-tuple-element.329, bf16[8,512,128]{2,1,0:T(8,128)(2,1)} %get-tuple-element.379, f32[512]{0:T(512)S(1)} %bitcast.459, f32[128]{0:T(128)S(1)} %get-tuple-element.331, f32[4096]{0:T(1024)S(1)} %add_rsqrt_fusion.19, ...), kind=kOutput, calls=%fused_computation.38.clone.1 | convolution fusion | flops 1090514944 | bytes 6588928 | tf_op jit(solution)/shard_map/while/body/eval_jaxpr/dot_general | solution.py:38
  187.6 5.8 %multiply_reduce_fusion.21 = (f32[4096]{0:T(1024)S(1)}, f32[4096,128]{1,0:T(8,128)}) fusion(f32[4096,128]{1,0:T(8,128)S(1)} %get-tuple-element.333, bf16[8,512,128]{2,1,0:T(8,128)(2,1)} %get-tuple-element.379, f32[512]{0:T(512)S(1)} %bitcast.458, f32[128]{0:T(128)S(1)} %get-tuple-element.335, f32[4096]{0:T(1024)S(1)} %add_rsqrt_fusion.20, ...), kind=kOutput, calls=%fused_computation.36.clone.1 | convolution fusion | flops 1090514944 | bytes 6588928 | tf_op jit(solution)/shard_map/while/body/eval_jaxpr/dot_general | solution.py:38
  193.4 5.9 %multiply_reduce_fusion.22 = (f32[4096]{0:T(1024)S(1)}, f32[4096,128]{1,0:T(8,128)S(1)}) fusion(f32[4096,128]{1,0:T(8,128)} %get-tuple-element.337, bf16[8,512,128]{2,1,0:T(8,128)(2,1)} %get-tuple-element.379, f32[512]{0:T(512)S(1)} %bitcast.457, f32[128]{0:T(128)S(1)} %get-tuple-element.339, f32[4096]{0:T(1024)S(1)} %add_rsqrt_fusion.21, ...), kind=kOutput, calls=%fused_computation.34.clone.1 | convolution fusion | flops 1090514944 | bytes 6588928 | tf_op jit(solution)/shard_map/while/body/eval_jaxpr/dot_general | solution.py:38
  199.4 5.8 %multiply_reduce_fusion.23 = (f32[4096]{0:T(1024)S(1)}, f32[4096,128]{1,0:T(8,128)}) fusion(f32[4096,128]{1,0:T(8,128)S(1)} %get-tuple-element.341, bf16[8,512,128]{2,1,0:T(8,128)(2,1)} %get-tuple-element.379, f32[512]{0:T(512)S(1)} %bitcast.456, f32[128]{0:T(128)S(1)} %get-tuple-element.343, f32[4096]{0:T(1024)S(1)} %add_rsqrt_fusion.22, ...), kind=kOutput, calls=%fused_computation.32.clone.1 | convolution fusion | flops 1090514944 | bytes 6588928 | tf_op jit(solution)/shard_map/while/body/eval_jaxpr/dot_general | solution.py:38
  205.2 6.6 %fusion.284 = bf16[4096,128]{1,0:T(8,128)(2,1)} fusion(f32[4096,128]{1,0:T(8,128)} %get-tuple-element.345, f32[512]{0:T(512)S(1)} %bitcast.455, f32[128]{0:T(128)S(1)} %get-tuple-element.347, f32[4096]{0:T(1024)S(1)} %add_rsqrt_fusion.23, bf16[8,512,128]{2,1,0:T(8,128)(2,1)} %get-tuple-element.379, bf16[8,128,512]{2,1,0:T(8,128)(2,1)} %get-tuple-element.377), kind=kOutput, calls=%fused_computation.30.clone.1 | convolution fusion | flops 1088946176 | bytes 5523968 | tf_op jit(solution)/shard_map/while/body/eval_jaxpr/dot_general | solution.py:38
  215.9 12.9 %all-to-all-start.2 = ((bf16[16,2,8192]{2,1,0:T(2,128)(2,1)}), bf16[16,2,8192]{2,1,0:T(2,128)(2,1)S(1)}, u32[]{:S(2)}, u32[]{:S(2)}) async-start(bf16[16,2,8192]{2,1,0:T(2,128)(2,1)} %reshape.394), calls=%async_computation.2 | async-start | bytes 1048576 | tf_op jit(solution)/shard_map/all_to_all | solution.py:104
  229.2 6.6 %all-to-all-done.2 = bf16[16,2,8192]{2,1,0:T(2,128)(2,1)S(1)} async-done(((bf16[16,2,8192]{2,1,0:T(2,128)(2,1)}), bf16[16,2,8192]{2,1,0:T(2,128)(2,1)S(1)}, u32[]{:S(2)}, u32[]{:S(2)}) %all-to-all-start.2) | async-done | bytes 524320 | tf_op jit(solution)/shard_map/all_to_all | solution.py:104
  237.8 7.1 %collective-permute-start = (bf16[1,8,64,128]{3,2,1,0:T(8,128)(2,1)S(1)}, bf16[1,8,64,128]{3,2,1,0:T(8,128)(2,1)S(1)}, u32[]{:S(2)}, u32[]{:S(2)}) collective-permute-start(bf16[1,8,64,128]{3,2,1,0:T(8,128)(2,1)S(1)} %get-tuple-element.205), channel_id=1, source_target_pairs={{0,16},{16,32},{32,48},{48,64},{64,80},{80,96},{96,112},{1,17},{17... | collective-permute-start | bytes 393224 | tf_op jit(solution)/shard_map/ppermute | solution.py:19
  246.9 2.5 fusion.179
  253.4 5.3 %collective-permute-start.3 = (bf16[10,1,64,128]{3,2,1,0:T(8,128)(2,1)S(1)}, bf16[10,1,64,128]{3,2,1,0:T(8,128)(2,1)S(1)}, u32[]{:S(2)}, u32[]{:S(2)}) collective-permute-start(bf16[10,1,64,128]{3,2,1,0:T(8,128)(2,1)S(1)} %get-tuple-element.204), channel_id=1, source_target_pairs={{1,0},{2,1},{3,2},{4,3},{5,4},{6,5},{7,6},{8,7},{9,8},{10,9},{11,1... | collective-permute-start | bytes 491528 | tf_op jit(solution)/shard_map/ppermute | solution.py:21
  261.2 2.5 fusion.120
  305.8 19.0 %multiply_convert_fusion.32 = bf16[8,8,64,128]{3,2,1,0:T(8,128)(2,1)} fusion(f32[8,8,64,128]{3,2,1,0:T(8,128)} %fusion.164, f32[8,8,64,128]{3,2,1,0:T(8,128)} %fusion.128, f32[8,8,64,128]{3,2,1,0:T(8,128)} %fusion.130, f32[8,8,64,128]{3,2,1,0:T(8,128)} %fusion.120, f32[8,8,64,128]{3,2,1,0:T(8,128)} %fusion.132, f32[8,8,64,128]{3,2,1,0:T(8,128)} %fusion.134, ...), kind=kOutput, calls=%fused_computation.141 | convolution fusion | flops 149946368 | bytes 57737216 | tf_op jit(solution)/shard_map/dot_general | solution.py:123
  326.3 31.5 %while.21 = (s32[]{:T(128)}, bf16[8,8,512,128]{3,2,1,0:T(8,128)(2,1)}, bf16[8,8,512,128]{3,2,1,0:T(8,128)(2,1)}, bf16[8,8,64,128]{3,1,0,2:T(8,128)(2,1)S(1)}, bf...) while((s32[]{:T(128)}, bf16[8,8,512,128]{3,2,1,0:T(8,128)(2,1)}, ...), condition=%wide.region_13.14_spmd, body=%wide.region_12.13_spmd.sunk | while | flops 136314880 | bytes 15336121 | solution.py:58
  (175 shorter events, 96.5 us)
Async XLA Ops:
  1.0 19.8 %copy-start.7 = (s32[64]{0:T(128)}, s32[64]{0:T(128)S(1)}, u32[]{:S(2)}) copy-start(s32[64]{0:T(128)S(1)} %get-tuple-element.208) | copy-start | bytes 772
  1.8 24.8 %all-to-all-start = ((bf16[16,1,2]{2,1,0:T(2,128)(2,1)}), bf16[16,1,2]{2,1,0:T(2,128)(2,1)S(1)}, u32[]{:S(2)}, u32[]{:S(2)}) async-start(bf16[16,1,2]{2,1,0:T(2,128)(2,1)} %convert_element_type.204), calls=%async_computation | async-start | bytes 16384 | tf_op jit(solution)/shard_map/all_to_all | solution.py:91
  26.7 57.0 %all-to-all-start.1 = ((bf16[16,2,65536]{2,1,0:T(2,128)(2,1)}), bf16[16,2,65536]{2,1,0:T(2,128)(2,1)}, u32[]{:S(2)}, u32[]{:S(2)}) async-start(bf16[16,2,65536]{2,1,0:T(2,128)(2,1)} %reshape.392), calls=%async_computation.1 | async-start | bytes 8388608 | tf_op jit(solution)/shard_map/all_to_all | solution.py:88
  33.5 55.6 %copy-start.9 = (s32[32]{0:T(128)}, s32[32]{0:T(128)S(1)}, u32[]{:S(2)}) copy-start(s32[32]{0:T(128)S(1)} %reshape.400) | copy-start | bytes 388
  89.0 2.9 copy-start.4
  89.0 2.9 copy-start.5
  92.0 122.4 %copy-start.10 = (s32[32]{0:T(128)S(1)}, s32[32]{0:T(128)}, u32[]{:S(2)}) copy-start(s32[32]{0:T(128)} %copy-done.9) | copy-start | bytes 388
  111.2 1.5 copy-start
  153.8 6.6 %copy-start.11 = (bf16[2,2,2,128,128]{4,3,2,1,0:T(8,128)(2,1)S(1)}, bf16[2,2,2,128,128]{4,3,2,1,0:T(8,128)(2,1)}, u32[]{:S(2)}) copy-start(bf16[2,2,2,128,128]{4,3,2,1,0:T(8,128)(2,1)} %get-tuple-element.380) | copy-start | bytes 786436 | tf_op jit(solution)/shard_map/while
  160.4 2.1 copy-start.1
  162.6 1.5 copy-start
  205.2 6.6 %copy-start.11 = (bf16[2,2,2,128,128]{4,3,2,1,0:T(8,128)(2,1)S(1)}, bf16[2,2,2,128,128]{4,3,2,1,0:T(8,128)(2,1)}, u32[]{:S(2)}) copy-start(bf16[2,2,2,128,128]{4,3,2,1,0:T(8,128)(2,1)} %get-tuple-element.380) | copy-start | bytes 786436 | tf_op jit(solution)/shard_map/while
  211.8 2.1 copy-start.1
  214.3 14.4 %copy-start.6 = (s32[2,2,16]{2,1,0:T(2,128)S(1)}, s32[2,2,16]{2,1,0:T(2,128)}, u32[]{:S(2)}) copy-start(s32[2,2,16]{2,1,0:T(2,128)} %param.14) | copy-start | bytes 772
  214.7 21.3 %copy-start.8 = (s32[64]{0:T(128)S(1)}, s32[64]{0:T(128)}, u32[]{:S(2)}) copy-start(s32[64]{0:T(128)} %copy-done.7) | copy-start | bytes 772
  215.9 19.9 %all-to-all-start.2 = ((bf16[16,2,8192]{2,1,0:T(2,128)(2,1)}), bf16[16,2,8192]{2,1,0:T(2,128)(2,1)S(1)}, u32[]{:S(2)}, u32[]{:S(2)}) async-start(bf16[16,2,8192]{2,1,0:T(2,128)(2,1)} %reshape.394), calls=%async_computation.2 | async-start | bytes 1048576 | tf_op jit(solution)/shard_map/all_to_all | solution.py:104
  237.8 11.6 %collective-permute-start = (bf16[1,8,64,128]{3,2,1,0:T(8,128)(2,1)S(1)}, bf16[1,8,64,128]{3,2,1,0:T(8,128)(2,1)S(1)}, u32[]{:S(2)}, u32[]{:S(2)}) collective-permute-start(bf16[1,8,64,128]{3,2,1,0:T(8,128)(2,1)S(1)} %get-tuple-element.205), channel_id=1, source_target_pairs={{0,16},{16,32},{32,48},{48,64},{64,80},{80,96},{96,112},{1,17},{17... | collective-permute-start | bytes 393224 | tf_op jit(solution)/shard_map/ppermute | solution.py:19
  245.0 6.3 %collective-permute-start.1 = (bf16[1,8,64,128]{3,2,1,0:T(8,128)(2,1)S(1)}, bf16[1,8,64,128]{3,2,1,0:T(8,128)(2,1)S(1)}, u32[]{:S(2)}, u32[]{:S(2)}) collective-permute-start(bf16[1,8,64,128]{3,2,1,0:T(8,128)(2,1)S(1)} %get-tuple-element.206), channel_id=1, source_target_pairs={{16,0},{32,16},{48,32},{64,48},{80,64},{96,80},{112,96},{17,1},{33... | collective-permute-start | bytes 393224 | tf_op jit(solution)/shard_map/ppermute | solution.py:21
  251.3 12.4 %collective-permute-start.2 = (bf16[10,1,64,128]{3,2,1,0:T(8,128)(2,1)S(1)}, bf16[10,1,64,128]{3,2,1,0:T(8,128)(2,1)S(1)}, u32[]{:S(2)}, u32[]{:S(2)}) collective-permute-start(bf16[10,1,64,128]{3,2,1,0:T(8,128)(2,1)S(1)} %get-tuple-element.203), channel_id=1, source_target_pairs={{0,1},{1,2},{2,3},{3,4},{4,5},{5,6},{6,7},{7,8},{8,9},{9,10},{10,1... | collective-permute-start | bytes 491528 | tf_op jit(solution)/shard_map/ppermute | solution.py:19
  253.4 10.3 %collective-permute-start.3 = (bf16[10,1,64,128]{3,2,1,0:T(8,128)(2,1)S(1)}, bf16[10,1,64,128]{3,2,1,0:T(8,128)(2,1)S(1)}, u32[]{:S(2)}, u32[]{:S(2)}) collective-permute-start(bf16[10,1,64,128]{3,2,1,0:T(8,128)(2,1)S(1)} %get-tuple-element.204), channel_id=1, source_target_pairs={{1,0},{2,1},{3,2},{4,3},{5,4},{6,5},{7,6},{8,7},{9,8},{10,9},{11,1... | collective-permute-start | bytes 491528 | tf_op jit(solution)/shard_map/ppermute | solution.py:21
  263.7 1.8 copy-start.3
  324.7 1.5 copy-start.2
where the time goes:
time: 365 us; the launch traced here: 358 us
  matrix products  184 us (50%)
  waiting for transfers between devices  58.6 us (16%)
  starting transfers between devices  43.8 us (12%)
  local copies, waits for them, and re-layouts  39.9 us (11%)
  loops' own time  20.2 us (6%)
  other arithmetic  10.9 us (3%)
    dot_general x16, matrix products, brick_down(): jnp.dot(hidden, w_out[layer], preferred_element_type=jnp.float32)  94.9 us
    dot_general x27, matrix products, local(): jnp.dot(moved, w_conv[d, e, f], preferred_element_type=jnp.float32)  66.7 us
    all_to_all x1, waiting for transfers between devices, local(): lax.all_to_all(packed.reshape(width, cap, voxels * chan), 'gy', split_axi...  50.2 us
    another operation x2, loops' own time, blockwise(): result = lax.map(lambda group: func(*group), shaped)  20.2 us
    all_to_all x1, starting transfers between devices, local(): lax.all_to_all(returned.reshape(width, cap, 64 * chan), 'gy', split_axis=...  12.9 us
    dot_general x1, matrix products, local(): jnp.dot(picker_bf, flat.reshape(slots, voxels * chan), preferred_element_...  11.1 us
    dynamic_slice x18, local copies, waits for them, and re-layouts, blockwise(): result = lax.map(lambda group: func(*group), shaped)  10.9 us
    ppermute x2, starting transfers between devices, extended(): lax.ppermute(tail, axis, [(i, (i + 1) % count) for i in range(ends)])  9.23 us
  transfers between devices with their start and end apart: 7, of which 3 were waited for; matrix products, arithmetic and copies ran while one was open for 7% of the time, Pallas kernels for 0%

commit v1 on v0

v1 whole, which is shorter than its diff:
```python
import functools

import jax
import jax.numpy as jnp
from jax import lax
from jax.experimental import pallas as pl
from jax.experimental.pallas import tpu as pltpu
from jax.sharding import PartitionSpec as P

BF16 = jnp.bfloat16
F32 = jnp.float32
GROUP = 4
CHUNK = 512


def transposed(eye, block):
    return lax.dot_general(eye, block, (((1,), (1,)), ((), ())), preferred_element_type=F32)


def identity(n):
    rows = lax.broadcasted_iota(jnp.int32, (n, n), 0)
    return (rows == lax.broadcasted_iota(jnp.int32, (n, n), 1)).astype(BF16)


def prepare_weights(eye, gain_ref, shift_ref, w_in_ref, w_out_ref, wi_ref, wo_ref):
    layers, chan, hid = w_in_ref.shape
    row = lax.broadcasted_iota(jnp.int32, (chan, hid), 0)

    def one(l, _):
        gain = gain_ref[l] * 0.5
        shift = shift_ref[l] * 0.5
        high = shift.astype(BF16).astype(F32)
        mid = (shift - high).astype(BF16).astype(F32)
        low = shift - high - mid
        parts = jnp.where(row == 0, high, jnp.where(row == 1, mid, jnp.where(row == 2, low, 0.0))).astype(BF16)
        w_in = w_in_ref[l]
        w_out = w_out_ref[l]
        for m in range(hid // chan):
            cut = slice(m * chan, (m + 1) * chan)
            wi_ref[l, cut, :chan] = (transposed(eye, w_in[:, cut]) * gain).astype(BF16)
            wi_ref[l, cut, chan:] = transposed(eye, parts[:, cut]).astype(BF16)
            wo_ref[l, :, cut] = transposed(eye, w_out[cut, :]).astype(BF16)
        return 0

    lax.fori_loop(0, layers, one, 0)


def feed_forward(s_ref, wi_ref, wo_ref):
    layers = wi_ref.shape[0]
    chan, width = s_ref.shape
    count = width // CHUNK
    ones = jnp.ones((chan, CHUNK), BF16)

    def hidden(step):
        l, c = divmod(step, count)
        x = s_ref[:, c * CHUNK : (c + 1) * CHUNK]
        scale = lax.rsqrt(jnp.mean(x * x, axis=0, keepdims=True) + 1e-06)
        normed = jnp.concatenate([(x * scale).astype(BF16), ones], axis=0)
        u = jnp.dot(wi_ref[l], normed, preferred_element_type=F32)
        return (u * jnp.tanh(u) + u).astype(BF16)

    def update(step, h):
        l, c = divmod(step, count)
        s_ref[:, c * CHUNK : (c + 1) * CHUNK] += jnp.dot(wo_ref[l], h, preferred_element_type=F32)

    held = hidden(0)
    for step in range(layers * count):
        following = hidden(step + 1) if step + 1 < layers * count else None
        update(step, held)
        held = following


def coarse_kernel(
    owner_ref, features_ref, gain_ref, shift_ref, w_in_ref, w_out_ref, w_down_ref,
    out_ref,
    list_ref, buf_ref, s_ref, t_ref, wi_ref, wo_ref, grid_ref, sems,
):
    slots = owner_ref.shape[0]
    chan = s_ref.shape[0]
    zcap = slots // 4
    eye = identity(chan)

    def note(slot, n):
        @pl.when(owner_ref[slot] >= 0)
        def _():
            list_ref[n] = slot

        return n + (owner_ref[slot] >= 0).astype(jnp.int32)

    total = lax.fori_loop(0, slots, note, 0)
    groups = (total + GROUP - 1) // GROUP

    def brick(g, t):
        return list_ref[jnp.minimum(g * GROUP + t, total - 1)]

    def copy(g, t):
        return pltpu.make_async_copy(
            features_ref.at[brick(g, t)], buf_ref.at[lax.rem(g, 2), t], sems.at[lax.rem(g, 2), t]
        )

    @pl.when(groups > 0)
    def _():
        for t in range(GROUP):
            copy(0, t).start()

    prepare_weights(eye, gain_ref, shift_ref, w_in_ref, w_out_ref, wi_ref, wo_ref)
    grid_ref[...] = jnp.zeros_like(grid_ref)
    half = lax.broadcasted_iota(jnp.int32, (16, 8, 1), 1) // 4

    def body(g, _):
        @pl.when(g + 1 < groups)
        def _():
            for t in range(GROUP):
                copy(g + 1, t).start()

        for t in range(GROUP):
            copy(g, t).wait()
        for t in range(GROUP):
            s_ref[:, t * 512 : (t + 1) * 512] = transposed(eye, buf_ref[lax.rem(g, 2), t])
        feed_forward(s_ref, wi_ref, wo_ref)
        for t in range(GROUP):
            for m in range(4):
                block = s_ref[:, t * 512 + m * 128 : t * 512 + (m + 1) * 128].astype(BF16)
                t_ref[t, m * 128 : (m + 1) * 128, :] = transposed(eye, block)
        for t in range(GROUP):
            total_down = jnp.zeros((128, 2 * chan), F32)
            for a in range(2):
                for c in range(2):
                    rows = jnp.concatenate(
                        [t_ref[t, pl.ds(128 * i + 64 * a + c, 32, stride=2), :] for i in range(4)], axis=0
                    ).astype(BF16)
                    weights = jnp.concatenate([w_down_ref[a, 0, c], w_down_ref[a, 1, c]], axis=1)
                    total_down += jnp.dot(rows, weights, preferred_element_type=F32)
            both = total_down.reshape(16, 8, 2 * chan)
            own = jnp.where(half == 0, both[:, :, :chan], both[:, :, chan:])
            down = own + jnp.concatenate([own[:, 4:, :], own[:, :4, :]], axis=1)
            made = down / (1.0 + jnp.exp(-down))
            slot = brick(g, t)
            column, r = slot // zcap, lax.rem(slot, zcap)
            x0, y0, zpair, odd = (column // 2) * 4, lax.rem(column, 2) * 4, r // 2, lax.rem(r, 2)

            @pl.when(g * GROUP + t < total)
            def _():
                for i in range(4):
                    for j in range(4):
                        old = grid_ref[x0 + i, y0 + j, zpair]
                        grid_ref[x0 + i, y0 + j, zpair] = jnp.where(half[0] == odd, made[4 * i + j], old)

        return 0

    lax.fori_loop(0, groups, body, 0)

    def finish(x, _):
        out_ref[x] = grid_ref[x].reshape(out_ref.shape[1:]).astype(BF16)
        return 0

    lax.fori_loop(0, out_ref.shape[0], finish, 0)


def coarse_grid(features, owner, gain, shift, w_in, w_out, w_down):
    slots, voxels, chan = features.shape
    layers, _, hid = w_in.shape
    vmem = pl.BlockSpec(memory_space=pltpu.VMEM)
    return pl.pallas_call(
        coarse_kernel,
        out_shape=jax.ShapeDtypeStruct((8, 8, slots, chan), BF16),
        in_specs=[pl.BlockSpec(memory_space=pltpu.SMEM), pl.BlockSpec(memory_space=pl.ANY)] + [vmem] * 5,
        out_specs=vmem,
        scratch_shapes=[
            pltpu.SMEM((slots,), jnp.int32),
            pltpu.VMEM((2, GROUP, voxels, chan), BF16),
            pltpu.VMEM((chan, GROUP * voxels), F32),
            pltpu.VMEM((GROUP, voxels, chan), F32),
            pltpu.VMEM((layers, hid, 2 * chan), BF16),
            pltpu.VMEM((layers, chan, hid), BF16),
            pltpu.VMEM((8, 8, slots // 8, 8, chan), F32),
            pltpu.SemaphoreType.DMA((2, GROUP)),
        ],
        compiler_params=pltpu.CompilerParams(vmem_limit_bytes=48 * 2**20),
        cost_estimate=pl.CostEstimate(flops=32 * 10**9, bytes_accessed=8 * 2**20, transcendentals=10**8),
        name="coarse",
    )(owner, features, gain[:, None, :], shift[:, None, :], w_in, w_out, w_down)


def lift_kernel(
    rim_ref, features_ref, live_ref, w_conv_ref, w_up_ref,
    out_ref,
    z_ref, wc_ref, a_ref,
):
    chan = rim_ref.shape[-1]
    gsz = rim_ref.shape[2]
    step = pl.program_id(0)

    @pl.when(step == 0)
    def _():
        row = lax.broadcasted_iota(jnp.int32, (gsz, chan), 0)
        wide = rim_ref.shape[1]

        def shift(n, _):
            x, y = n // wide, lax.rem(n, wide)
            whole = rim_ref[x, y].astype(F32)
            z_ref[0, x, y] = jnp.where(row == 0, 0.0, pltpu.roll(whole, 1, 0)).astype(BF16)
            z_ref[1, x, y] = rim_ref[x, y]
            z_ref[2, x, y] = jnp.where(row == gsz - 1, 0.0, pltpu.roll(whole, gsz - 1, 0)).astype(BF16)
            return 0

        lax.fori_loop(0, rim_ref.shape[0] * wide, shift, 0, unroll=4)
        empty = jnp.zeros((chan, chan), BF16)
        for d in range(3):
            for f in range(3):
                for k in range(4):
                    for o in range(2):
                        e = k - o
                        wc_ref[3 * d + f, k * chan : (k + 1) * chan, o * chan : (o + 1) * chan] = (
                            w_conv_ref[d, e, f] if 0 <= e <= 2 else empty
                        )
        a_ref[...] = jnp.zeros_like(a_ref)

    x0, y0 = (step // 2) * 4, lax.rem(step, 2) * 4
    live = live_ref[0]
    for pair in range(2):
        y = y0 + 2 * pair
        total = jnp.zeros((4 * gsz, 2 * chan), F32)
        for d in range(3):
            for f in range(3):
                rows = jnp.concatenate(
                    [z_ref[f, pl.ds(x0 + d, 4), y + k].reshape(4 * gsz, chan) for k in range(4)], axis=1
                )
                total += jnp.dot(rows, wc_ref[3 * d + f], preferred_element_type=F32)
        for o in range(2):
            own = rim_ref[pl.ds(x0 + 1, 4), y + o + 1].reshape(4 * gsz, chan).astype(F32)
            mixed = total[:, o * chan : (o + 1) * chan] + own
            a_ref[o, 0, pl.ds(0, 4 * gsz, stride=2), :] = mixed
            a_ref[o, 1, pl.ds(1, 4 * gsz, stride=2), :] = mixed
            spread = jnp.concatenate([a_ref[o, 0], a_ref[o, 1]], axis=1).astype(BF16)
            j = 2 * pair + o
            for a in range(2):
                weights = jnp.concatenate(
                    [jnp.concatenate([w_up_ref[a, b, c] for b in range(2)], axis=1) for c in range(2)], axis=0
                )
                upward = jnp.dot(spread, weights, preferred_element_type=F32)
                for i in range(4):
                    part = upward[2 * gsz * i : 2 * gsz * (i + 1)].reshape(gsz // 4, 8, 2 * chan)
                    part = jnp.concatenate([part[:, :, :chan], part[:, :, chan:]], axis=1)
                    base = 128 * i + 64 * a + 16 * j
                    given = features_ref[:, base : base + 16, :].astype(F32)
                    out_ref[:, base : base + 16, :] = ((given + part) * live).astype(BF16)


def lift(rim, features, live, w_conv, w_up):
    slots, voxels, chan = features.shape
    gsx, gsy, gsz, _ = rim.shape
    columns = 4
    zcap = slots // columns
    vmem = pl.BlockSpec(memory_space=pltpu.VMEM)
    block = pl.BlockSpec((zcap, voxels, chan), lambda s: (s, 0, 0))
    return pl.pallas_call(
        lift_kernel,
        grid=(columns,),
        out_shape=jax.ShapeDtypeStruct(features.shape, BF16),
        in_specs=[
            vmem,
            block,
            pl.BlockSpec((1, zcap, 1, chan), lambda s: (s, 0, 0, 0)),
            vmem,
            vmem,
        ],
        out_specs=block,
        scratch_shapes=[
            pltpu.VMEM((3, gsx, gsy, gsz, chan), BF16),
            pltpu.VMEM((9, 4 * chan, 2 * chan), BF16),
            pltpu.VMEM((2, 2, 8 * gsz, chan), F32),
        ],
        compiler_params=pltpu.CompilerParams(vmem_limit_bytes=48 * 2**20),
        cost_estimate=pl.CostEstimate(flops=5 * 10**9, bytes_accessed=18 * 2**20, transcendentals=0),
        name="lift",
    )(rim, features, live, w_conv, w_up)


def extended(cells, sides, width):
    for axis, dim in sides:
        count = lax.axis_size(axis)
        ends = count - 1
        head = lax.slice_in_dim(cells, 0, width, axis=dim)
        tail = lax.slice_in_dim(cells, cells.shape[dim] - width, cells.shape[dim], axis=dim)
        cells = jnp.concatenate(
            [
                lax.ppermute(tail, axis, [(i, (i + 1) % count) for i in range(ends)]),
                cells,
                lax.ppermute(head, axis, [((i + 1) % count, i) for i in range(ends)]),
            ],
            axis=dim,
        )
    return cells


def local(features, owner, norm_gain, time_shift, w_in, w_out, w_down, w_conv, w_up):
    cols_x, cols_y, zcap, voxels, chan = features.shape
    slots = cols_x * cols_y * zcap
    flat = features.reshape(slots, voxels, chan)
    code = owner.reshape(slots)
    grid = coarse_grid(flat, code, norm_gain, time_shift, w_in, w_out, w_down)
    rimmed = extended(grid, (("gx", 0), ("gy", 1)), 1)
    live = jnp.broadcast_to(
        (code >= 0).astype(F32).reshape(cols_x * cols_y, zcap, 1, 1), (cols_x * cols_y, zcap, 1, chan)
    )
    result = lift(rimmed, flat, live, w_conv, w_up)
    return result.reshape(features.shape)


def solution(mesh):
    in_specs = (
        P("gx", "gy", None, None, None),
        P("gx", "gy", None),
        P(),
        P(),
        P(),
        P(),
        P(),
        P(),
        P(),
    )
    out_specs = P("gx", "gy", None, None, None)
    return jax.shard_map(local, mesh=mesh, in_specs=in_specs, out_specs=out_specs, check_vma=False)
```

time: 365 us -> 122 us (0.33)
  the two profiles are of different devices: /device:TPU:9 before, /device:TPU:13 now
where the time goes in v1:
time: 122 us
  starting transfers between devices  64.5 us (53%)
  Pallas kernels  41.5 us (34%)
  waiting for transfers between devices  9.71 us (8%)
  local copies, waits for them, and re-layouts  5.73 us (5%)
    ppermute x2, starting transfers between devices, extended(): lax.ppermute(tail, axis, [(i, (i + 1) % count) for i in range(ends)])  56.1 us
    pallas_call x1, Pallas kernels, coarse_grid(): pl.pallas_call(coarse_kernel, out_shape=jax.ShapeDtypeStruct((8, 8, slots...  22 us
    pallas_call x1, Pallas kernels, lift(): pl.pallas_call(lift_kernel, grid=(columns,), out_shape=jax.ShapeDtypeStru...  19.6 us
    ppermute x2, starting transfers between devices, extended(): lax.ppermute(head, axis, [((i + 1) % count, i) for i in range(ends)])  8.33 us
    ppermute x2, waiting for transfers between devices, extended(): lax.ppermute(head, axis, [((i + 1) % count, i) for i in range(ends)])  7.84 us
    unnamed x14, local copies, waits for them, and re-layouts  4.1 us
  transfers between devices with their start and end apart: 4, of which 3 were waited for; matrix products, arithmetic and copies ran while one was open for 0% of the time, Pallas kernels for 0%

profile of v1, /device:TPU:13, one launch (start us, length us, event | category | flops | bytes accessed | tf_op | source)
XLA Modules:
  0.0 122.0 jit_solution(10681449455367372891)
XLA Ops:
  0.0 0.8 reshape.22.owner_ref
  0.8 0.7 broadcast_in_dim.12.shift_ref
  1.5 0.0 copy-start.2
  1.5 1.2 copy-done.2
  2.7 0.0 copy-start.3
  2.7 1.2 %copy-done.3 = bf16[8,512,128]{2,1,0:T(8,128)(2,1)S(1)} copy-done((bf16[8,512,128]{2,1,0:T(8,128)(2,1)S(1)}, bf16[8,512,128]{2,1,0:T(8,128)(2,1)}, u32[]{:S(2)}) %copy-start.3) | copy-done | bytes 1048600
  4.0 0.0 copy-start.4
  4.0 0.9 copy-done.4
  4.9 0.0 copy-start.5
  4.9 0.7 copy-done.5
  5.6 22.0 %coarse.1 = bf16[8,8,64,128]{3,2,1,0:T(8,128)(2,1)S(1)} custom-call(s32[64]{0:T(128)S(1)} %reshape.22.owner_ref, bf16[64,512,128]{2,1,0:T(8,128)(2,1)} %bitcast.5, f32[8,1,128]{2,1,0:T(1,128)S(1)} %bitcast.4, f32[8,1,512]{2,1,0:T(1,128)S(1)} %broadcast_in_dim.12.shift_ref, bf16[8,128,512]{2,1,0:T(8,128)(2,1)S(1)} %copy-done.2, ...), custom_call_target="tpu_custom_call" | custom-call | flops 32000000000 | bytes 8388608 | tf_op jit(solution)/shard_map/coarse/pallas_call | solution.py:164
  27.6 0.0 copy-start.6
  27.6 21.2 %collective-permute-start = (bf16[1,8,64,128]{3,2,1,0:T(8,128)(2,1)S(1)}, bf16[1,8,64,128]{3,2,1,0:T(8,128)(2,1)S(1)}, u32[]{:S(2)}, u32[]{:S(2)}) collective-permute-start(bf16[1,8,64,128]{3,2,1,0:T(8,128)(2,1)S(1)} %get-tuple-element.7), channel_id=1, source_target_pairs={{0,16},{16,32},{32,48},{48,64},{64,80},{80,96},{96,112},{1,17},{17... | collective-permute-start | bytes 393224 | tf_op jit(solution)/shard_map/ppermute | solution.py:288
  48.8 1.9 %collective-permute-start.1 = (bf16[1,8,64,128]{3,2,1,0:T(8,128)(2,1)S(1)}, bf16[1,8,64,128]{3,2,1,0:T(8,128)(2,1)S(1)}, u32[]{:S(2)}, u32[]{:S(2)}) collective-permute-start(bf16[1,8,64,128]{3,2,1,0:T(8,128)(2,1)S(1)} %get-tuple-element.8), channel_id=1, source_target_pairs={{16,0},{32,16},{48,32},{64,48},{80,64},{96,80},{112,96},{17,1},{33... | collective-permute-start | bytes 393224 | tf_op jit(solution)/shard_map/ppermute | solution.py:290
  50.7 0.0 collective-permute-done
  50.7 4.3 %collective-permute-done.1 = bf16[1,8,64,128]{3,2,1,0:T(8,128)(2,1)S(1)} collective-permute-done((bf16[1,8,64,128]{3,2,1,0:T(8,128)(2,1)S(1)}, bf16[1,8,64,128]{3,2,1,0:T(8,128)(2,1)S(1)}, u32[]{:S(2)}, u32[]{:S(2)}) %collective-permute-start.1) | collective-permute-done | bytes 131104 | tf_op jit(solution)/shard_map/ppermute | solution.py:290
  55.1 34.9 %collective-permute-start.2 = (bf16[10,1,64,128]{3,2,1,0:T(8,128)(2,1)S(1)}, bf16[10,1,64,128]{3,2,1,0:T(8,128)(2,1)S(1)}, u32[]{:S(2)}, u32[]{:S(2)}) collective-permute-start(bf16[10,1,64,128]{3,2,1,0:T(8,128)(2,1)S(1)} %get-tuple-element.5), channel_id=1, source_target_pairs={{0,1},{1,2},{2,3},{3,4},{4,5},{5,6},{6,7},{7,8},{8,9},{9,10},{10,1... | collective-permute-start | bytes 491528 | tf_op jit(solution)/shard_map/ppermute | solution.py:288
  90.1 6.4 %collective-permute-start.3 = (bf16[10,1,64,128]{3,2,1,0:T(8,128)(2,1)S(1)}, bf16[10,1,64,128]{3,2,1,0:T(8,128)(2,1)S(1)}, u32[]{:S(2)}, u32[]{:S(2)}) collective-permute-start(bf16[10,1,64,128]{3,2,1,0:T(8,128)(2,1)S(1)} %get-tuple-element.6), channel_id=1, source_target_pairs={{1,0},{2,1},{3,2},{4,3},{5,4},{6,5},{7,6},{8,7},{9,8},{10,9},{11,1... | collective-permute-start | bytes 491528 | tf_op jit(solution)/shard_map/ppermute | solution.py:290
  96.5 0.0 copy-done.6
  96.5 0.0 copy-start
  96.5 0.0 copy-start.1
  96.6 1.9 %collective-permute-done.2 = bf16[10,1,64,128]{3,2,1,0:T(8,128)(2,1)S(1)} collective-permute-done((bf16[10,1,64,128]{3,2,1,0:T(8,128)(2,1)S(1)}, bf16[10,1,64,128]{3,2,1,0:T(8,128)(2,1)S(1)}, u32[]{:S(2)}, u32[]{:S(2)}) %collective-permute-start.2) | collective-permute-done | bytes 163872 | tf_op jit(solution)/shard_map/ppermute | solution.py:288
  98.4 3.5 %collective-permute-done.3 = bf16[10,1,64,128]{3,2,1,0:T(8,128)(2,1)S(1)} collective-permute-done((bf16[10,1,64,128]{3,2,1,0:T(8,128)(2,1)S(1)}, bf16[10,1,64,128]{3,2,1,0:T(8,128)(2,1)S(1)}, u32[]{:S(2)}, u32[]{:S(2)}) %collective-permute-start.3) | collective-permute-done | bytes 163872 | tf_op jit(solution)/shard_map/ppermute | solution.py:290
  101.9 0.3 pad_maximum_fusion.rim_ref
  102.2 0.1 broadcast_in_dim.13.live_ref
  102.3 0.0 copy-done
  102.4 0.0 copy-done.1
  102.4 19.6 %lift.1 = bf16[64,512,128]{2,1,0:T(8,128)(2,1)} custom-call(bf16[10,10,64,128]{3,2,1,0:T(8,128)(2,1)S(1)} %pad_maximum_fusion.rim_ref, bf16[64,512,128]{2,1,0:T(8,128)(2,1)} %bitcast.6, f32[4,16,1,128]{3,2,1,0:T(1,128)S(1)} %broadcast_in_dim.13.live_ref, bf16[3,3,3,128,128]{4,3,2,1,0:T(8,128)(2,1)S(1)} %copy-done, bf16[2,2,2,128,128]{4,3,2,1,0:T(8,128)(2,1)S(1)} %copy-done.1), custom_call_target="tpu_custom_call" | custom-call | flops 5000000000 | bytes 18874368 | tf_op jit(solution)/shard_map/lift/pallas_call | solution.py:257
  (3 shorter events, 0.1 us)
Async XLA Ops:
  1.5 1.2 %copy-start.2 = (bf16[8,128,512]{2,1,0:T(8,128)(2,1)S(1)}, bf16[8,128,512]{2,1,0:T(8,128)(2,1)}, u32[]{:S(2)}) copy-start(bf16[8,128,512]{2,1,0:T(8,128)(2,1)} %w_in_ref.1) | copy-start | bytes 3145732
  2.7 1.2 %copy-start.3 = (bf16[8,512,128]{2,1,0:T(8,128)(2,1)S(1)}, bf16[8,512,128]{2,1,0:T(8,128)(2,1)}, u32[]{:S(2)}) copy-start(bf16[8,512,128]{2,1,0:T(8,128)(2,1)} %w_out_ref.1) | copy-start | bytes 3145732
  4.0 0.9 copy-start.4
  4.9 0.7 copy-start.5
  27.6 68.9 %copy-start.6 = (s32[2,2,16]{2,1,0:T(2,128)S(1)}, s32[2,2,16]{2,1,0:T(2,128)}, u32[]{:S(2)}) copy-start(s32[2,2,16]{2,1,0:T(2,128)} %param.10) | copy-start | bytes 772
  27.6 23.1 %collective-permute-start = (bf16[1,8,64,128]{3,2,1,0:T(8,128)(2,1)S(1)}, bf16[1,8,64,128]{3,2,1,0:T(8,128)(2,1)S(1)}, u32[]{:S(2)}, u32[]{:S(2)}) collective-permute-start(bf16[1,8,64,128]{3,2,1,0:T(8,128)(2,1)S(1)} %get-tuple-element.7), channel_id=1, source_target_pairs={{0,16},{16,32},{32,48},{48,64},{64,80},{80,96},{96,112},{1,17},{17... | collective-permute-start | bytes 393224 | tf_op jit(solution)/shard_map/ppermute | solution.py:288
  48.8 6.3 %collective-permute-start.1 = (bf16[1,8,64,128]{3,2,1,0:T(8,128)(2,1)S(1)}, bf16[1,8,64,128]{3,2,1,0:T(8,128)(2,1)S(1)}, u32[]{:S(2)}, u32[]{:S(2)}) collective-permute-start(bf16[1,8,64,128]{3,2,1,0:T(8,128)(2,1)S(1)} %get-tuple-element.8), channel_id=1, source_target_pairs={{16,0},{32,16},{48,32},{64,48},{80,64},{96,80},{112,96},{17,1},{33... | collective-permute-start | bytes 393224 | tf_op jit(solution)/shard_map/ppermute | solution.py:290
  55.1 43.3 %collective-permute-start.2 = (bf16[10,1,64,128]{3,2,1,0:T(8,128)(2,1)S(1)}, bf16[10,1,64,128]{3,2,1,0:T(8,128)(2,1)S(1)}, u32[]{:S(2)}, u32[]{:S(2)}) collective-permute-start(bf16[10,1,64,128]{3,2,1,0:T(8,128)(2,1)S(1)} %get-tuple-element.5), channel_id=1, source_target_pairs={{0,1},{1,2},{2,3},{3,4},{4,5},{5,6},{6,7},{7,8},{8,9},{9,10},{10,1... | collective-permute-start | bytes 491528 | tf_op jit(solution)/shard_map/ppermute | solution.py:288
  90.1 11.8 %collective-permute-start.3 = (bf16[10,1,64,128]{3,2,1,0:T(8,128)(2,1)S(1)}, bf16[10,1,64,128]{3,2,1,0:T(8,128)(2,1)S(1)}, u32[]{:S(2)}, u32[]{:S(2)}) collective-permute-start(bf16[10,1,64,128]{3,2,1,0:T(8,128)(2,1)S(1)} %get-tuple-element.6), channel_id=1, source_target_pairs={{1,0},{2,1},{3,2},{4,3},{5,4},{6,5},{7,6},{8,7},{9,8},{10,9},{11,1... | collective-permute-start | bytes 491528 | tf_op jit(solution)/shard_map/ppermute | solution.py:290
  96.5 5.8 %copy-start = (bf16[3,3,3,128,128]{4,3,2,1,0:T(8,128)(2,1)S(1)}, bf16[3,3,3,128,128]{4,3,2,1,0:T(8,128)(2,1)}, u32[]{:S(2)}) copy-start(bf16[3,3,3,128,128]{4,3,2,1,0:T(8,128)(2,1)} %w_conv_ref.1) | copy-start | bytes 2654212
  96.5 5.8 %copy-start.1 = (bf16[2,2,2,128,128]{4,3,2,1,0:T(8,128)(2,1)S(1)}, bf16[2,2,2,128,128]{4,3,2,1,0:T(8,128)(2,1)}, u32[]{:S(2)}) copy-start(bf16[2,2,2,128,128]{4,3,2,1,0:T(8,128)(2,1)} %w_up_ref.1) | copy-start | bytes 786436

commit v2 on v1

--- a/solution.py
+++ b/solution.py
@@ -27,8 +27,8 @@
     row = lax.broadcasted_iota(jnp.int32, (chan, hid), 0)
 
     def one(l, _):
-        gain = gain_ref[l] * 0.5
-        shift = shift_ref[l] * 0.5
+        gain = gain_ref[pl.ds(l, 1), :] * 0.5
+        shift = shift_ref[pl.ds(l, 1), :] * 0.5
         high = shift.astype(BF16).astype(F32)
         mid = (shift - high).astype(BF16).astype(F32)
         low = shift - high - mid
@@ -71,21 +71,30 @@
 
 
 def coarse_kernel(
-    owner_ref, features_ref, gain_ref, shift_ref, w_in_ref, w_out_ref, w_down_ref,
+    owner_ref, features_ref, gain_ref, shift_ref, w_in_hbm, w_out_hbm, w_down_hbm,
     out_ref,
-    list_ref, buf_ref, s_ref, t_ref, wi_ref, wo_ref, grid_ref, sems,
+    list_ref, buf_ref, s_ref, t_ref, wi_ref, wo_ref, grid_ref, w_in_ref, w_out_ref, w_down_ref, sems, w_sems,
 ):
-    slots = owner_ref.shape[0]
+    _, cols_y, zcap = owner_ref.shape
+    slots = out_ref.shape[2]
     chan = s_ref.shape[0]
-    zcap = slots // 4
     eye = identity(chan)
+    weights = [
+        pltpu.make_async_copy(src, dst, w_sems.at[n])
+        for n, (src, dst) in enumerate(((w_in_hbm, w_in_ref), (w_out_hbm, w_out_ref), (w_down_hbm, w_down_ref)))
+    ]
+    for w in weights:
+        w.start()
 
     def note(slot, n):
-        @pl.when(owner_ref[slot] >= 0)
+        column, r = slot // zcap, lax.rem(slot, zcap)
+        alive = owner_ref[column // cols_y, lax.rem(column, cols_y), r] >= 0
+
+        @pl.when(alive)
         def _():
             list_ref[n] = slot
 
-        return n + (owner_ref[slot] >= 0).astype(jnp.int32)
+        return n + alive.astype(jnp.int32)
 
     total = lax.fori_loop(0, slots, note, 0)
     groups = (total + GROUP - 1) // GROUP
@@ -103,8 +112,10 @@
         for t in range(GROUP):
             copy(0, t).start()
 
+    grid_ref[...] = jnp.zeros_like(grid_ref)
+    for w in weights:
+        w.wait()
     prepare_weights(eye, gain_ref, shift_ref, w_in_ref, w_out_ref, wi_ref, wo_ref)
-    grid_ref[...] = jnp.zeros_like(grid_ref)
     half = lax.broadcasted_iota(jnp.int32, (16, 8, 1), 1) // 4
 
     def body(g, _):
@@ -161,10 +172,11 @@
     slots, voxels, chan = features.shape
     layers, _, hid = w_in.shape
     vmem = pl.BlockSpec(memory_space=pltpu.VMEM)
+    hbm = pl.BlockSpec(memory_space=pl.ANY)
     return pl.pallas_call(
         coarse_kernel,
         out_shape=jax.ShapeDtypeStruct((8, 8, slots, chan), BF16),
-        in_specs=[pl.BlockSpec(memory_space=pltpu.SMEM), pl.BlockSpec(memory_space=pl.ANY)] + [vmem] * 5,
+        in_specs=[pl.BlockSpec(memory_space=pltpu.SMEM), hbm, vmem, vmem, hbm, hbm, hbm],
         out_specs=vmem,
         scratch_shapes=[
             pltpu.SMEM((slots,), jnp.int32),
@@ -174,66 +186,66 @@
             pltpu.VMEM((layers, hid, 2 * chan), BF16),
             pltpu.VMEM((layers, chan, hid), BF16),
             pltpu.VMEM((8, 8, slots // 8, 8, chan), F32),
+            pltpu.VMEM(w_in.shape, BF16),
+            pltpu.VMEM(w_out.shape, BF16),
+            pltpu.VMEM(w_down.shape, BF16),
             pltpu.SemaphoreType.DMA((2, GROUP)),
+            pltpu.SemaphoreType.DMA((3,)),
         ],
         compiler_params=pltpu.CompilerParams(vmem_limit_bytes=48 * 2**20),
         cost_estimate=pl.CostEstimate(flops=32 * 10**9, bytes_accessed=8 * 2**20, transcendentals=10**8),
         name="coarse",
-    )(owner, features, gain[:, None, :], shift[:, None, :], w_in, w_out, w_down)
+    )(owner, features, gain, shift, w_in, w_out, w_down)
 
 
 def lift_kernel(
-    rim_ref, features_ref, live_ref, w_conv_ref, w_up_ref,
+    owner_ref, rim_ref, features_ref, w_conv_ref, w_up_ref,
     out_ref,
-    z_ref, wc_ref, a_ref,
+    wc_ref, a_ref,
 ):
     chan = rim_ref.shape[-1]
     gsz = rim_ref.shape[2]
+    zcap = owner_ref.shape[2]
     step = pl.program_id(0)
+    p, q = step // 2, lax.rem(step, 2)
 
     @pl.when(step == 0)
     def _():
-        row = lax.broadcasted_iota(jnp.int32, (gsz, chan), 0)
-        wide = rim_ref.shape[1]
-
-        def shift(n, _):
-            x, y = n // wide, lax.rem(n, wide)
-            whole = rim_ref[x, y].astype(F32)
-            z_ref[0, x, y] = jnp.where(row == 0, 0.0, pltpu.roll(whole, 1, 0)).astype(BF16)
-            z_ref[1, x, y] = rim_ref[x, y]
-            z_ref[2, x, y] = jnp.where(row == gsz - 1, 0.0, pltpu.roll(whole, gsz - 1, 0)).astype(BF16)
-            return 0
-
-        lax.fori_loop(0, rim_ref.shape[0] * wide, shift, 0, unroll=4)
         empty = jnp.zeros((chan, chan), BF16)
         for d in range(3):
-            for f in range(3):
-                for k in range(4):
-                    for o in range(2):
-                        e = k - o
-                        wc_ref[3 * d + f, k * chan : (k + 1) * chan, o * chan : (o + 1) * chan] = (
+            for k in range(4):
+                for o in range(2):
+                    e = k - o
+                    for f in range(3):
+                        col = (2 * f + o) * chan
+                        wc_ref[d, k * chan : (k + 1) * chan, col : col + chan] = (
                             w_conv_ref[d, e, f] if 0 <= e <= 2 else empty
                         )
         a_ref[...] = jnp.zeros_like(a_ref)
 
-    x0, y0 = (step // 2) * 4, lax.rem(step, 2) * 4
-    live = live_ref[0]
+    x0, y0 = p * 4, q * 4
+    live = jnp.concatenate(
+        [jnp.full((1, 16, chan), (owner_ref[p, q, r] >= 0).astype(F32)) for r in range(zcap)], axis=0
+    )
+    z = lax.rem(lax.broadcasted_iota(jnp.int32, (4 * gsz, 2 * chan), 0), gsz)
     for pair in range(2):
         y = y0 + 2 * pair
-        total = jnp.zeros((4 * gsz, 2 * chan), F32)
+        total = jnp.zeros((4 * gsz, 6 * chan), F32)
         for d in range(3):
-            for f in range(3):
-                rows = jnp.concatenate(
-                    [z_ref[f, pl.ds(x0 + d, 4), y + k].reshape(4 * gsz, chan) for k in range(4)], axis=1
-                )
-                total += jnp.dot(rows, wc_ref[3 * d + f], preferred_element_type=F32)
+            rows = jnp.concatenate(
+                [rim_ref[pl.ds(x0 + d, 4), y + k].reshape(4 * gsz, chan) for k in range(4)], axis=1
+            )
+            total += jnp.dot(rows, wc_ref[d], preferred_element_type=F32)
+        below = pltpu.roll(total[:, : 2 * chan], 1, 0)
+        above = pltpu.roll(total[:, 4 * chan :], 4 * gsz - 1, 0)
+        summed = total[:, 2 * chan : 4 * chan] + jnp.where(z == 0, 0.0, below) + jnp.where(z == gsz - 1, 0.0, above)
         for o in range(2):
             own = rim_ref[pl.ds(x0 + 1, 4), y + o + 1].reshape(4 * gsz, chan).astype(F32)
-            mixed = total[:, o * chan : (o + 1) * chan] + own
-            a_ref[o, 0, pl.ds(0, 4 * gsz, stride=2), :] = mixed
-            a_ref[o, 1, pl.ds(1, 4 * gsz, stride=2), :] = mixed
-            spread = jnp.concatenate([a_ref[o, 0], a_ref[o, 1]], axis=1).astype(BF16)
+            mixed = summed[:, o * chan : (o + 1) * chan] + own
             j = 2 * pair + o
+            a_ref[j, 0, pl.ds(0, 4 * gsz, stride=2), :] = mixed
+            a_ref[j, 1, pl.ds(1, 4 * gsz, stride=2), :] = mixed
+            spread = jnp.concatenate([a_ref[j, 0], a_ref[j, 1]], axis=1).astype(BF16)
             for a in range(2):
                 weights = jnp.concatenate(
                     [jnp.concatenate([w_up_ref[a, b, c] for b in range(2)], axis=1) for c in range(2)], axis=0
@@ -247,64 +259,102 @@
                     out_ref[:, base : base + 16, :] = ((given + part) * live).astype(BF16)
 
 
-def lift(rim, features, live, w_conv, w_up):
+def lift(owner, rim, features, w_conv, w_up):
     slots, voxels, chan = features.shape
-    gsx, gsy, gsz, _ = rim.shape
+    gsz = rim.shape[2]
     columns = 4
-    zcap = slots // columns
     vmem = pl.BlockSpec(memory_space=pltpu.VMEM)
-    block = pl.BlockSpec((zcap, voxels, chan), lambda s: (s, 0, 0))
+    block = pl.BlockSpec((slots // columns, voxels, chan), lambda s: (s, 0, 0))
     return pl.pallas_call(
         lift_kernel,
         grid=(columns,),
         out_shape=jax.ShapeDtypeStruct(features.shape, BF16),
-        in_specs=[
-            vmem,
-            block,
-            pl.BlockSpec((1, zcap, 1, chan), lambda s: (s, 0, 0, 0)),
-            vmem,
-            vmem,
-        ],
+        in_specs=[pl.BlockSpec(memory_space=pltpu.SMEM), vmem, block, vmem, vmem],
         out_specs=block,
         scratch_shapes=[
-            pltpu.VMEM((3, gsx, gsy, gsz, chan), BF16),
-            pltpu.VMEM((9, 4 * chan, 2 * chan), BF16),
-            pltpu.VMEM((2, 2, 8 * gsz, chan), F32),
+            pltpu.VMEM((3, 4 * chan, 6 * chan), BF16),
+            pltpu.VMEM((4, 2, 8 * gsz, chan), F32),
         ],
         compiler_params=pltpu.CompilerParams(vmem_limit_bytes=48 * 2**20),
         cost_estimate=pl.CostEstimate(flops=5 * 10**9, bytes_accessed=18 * 2**20, transcendentals=0),
         name="lift",
-    )(rim, features, live, w_conv, w_up)
-
-
-def extended(cells, sides, width):
-    for axis, dim in sides:
-        count = lax.axis_size(axis)
-        ends = count - 1
-        head = lax.slice_in_dim(cells, 0, width, axis=dim)
-        tail = lax.slice_in_dim(cells, cells.shape[dim] - width, cells.shape[dim], axis=dim)
-        cells = jnp.concatenate(
-            [
-                lax.ppermute(tail, axis, [(i, (i + 1) % count) for i in range(ends)]),
-                cells,
-                lax.ppermute(head, axis, [((i + 1) % count, i) for i in range(ends)]),
-            ],
-            axis=dim,
+    )(owner, rim, features, w_conv, w_up)
+
+
+def rim_kernel(grid_ref, out_ref, send_sems, recv_sems):
+    gsx, gsy = grid_ref.shape[:2]
+    gx, gy = lax.axis_index("gx"), lax.axis_index("gy")
+    nx, ny = lax.axis_size("gx"), lax.axis_size("gy")
+    sides = [(dx, dy) for dx in (-1, 0, 1) for dy in (-1, 0, 1) if (dx, dy) != (0, 0)]
+
+    def device(dx, dy):
+        return (lax.rem(gx + dx + nx, nx), lax.rem(gy + dy + ny, ny))
+
+    barrier = pltpu.get_barrier_semaphore()
+    for side in sides:
+        pl.semaphore_signal(barrier, inc=1, device_id=device(*side), device_id_type=pl.DeviceIdType.MESH)
+    pl.semaphore_wait(barrier, len(sides))
+
+    def cut(side, size):
+        return {-1: pl.ds(0, 1), 0: pl.ds(0, size), 1: pl.ds(size - 1, 1)}[side]
+
+    def place(side, size):
+        return {-1: pl.ds(size + 1, 1), 0: pl.ds(1, size), 1: pl.ds(0, 1)}[side]
+
+    copies = []
+    for n, (dx, dy) in enumerate(sides):
+        copy = pltpu.make_async_remote_copy(
+            src_ref=grid_ref.at[cut(dx, gsx), cut(dy, gsy)],
+            dst_ref=out_ref.at[place(dx, gsx), place(dy, gsy)],
+            send_sem=send_sems.at[n],
+            recv_sem=recv_sems.at[n],
+            device_id=device(dx, dy),
+            device_id_type=pl.DeviceIdType.MESH,
         )
-    return cells
+        copy.start()
+        copies.append(copy)
+    out_ref[pl.ds(1, gsx), pl.ds(1, gsy)] = grid_ref[...]
+    for copy in copies:
+        copy.wait()
+
+    @pl.when(gx == 0)
+    def _():
+        out_ref[0] = jnp.zeros_like(out_ref[0])
+
+    @pl.when(gx == nx - 1)
+    def _():
+        out_ref[gsx + 1] = jnp.zeros_like(out_ref[gsx + 1])
+
+    @pl.when(gy == 0)
+    def _():
+        out_ref[:, 0] = jnp.zeros_like(out_ref[:, 0])
+
+    @pl.when(gy == ny - 1)
+    def _():
+        out_ref[:, gsy + 1] = jnp.zeros_like(out_ref[:, gsy + 1])
+
+
+def with_rim(grid):
+    gsx, gsy, gsz, chan = grid.shape
+    vmem = pl.BlockSpec(memory_space=pltpu.VMEM)
+    return pl.pallas_call(
+        rim_kernel,
+        out_shape=jax.ShapeDtypeStruct((gsx + 2, gsy + 2, gsz, chan), BF16),
+        in_specs=[vmem],
+        out_specs=vmem,
+        scratch_shapes=[pltpu.SemaphoreType.DMA((8,)), pltpu.SemaphoreType.DMA((8,))],
+        compiler_params=pltpu.CompilerParams(
+            collective_id=0, has_side_effects=True, vmem_limit_bytes=32 * 2**20
+        ),
+        name="rim",
+    )(grid)
 
 
 def local(features, owner, norm_gain, time_shift, w_in, w_out, w_down, w_conv, w_up):
     cols_x, cols_y, zcap, voxels, chan = features.shape
-    slots = cols_x * cols_y * zcap
-    flat = features.reshape(slots, voxels, chan)
-    code = owner.reshape(slots)
-    grid = coarse_grid(flat, code, norm_gain, time_shift, w_in, w_out, w_down)
-    rimmed = extended(grid, (("gx", 0), ("gy", 1)), 1)
-    live = jnp.broadcast_to(
-        (code >= 0).astype(F32).reshape(cols_x * cols_y, zcap, 1, 1), (cols_x * cols_y, zcap, 1, chan)
-    )
-    result = lift(rimmed, flat, live, w_conv, w_up)
+    flat = features.reshape(cols_x * cols_y * zcap, voxels, chan)
+    grid = coarse_grid(flat, owner, norm_gain, time_shift, w_in, w_out, w_down)
+    result = lift(owner, with_rim(grid), flat, w_conv, w_up)
     return result.reshape(features.shape)
 
 

time: 122 us -> 110 us (0.902)
  the two profiles are of different devices: /device:TPU:13 before, /device:TPU:1 now
where the time goes in v2:
time: 110 us
  Pallas kernels  104 us (95%)
  local copies, waits for them, and re-layouts  5.49 us (5%)
    pallas_call x1, Pallas kernels, coarse_grid(): pl.pallas_call(coarse_kernel, out_shape=jax.ShapeDtypeStruct((8, 8, slots...  76.3 us
    pallas_call x1, Pallas kernels, lift(): pl.pallas_call(lift_kernel, grid=(columns,), out_shape=jax.ShapeDtypeStru...  14.7 us
    pallas_call x1, Pallas kernels, with_rim(): pl.pallas_call(rim_kernel, out_shape=jax.ShapeDtypeStruct((gsx + 2, gsy +...  13.3 us
    unnamed x16, local copies, waits for them, and re-layouts  5.49 us

profile of v2, /device:TPU:1, one launch (start us, length us, event | category | flops | bytes accessed | tf_op | source)
XLA Modules:
  0.0 109.8 jit_solution(3617391973644827743)
XLA Ops:
  0.0 0.0 copy-start.2
  0.0 0.7 copy-done.2
  0.7 0.0 copy-start.3
  0.7 1.2 %copy-done.3 = bf16[8,128,512]{2,1,0:T(8,128)(2,1)S(1)} copy-done((bf16[8,128,512]{2,1,0:T(8,128)(2,1)S(1)}, bf16[8,128,512]{2,1,0:T(8,128)(2,1)}, u32[]{:S(2)}) %copy-start.3) | copy-done | bytes 1048600
  1.9 0.0 copy-start.4
  1.9 1.2 %copy-done.4 = bf16[8,512,128]{2,1,0:T(8,128)(2,1)S(1)} copy-done((bf16[8,512,128]{2,1,0:T(8,128)(2,1)S(1)}, bf16[8,512,128]{2,1,0:T(8,128)(2,1)}, u32[]{:S(2)}) %copy-start.4) | copy-done | bytes 1048600
  3.1 0.0 copy-start.5
  3.1 0.9 copy-done.5
  4.1 0.0 copy-start.6
  4.1 0.7 copy-done.6
  4.8 0.0 copy-start.7
  4.8 0.7 copy-done.7
  5.5 0.0 copy-start
  5.5 0.0 copy-start.1
  5.5 76.3 %coarse.1.grid_ref = bf16[8,8,64,128]{3,2,1,0:T(8,128)(2,1)S(1)} custom-call(s32[2,2,16]{2,1,0:T(2,128)S(1)} %copy-done.2, bf16[64,512,128]{2,1,0:T(8,128)(2,1)} %bitcast.2, f32[8,128]{1,0:T(8,128)S(1)} %copy-done.7, f32[8,512]{1,0:T(8,128)S(1)} %copy-done.6, bf16[8,128,512]{2,1,0:T(8,128)(2,1)S(1)} %copy-done.3, bf16[8,512,128]{2,1,0:T(8,128)(2,1)S(1)} %copy-done.4, ...), custom_call_target="tpu_custom_call" | custom-call | flops 32000000000 | bytes 8388608 | tf_op jit(solution)/shard_map/coarse/pallas_call | solution.py:176
  81.8 13.3 %rim.1.rim_ref = bf16[10,10,64,128]{3,2,1,0:T(8,128)(2,1)S(1)} custom-call(bf16[8,8,64,128]{3,2,1,0:T(8,128)(2,1)S(1)} %coarse.1.grid_ref), custom_call_target="tpu_custom_call" | custom-call | tf_op jit(solution)/shard_map/rim/pallas_call | solution.py:340
  95.1 0.0 copy-done
  95.1 0.0 copy-done.1
  95.1 14.7 %lift.1 = bf16[64,512,128]{2,1,0:T(8,128)(2,1)} custom-call(s32[2,2,16]{2,1,0:T(2,128)S(1)} %copy-done.2, bf16[10,10,64,128]{3,2,1,0:T(8,128)(2,1)S(1)} %rim.1.rim_ref, bf16[64,512,128]{2,1,0:T(8,128)(2,1)} %bitcast.3, bf16[3,3,3,128,128]{4,3,2,1,0:T(8,128)(2,1)S(1)} %copy-done, bf16[2,2,2,128,128]{4,3,2,1,0:T(8,128)(2,1)S(1)} %copy-done.1), custom_call_target="tpu_custom_call" | custom-call | flops 5000000000 | bytes 18874368 | tf_op jit(solution)/shard_map/lift/pallas_call | solution.py:268
Async XLA Ops:
  0.0 0.7 copy-start.2
  0.7 1.2 %copy-start.3 = (bf16[8,128,512]{2,1,0:T(8,128)(2,1)S(1)}, bf16[8,128,512]{2,1,0:T(8,128)(2,1)}, u32[]{:S(2)}) copy-start(bf16[8,128,512]{2,1,0:T(8,128)(2,1)} %w_in_hbm.1) | copy-start | bytes 3145732
  1.9 1.2 %copy-start.4 = (bf16[8,512,128]{2,1,0:T(8,128)(2,1)S(1)}, bf16[8,512,128]{2,1,0:T(8,128)(2,1)}, u32[]{:S(2)}) copy-start(bf16[8,512,128]{2,1,0:T(8,128)(2,1)} %w_out_hbm.1) | copy-start | bytes 3145732
  3.1 0.9 copy-start.5
  4.1 0.7 copy-start.6
  4.8 0.7 copy-start.7
  5.5 89.6 %copy-start = (bf16[3,3,3,128,128]{4,3,2,1,0:T(8,128)(2,1)S(1)}, bf16[3,3,3,128,128]{4,3,2,1,0:T(8,128)(2,1)}, u32[]{:S(2)}) copy-start(bf16[3,3,3,128,128]{4,3,2,1,0:T(8,128)(2,1)} %w_conv_ref.1) | copy-start | bytes 2654212
  5.5 89.6 %copy-start.1 = (bf16[2,2,2,128,128]{4,3,2,1,0:T(8,128)(2,1)S(1)}, bf16[2,2,2,128,128]{4,3,2,1,0:T(8,128)(2,1)}, u32[]{:S(2)}) copy-start(bf16[2,2,2,128,128]{4,3,2,1,0:T(8,128)(2,1)} %w_up_ref.1) | copy-start | bytes 786436

commit v3 on v2

--- a/solution.py
+++ b/solution.py
@@ -70,62 +70,313 @@
         held = following
 
 
+def list_kernel(owner_ref, list_ref, count_ref):
+    cols_x, cols_y, zcap = owner_ref.shape
+    slots = cols_x * cols_y * zcap
+
+    def note(slot, n):
+        column, r = slot // zcap, lax.rem(slot, zcap)
+        alive = owner_ref[column // cols_y, lax.rem(column, cols_y), r] >= 0
+
+        @pl.when(alive)
+        def _():
+            list_ref[n] = slot
+
+        return n + alive.astype(jnp.int32)
+
+    def clear(k, _):
+        list_ref[k] = 0
+        return 0
+
+    lax.fori_loop(0, list_ref.shape[0], clear, 0)
+    total = lax.fori_loop(0, slots, note, 0)
+    list_ref[slots] = total
+    count_ref[...] = jnp.full(count_ref.shape, total, jnp.int32)
+
+
+def occupied(owner):
+    return pl.pallas_call(
+        list_kernel,
+        out_shape=(jax.ShapeDtypeStruct((128,), jnp.int32), jax.ShapeDtypeStruct((8, 128), jnp.int32)),
+        in_specs=[pl.BlockSpec(memory_space=pltpu.SMEM)],
+        out_specs=(pl.BlockSpec(memory_space=pltpu.SMEM), pl.BlockSpec(memory_space=pltpu.VMEM)),
+        name="occupied",
+    )(owner)
+
+
+PAIRS = ("x0", "y0", "z0", "x1", "y1", "z1", "c")
+CAPS = {"c": 4}
+NEAR = 3
+SWEEPS = 3
+
+
+def cap_of(name):
+    return CAPS.get(name, NEAR)
+
+
+BASES = {name: sum(cap_of(other) for other in PAIRS[:k]) for k, name in enumerate(PAIRS)}
+PLACES = sum(cap_of(name) for name in PAIRS)
+
+
+def partner_device(name):
+    gx, gy = lax.axis_index("gx"), lax.axis_index("gy")
+    if name == "c":
+        return (gx + 1 - 2 * lax.rem(gx, 2), gy)
+    parity = int(name[1])
+    if name[0] == "x":
+        sign = 1 - 2 * lax.rem(gx // 2 + parity, 2)
+        return (lax.rem(gx + 2 * sign + 8, 8), gy)
+    if name[0] == "y":
+        sign = 1 - 2 * lax.rem(gy // 4 + parity, 2)
+        return (gx, lax.rem(gy + 4 * sign + 16, 16))
+    sign = 1 - 2 * lax.rem(lax.rem(gy, 4) + parity, 2)
+    return (gx, (gy // 4) * 4 + lax.rem(lax.rem(gy, 4) + sign + 4, 4))
+
+
+def make_plan(count):
+    gx, gy = lax.axis_index("gx"), lax.axis_index("gy")
+    ax = lax.rem(lax.broadcasted_iota(jnp.int32, count.shape, 0) + gx, 8)
+    ay = lax.rem(lax.broadcasted_iota(jnp.int32, count.shape, 1) + gy, 16)
+    core, x, y, z = lax.rem(ax, 2), ax // 2, ay // 4, lax.rem(ay, 4)
+
+    def ahead(v, by, axis):
+        return pltpu.roll(v, (-by) % v.shape[axis], axis)
+
+    def partner(v, name, low):
+        if name == "c":
+            return jnp.where(low, ahead(v, 1, 0), ahead(v, -1, 0))
+        if name[0] == "x":
+            return jnp.where(low, ahead(v, 2, 0), ahead(v, -2, 0))
+        if name[0] == "y":
+            return jnp.where(low, ahead(v, 4, 1), ahead(v, -4, 1))
+        if name == "z0":
+            return jnp.where(low, ahead(v, 1, 1), ahead(v, -1, 1))
+        up = jnp.where(z == 3, ahead(v, -3, 1), ahead(v, 1, 1))
+        down = jnp.where(z == 0, ahead(v, 3, 1), ahead(v, -1, 1))
+        return jnp.where(low, up, down)
+
+    low = {"c": core == 0}
+    for k in range(2):
+        low.update({"x%d" % k: lax.rem(x, 2) == k, "y%d" % k: lax.rem(y, 2) == k, "z%d" % k: lax.rem(z, 2) == k})
+    flow = {name: jnp.zeros_like(count) for name in PAIRS}
+    load, spare = count, count
+    order = ("c", "x0", "y0", "z0", "x1", "y1", "z1")
+    for k in range(SWEEPS * len(order)):
+        name = order[k % len(order)]
+        up = k % 2
+        given = flow[name]
+        diff = load - partner(load, name, low[name])
+        limit = jnp.maximum(given, 0) + spare
+        want = given + jnp.where(low[name], (diff + up) >> 1, -((up - diff) >> 1))
+        want = jnp.clip(want, -cap_of(name), cap_of(name))
+        want = jnp.maximum(jnp.minimum(want, limit), -partner(limit, name, low[name]))
+        spare = limit - jnp.maximum(want, 0)
+        load = load + given - want
+        flow[name] = want
+    return flow
+
+
+def spread_kernel(
+    list_ref, count_ref, features_hbm, gain_ref, shift_ref, w_in_hbm, w_out_hbm,
+    plan_ref, got_hbm, wi_hbm, wo_hbm,
+    bricks_ref, send_ref, first_ref, second_ref, own_ref, plan_smem, w_in_ref, w_out_ref, wi_ref, wo_ref,
+    sems, count_send, count_recv, brick_send, brick_recv,
+):
+    gx, gy = lax.axis_index("gx"), lax.axis_index("gy")
+    eye = identity(w_out_ref.shape[2])
+    load_bricks = pltpu.make_async_copy(features_hbm, bricks_ref, sems.at[0])
+    load_in = pltpu.make_async_copy(w_in_hbm, w_in_ref, sems.at[1])
+    load_out = pltpu.make_async_copy(w_out_hbm, w_out_ref, sems.at[2])
+    load_in.start()
+    load_out.start()
+    load_bricks.start()
+
+    along_x = [(lax.rem(gx + k, 8), gy) for k in range(1, 8)]
+    along_y = [(gx, lax.rem(gy + k, 16)) for k in range(1, 16)]
+    barrier = pltpu.get_barrier_semaphore()
+    for device in along_x + along_y:
+        pl.semaphore_signal(barrier, inc=1, device_id=device, device_id_type=pl.DeviceIdType.MESH)
+    pl.semaphore_wait(barrier, len(along_x) + len(along_y))
+
+    def send(src, dst, send_sem, recv_sem, device):
+        copy = pltpu.make_async_remote_copy(
+            src_ref=src, dst_ref=dst, send_sem=send_sem, recv_sem=recv_sem,
+            device_id=device, device_id_type=pl.DeviceIdType.MESH,
+        )
+        copy.start()
+        return copy
+
+    copies = [
+        send(count_ref, first_ref.at[k], count_send.at[k], count_recv.at[k], along_x[k - 1]) for k in range(1, 8)
+    ]
+    load_in.wait()
+    load_out.wait()
+    for copy in copies:
+        copy.wait()
+    row = lax.broadcasted_iota(jnp.int32, count_ref.shape, 0)
+    lane = lax.rem(lax.broadcasted_iota(jnp.int32, count_ref.shape, 1), 16)
+    column = count_ref[...]
+    for k in range(1, 8):
+        column = jnp.where(row == 8 - k, first_ref[k], column)
+    own_ref[...] = column
+    copies = [
+        send(own_ref, second_ref.at[k], count_send.at[7 + k], count_recv.at[7 + k], along_y[k - 1])
+        for k in range(1, 16)
+    ]
+    prepare_weights(eye, gain_ref, shift_ref, w_in_ref, w_out_ref, wi_ref, wo_ref)
+    store_wi = pltpu.make_async_copy(wi_ref, wi_hbm, sems.at[1])
+    store_wo = pltpu.make_async_copy(wo_ref, wo_hbm, sems.at[2])
+    store_wi.start()
+    store_wo.start()
+    for copy in copies:
+        copy.wait()
+    counts = column
+    for k in range(1, 16):
+        counts = jnp.where(lane == 16 - k, second_ref[k], counts)
+
+    flow = make_plan(counts)
+    sent = jnp.zeros_like(counts)
+    got = jnp.zeros_like(counts)
+    for k, name in enumerate(PAIRS):
+        sent = jnp.where(row == k, pltpu.roll(jnp.maximum(flow[name], 0), k, 0), sent)
+        got = jnp.where(row == k, pltpu.roll(jnp.maximum(-flow[name], 0), k, 0), got)
+    plan_ref[0:8, :] = sent
+    plan_ref[8:16, :] = got
+    to_smem = pltpu.make_async_copy(plan_ref, plan_smem, sems.at[3])
+    to_smem.start()
+    load_bricks.wait()
+    to_smem.wait()
+
+    last = list_ref[64] - 1
+    copies = []
+    for k, name in enumerate(PAIRS):
+        for t in range(cap_of(name)):
+            slot = list_ref[jnp.clip(last - t, 0, 63)]
+            send_ref[BASES[name] + t] = bricks_ref[slot]
+        last = last - plan_smem[k, 0]
+        places = pl.ds(BASES[name], cap_of(name))
+        copies.append(
+            send(send_ref.at[places], got_hbm.at[places], brick_send.at[k], brick_recv.at[k], partner_device(name))
+        )
+    for copy in copies:
+        copy.wait()
+    store_wi.wait()
+    store_wo.wait()
+
+
+def spread(listed, count, features, gain, shift, w_in, w_out):
+    slots, voxels, chan = features.shape
+    layers, _, hid = w_in.shape
+    vmem = pl.BlockSpec(memory_space=pltpu.VMEM)
+    hbm = pl.BlockSpec(memory_space=pltpu.HBM)
+    return pl.pallas_call(
+        spread_kernel,
+        out_shape=(
+            jax.ShapeDtypeStruct((16, 128), jnp.int32),
+            jax.ShapeDtypeStruct((PLACES, voxels, chan), BF16),
+            jax.ShapeDtypeStruct((layers, hid, 2 * chan), BF16),
+            jax.ShapeDtypeStruct((layers, chan, hid), BF16),
+        ),
+        in_specs=[pl.BlockSpec(memory_space=pltpu.SMEM), vmem, hbm, vmem, vmem, hbm, hbm],
+        out_specs=(vmem, hbm, hbm, hbm),
+        scratch_shapes=[
+            pltpu.VMEM(features.shape, BF16),
+            pltpu.VMEM((PLACES, voxels, chan), BF16),
+            pltpu.VMEM((8, 8, 128), jnp.int32),
+            pltpu.VMEM((16, 8, 128), jnp.int32),
+            pltpu.VMEM((8, 128), jnp.int32),
+            pltpu.SMEM((16, 128), jnp.int32),
+            pltpu.VMEM(w_in.shape, BF16),
+            pltpu.VMEM(w_out.shape, BF16),
+            pltpu.VMEM((layers, hid, 2 * chan), BF16),
+            pltpu.VMEM((layers, chan, hid), BF16),
+            pltpu.SemaphoreType.DMA((4,)),
+            pltpu.SemaphoreType.DMA((23,)),
+            pltpu.SemaphoreType.DMA((23,)),
+            pltpu.SemaphoreType.DMA((7,)),
+            pltpu.SemaphoreType.DMA((7,)),
+        ],
+        compiler_params=pltpu.CompilerParams(
+            collective_id=0, has_side_effects=True, vmem_limit_bytes=48 * 2**20
+        ),
+        name="spread",
+    )(listed, count, features, gain, shift, w_in, w_out)
+
+
 def coarse_kernel(
-    owner_ref, features_ref, gain_ref, shift_ref, w_in_hbm, w_out_hbm, w_down_hbm,
-    out_ref,
-    list_ref, buf_ref, s_ref, t_ref, wi_ref, wo_ref, grid_ref, w_in_ref, w_out_ref, w_down_ref, sems, w_sems,
+    list_ref, plan_ref, features_ref, got_ref, wi_hbm, wo_hbm, w_down_hbm,
+    out_ref, back_ref, map_ref,
+    place_ref, buf_ref, s_ref, t_ref, grid_ref, wi_ref, wo_ref, w_down_ref, sems, w_sems,
 ):
-    _, cols_y, zcap = owner_ref.shape
-    slots = out_ref.shape[2]
+    zcap = 16
     chan = s_ref.shape[0]
     eye = identity(chan)
     weights = [
         pltpu.make_async_copy(src, dst, w_sems.at[n])
-        for n, (src, dst) in enumerate(((w_in_hbm, w_in_ref), (w_out_hbm, w_out_ref), (w_down_hbm, w_down_ref)))
+        for n, (src, dst) in enumerate(((wi_hbm, wi_ref), (wo_hbm, wo_ref), (w_down_hbm, w_down_ref)))
     ]
     for w in weights:
         w.start()
 
-    def note(slot, n):
-        column, r = slot // zcap, lax.rem(slot, zcap)
-        alive = owner_ref[column // cols_y, lax.rem(column, cols_y), r] >= 0
-
-        @pl.when(alive)
-        def _():
-            list_ref[n] = slot
-
-        return n + alive.astype(jnp.int32)
-
-    total = lax.fori_loop(0, slots, note, 0)
+    def clear(k, _):
+        map_ref[k] = -1
+        return 0
+
+    lax.fori_loop(0, map_ref.shape[0], clear, 0)
+    kept, others = list_ref[64], 0
+    for k, name in enumerate(PAIRS):
+        sent, came = plan_ref[k, 0], plan_ref[8 + k, 0]
+        for t in range(cap_of(name)):
+
+            @pl.when(t < sent)
+            def _():
+                map_ref[list_ref[kept - 1 - t]] = BASES[name] + t
+
+            @pl.when(t < came)
+            def _():
+                place_ref[others + t] = BASES[name] + t
+
+        kept, others = kept - sent, others + came
+    total = kept + others
     groups = (total + GROUP - 1) // GROUP
 
-    def brick(g, t):
-        return list_ref[jnp.minimum(g * GROUP + t, total - 1)]
-
-    def copy(g, t):
-        return pltpu.make_async_copy(
-            features_ref.at[brick(g, t)], buf_ref.at[lax.rem(g, 2), t], sems.at[lax.rem(g, 2), t]
+    def copies(g, t):
+        k = jnp.minimum(g * GROUP + t, total - 1)
+        half = lax.rem(g, 2)
+        own = pltpu.make_async_copy(features_ref.at[list_ref[jnp.clip(k, 0, 63)]], buf_ref.at[half, t], sems.at[half, t])
+        other = pltpu.make_async_copy(
+            got_ref.at[place_ref[jnp.clip(k - kept, 0, PLACES - 1)]], buf_ref.at[half, t], sems.at[half, t]
         )
+        return k, own, other
+
+    def fetch(g):
+        for t in range(GROUP):
+            k, own, other = copies(g, t)
+
+            @pl.when(k < kept)
+            def _():
+                own.start()
+
+            @pl.when(k >= kept)
+            def _():
+                other.start()
 
     @pl.when(groups > 0)
     def _():
-        for t in range(GROUP):
-            copy(0, t).start()
+        fetch(0)
 
     grid_ref[...] = jnp.zeros_like(grid_ref)
     for w in weights:
         w.wait()
-    prepare_weights(eye, gain_ref, shift_ref, w_in_ref, w_out_ref, wi_ref, wo_ref)
     half = lax.broadcasted_iota(jnp.int32, (16, 8, 1), 1) // 4
 
     def body(g, _):
         @pl.when(g + 1 < groups)
         def _():
-            for t in range(GROUP):
-                copy(g + 1, t).start()
+            fetch(g + 1)
 
         for t in range(GROUP):
-            copy(g, t).wait()
+            pltpu.make_async_copy(features_ref.at[0], buf_ref.at[lax.rem(g, 2), t], sems.at[lax.rem(g, 2), t]).wait()
         for t in range(GROUP):
             s_ref[:, t * 512 : (t + 1) * 512] = transposed(eye, buf_ref[lax.rem(g, 2), t])
         feed_forward(s_ref, wi_ref, wo_ref)
@@ -140,23 +391,29 @@
                     rows = jnp.concatenate(
                         [t_ref[t, pl.ds(128 * i + 64 * a + c, 32, stride=2), :] for i in range(4)], axis=0
                     ).astype(BF16)
-                    weights = jnp.concatenate([w_down_ref[a, 0, c], w_down_ref[a, 1, c]], axis=1)
-                    total_down += jnp.dot(rows, weights, preferred_element_type=F32)
+                    both_b = jnp.concatenate([w_down_ref[a, 0, c], w_down_ref[a, 1, c]], axis=1)
+                    total_down += jnp.dot(rows, both_b, preferred_element_type=F32)
             both = total_down.reshape(16, 8, 2 * chan)
             own = jnp.where(half == 0, both[:, :, :chan], both[:, :, chan:])
             down = own + jnp.concatenate([own[:, 4:, :], own[:, :4, :]], axis=1)
             made = down / (1.0 + jnp.exp(-down))
-            slot = brick(g, t)
-            column, r = slot // zcap, lax.rem(slot, zcap)
-            x0, y0, zpair, odd = (column // 2) * 4, lax.rem(column, 2) * 4, r // 2, lax.rem(r, 2)
-
-            @pl.when(g * GROUP + t < total)
+            k = g * GROUP + t
+
+            @pl.when(k < kept)
             def _():
+                slot = list_ref[jnp.minimum(k, 63)]
+                column, r = slot // zcap, lax.rem(slot, zcap)
+                x0, y0, zpair, odd = (column // 2) * 4, lax.rem(column, 2) * 4, r // 2, lax.rem(r, 2)
                 for i in range(4):
                     for j in range(4):
                         old = grid_ref[x0 + i, y0 + j, zpair]
                         grid_ref[x0 + i, y0 + j, zpair] = jnp.where(half[0] == odd, made[4 * i + j], old)
 
+            @pl.when((k >= kept) & (k < total))
+            def _():
+                place = place_ref[jnp.clip(k - kept, 0, PLACES - 1)]
+                back_ref[place] = made.reshape(128, chan).astype(BF16)
+
         return 0
 
     lax.fori_loop(0, groups, body, 0)
@@ -168,34 +425,36 @@
     lax.fori_loop(0, out_ref.shape[0], finish, 0)
 
 
-def coarse_grid(features, owner, gain, shift, w_in, w_out, w_down):
+def coarse_grid(listed, plan, features, got, wi, wo, w_down):
     slots, voxels, chan = features.shape
-    layers, _, hid = w_in.shape
     vmem = pl.BlockSpec(memory_space=pltpu.VMEM)
-    hbm = pl.BlockSpec(memory_space=pl.ANY)
+    hbm = pl.BlockSpec(memory_space=pltpu.HBM)
+    smem = pl.BlockSpec(memory_space=pltpu.SMEM)
     return pl.pallas_call(
         coarse_kernel,
-        out_shape=jax.ShapeDtypeStruct((8, 8, slots, chan), BF16),
-        in_specs=[pl.BlockSpec(memory_space=pltpu.SMEM), hbm, vmem, vmem, hbm, hbm, hbm],
-        out_specs=vmem,
+        out_shape=(
+            jax.ShapeDtypeStruct((8, 8, slots, chan), BF16),
+            jax.ShapeDtypeStruct((PLACES, 128, chan), BF16),
+            jax.ShapeDtypeStruct((slots,), jnp.int32),
+        ),
+        in_specs=[smem, smem, hbm, hbm, hbm, hbm, hbm],
+        out_specs=(vmem, vmem, smem),
         scratch_shapes=[
-            pltpu.SMEM((slots,), jnp.int32),
+            pltpu.SMEM((PLACES,), jnp.int32),
             pltpu.VMEM((2, GROUP, voxels, chan), BF16),
             pltpu.VMEM((chan, GROUP * voxels), F32),
             pltpu.VMEM((GROUP, voxels, chan), F32),
-            pltpu.VMEM((layers, hid, 2 * chan), BF16),
-            pltpu.VMEM((layers, chan, hid), BF16),
             pltpu.VMEM((8, 8, slots // 8, 8, chan), F32),
-            pltpu.VMEM(w_in.shape, BF16),
-            pltpu.VMEM(w_out.shape, BF16),
+            pltpu.VMEM(wi.shape, BF16),
+            pltpu.VMEM(wo.shape, BF16),
             pltpu.VMEM(w_down.shape, BF16),
             pltpu.SemaphoreType.DMA((2, GROUP)),
             pltpu.SemaphoreType.DMA((3,)),
         ],
         compiler_params=pltpu.CompilerParams(vmem_limit_bytes=48 * 2**20),
-        cost_estimate=pl.CostEstimate(flops=32 * 10**9, bytes_accessed=8 * 2**20, transcendentals=10**8),
+        cost_estimate=pl.CostEstimate(flops=17 * 10**9, bytes_accessed=8 * 2**20, transcendentals=10**8),
         name="coarse",
-    )(owner, features, gain, shift, w_in, w_out, w_down)
+    )(listed, plan, features, got, wi, wo, w_down)
 
 
 def lift_kernel(
@@ -281,39 +540,76 @@
     )(owner, rim, features, w_conv, w_up)
 
 
-def rim_kernel(grid_ref, out_ref, send_sems, recv_sems):
-    gsx, gsy = grid_ref.shape[:2]
+def rim_kernel(
+    map_ref, grid_ref, back_ref,
+    out_ref,
+    whole_ref, home_ref, send_sems, recv_sems,
+):
+    gsx, gsy, gsz, chan = grid_ref.shape
     gx, gy = lax.axis_index("gx"), lax.axis_index("gy")
     nx, ny = lax.axis_size("gx"), lax.axis_size("gy")
     sides = [(dx, dy) for dx in (-1, 0, 1) for dy in (-1, 0, 1) if (dx, dy) != (0, 0)]
-
-    def device(dx, dy):
-        return (lax.rem(gx + dx + nx, nx), lax.rem(gy + dy + ny, ny))
+    devices = [(lax.rem(gx + dx + nx, nx), lax.rem(gy + dy + ny, ny)) for dx, dy in sides]
+    partners = [partner_device(name) for name in PAIRS]
 
     barrier = pltpu.get_barrier_semaphore()
-    for side in sides:
-        pl.semaphore_signal(barrier, inc=1, device_id=device(*side), device_id_type=pl.DeviceIdType.MESH)
-    pl.semaphore_wait(barrier, len(sides))
+    for device in devices + partners:
+        pl.semaphore_signal(barrier, inc=1, device_id=device, device_id_type=pl.DeviceIdType.MESH)
+    pl.semaphore_wait(barrier, len(devices) + len(partners))
+
+    def send(n, src, dst, device):
+        copy = pltpu.make_async_remote_copy(
+            src_ref=src, dst_ref=dst, send_sem=send_sems.at[n], recv_sem=recv_sems.at[n],
+            device_id=device, device_id_type=pl.DeviceIdType.MESH,
+        )
+        copy.start()
+        return copy
+
+    copies = []
+    for k, name in enumerate(PAIRS):
+        places = pl.ds(BASES[name], cap_of(name))
+        copies.append(send(len(sides) + k, back_ref.at[places], home_ref.at[places], partners[k]))
+    for copy in copies:
+        copy.wait()
+
+    odd = lax.broadcasted_iota(jnp.int32, (16, 8, chan), 1) // 4
+    for column in range(4):
+        x0, y0 = (column // 2) * 4, (column % 2) * 4
+
+        def merge(m, _):
+            zs = pl.ds(pl.multiple_of(m * 16, 16), 16)
+            old = grid_ref[x0 : x0 + 4, y0 : y0 + 4, zs, :].astype(F32).reshape(16, 16, chan)
+            new = []
+            for pair in range(2):
+                value = old[:, 8 * pair : 8 * pair + 8, :]
+                for side in range(2):
+                    place = map_ref[column * 16 + m * 4 + 2 * pair + side]
+                    brick = home_ref[jnp.maximum(place, 0)].astype(F32).reshape(16, 8, chan)
+                    taken = jnp.full((16, 8, chan), place, jnp.int32) >= 0
+                    value = jnp.where(taken & (odd == side), brick, value)
+                new.append(value)
+            merged = jnp.concatenate(new, axis=1).reshape(4, 4, 16, chan).astype(BF16)
+            whole_ref[x0 : x0 + 4, y0 : y0 + 4, zs, :] = merged
+            return 0
+
+        lax.fori_loop(0, gsz // 16, merge, 0)
 
     def cut(side, size):
         return {-1: pl.ds(0, 1), 0: pl.ds(0, size), 1: pl.ds(size - 1, 1)}[side]
 
-    def place(side, size):
+    def place_of(side, size):
         return {-1: pl.ds(size + 1, 1), 0: pl.ds(1, size), 1: pl.ds(0, 1)}[side]
 
-    copies = []
-    for n, (dx, dy) in enumerate(sides):
-        copy = pltpu.make_async_remote_copy(
-            src_ref=grid_ref.at[cut(dx, gsx), cut(dy, gsy)],
-            dst_ref=out_ref.at[place(dx, gsx), place(dy, gsy)],
-            send_sem=send_sems.at[n],
-            recv_sem=recv_sems.at[n],
-            device_id=device(dx, dy),
-            device_id_type=pl.DeviceIdType.MESH,
+    copies = [
+        send(
+            n,
+            whole_ref.at[cut(dx, gsx), cut(dy, gsy)],
+            out_ref.at[place_of(dx, gsx), place_of(dy, gsy)],
+            devices[n],
         )
-        copy.start()
-        copies.append(copy)
-    out_ref[pl.ds(1, gsx), pl.ds(1, gsy)] = grid_ref[...]
+        for n, (dx, dy) in enumerate(sides)
+    ]
+    out_ref[pl.ds(1, gsx), pl.ds(1, gsy)] = whole_ref[...]
     for copy in copies:
         copy.wait()
 
@@ -334,27 +630,34 @@
         out_ref[:, gsy + 1] = jnp.zeros_like(out_ref[:, gsy + 1])
 
 
-def with_rim(grid):
+def with_rim(where, grid, back):
     gsx, gsy, gsz, chan = grid.shape
     vmem = pl.BlockSpec(memory_space=pltpu.VMEM)
     return pl.pallas_call(
         rim_kernel,
         out_shape=jax.ShapeDtypeStruct((gsx + 2, gsy + 2, gsz, chan), BF16),
-        in_specs=[vmem],
+        in_specs=[pl.BlockSpec(memory_space=pltpu.SMEM), vmem, vmem],
         out_specs=vmem,
-        scratch_shapes=[pltpu.SemaphoreType.DMA((8,)), pltpu.SemaphoreType.DMA((8,))],
+        scratch_shapes=[
+            pltpu.VMEM(grid.shape, BF16),
+            pltpu.VMEM(back.shape, BF16),
+            pltpu.SemaphoreType.DMA((15,)),
+            pltpu.SemaphoreType.DMA((15,)),
+        ],
         compiler_params=pltpu.CompilerParams(
-            collective_id=0, has_side_effects=True, vmem_limit_bytes=32 * 2**20
+            collective_id=1, has_side_effects=True, vmem_limit_bytes=32 * 2**20
         ),
         name="rim",
-    )(grid)
+    )(where, grid, back)
 
 
 def local(features, owner, norm_gain, time_shift, w_in, w_out, w_down, w_conv, w_up):
     cols_x, cols_y, zcap, voxels, chan = features.shape
     flat = features.reshape(cols_x * cols_y * zcap, voxels, chan)
-    grid = coarse_grid(flat, owner, norm_gain, time_shift, w_in, w_out, w_down)
-    result = lift(owner, with_rim(grid), flat, w_conv, w_up)
+    listed, count = occupied(owner)
+    plan, got, wi, wo = spread(listed, count, flat, norm_gain, time_shift, w_in, w_out)
+    grid, back, where = coarse_grid(listed, plan, flat, got, wi, wo, w_down)
+    result = lift(owner, with_rim(where, grid, back), flat, w_conv, w_up)
     return result.reshape(features.shape)
 
 

time: 110 us -> 118 us (1.073)
  Pallas kernels: 104 us -> 112 us
    pallas_call x1, Pallas kernels: 13.3 us -> 25.4 us  [with_rim(): pl.pallas_call(rim_kernel, out_shape=jax.ShapeDtypeStruct((gsx + 2, gsy +...]
    pallas_call x1 -> x3, Pallas kernels: 76.3 us -> 72.1 us  [the longest x1 39 us: coarse_grid(): pl.pallas_call(coarse_kernel, out_shape=(jax.ShapeDtypeStruct((8, 8, slot...]
    unnamed x16 -> x20, local copies, waits for them, and re-layouts: 5.49 us -> 5.17 us
where the time goes in v3:
time: 118 us
  Pallas kernels  112 us (95%)
  local copies, waits for them, and re-layouts  5.17 us (4%)
    pallas_call x1, Pallas kernels, coarse_grid(): pl.pallas_call(coarse_kernel, out_shape=(jax.ShapeDtypeStruct((8, 8, slot...  39 us
    pallas_call x1, Pallas kernels, spread(): pl.pallas_call(spread_kernel, out_shape=(jax.ShapeDtypeStruct((16, 128),...  29.5 us
    pallas_call x1, Pallas kernels, with_rim(): pl.pallas_call(rim_kernel, out_shape=jax.ShapeDtypeStruct((gsx + 2, gsy +...  25.4 us
    pallas_call x1, Pallas kernels, lift(): pl.pallas_call(lift_kernel, grid=(columns,), out_shape=jax.ShapeDtypeStru...  14.8 us
    unnamed x20, local copies, waits for them, and re-layouts  5.17 us
    pallas_call x1, Pallas kernels, occupied(): pl.pallas_call(list_kernel, out_shape=(jax.ShapeDtypeStruct((128,), jnp.i...  3.68 us

profile of v3, /device:TPU:1, one launch (start us, length us, event | category | flops | bytes accessed | tf_op | source)
XLA Modules:
  0.0 117.6 jit_solution(7487776537932518074)
XLA Ops:
  0.0 3.7 %occupied.1 = (s32[128]{0:T(128)}, s32[8,128]{1,0:T(8,128)}) custom-call(s32[2,2,16]{2,1,0:T(2,128)} %owner_ref.3), custom_call_target="tpu_custom_call" | custom-call | tf_op jit(solution)/shard_map/occupied/pallas_call | solution.py:98
  3.7 0.0 copy-start
  3.7 1.2 %copy-done = bf16[8,128,512]{2,1,0:T(8,128)(2,1)S(1)} copy-done((bf16[8,128,512]{2,1,0:T(8,128)(2,1)S(1)}, bf16[8,128,512]{2,1,0:T(8,128)(2,1)}, u32[]{:S(2)}) %copy-start) | copy-done | bytes 1048600
  4.9 0.0 copy-start.1
  4.9 1.2 %copy-done.1 = bf16[8,512,128]{2,1,0:T(8,128)(2,1)S(1)} copy-done((bf16[8,512,128]{2,1,0:T(8,128)(2,1)S(1)}, bf16[8,512,128]{2,1,0:T(8,128)(2,1)}, u32[]{:S(2)}) %copy-start.1) | copy-done | bytes 1048600
  6.1 0.0 copy-start.4
  6.1 0.7 copy-done.4
  6.9 0.0 copy-start.6
  6.9 0.7 copy-done.6
  7.5 0.0 copy-start.7
  7.5 0.7 copy-done.7
  8.2 0.0 copy-start.8
  8.2 0.6 copy-done.8
  8.8 0.0 copy-start.9
  8.9 29.5 %spread.1 = (s32[16,128]{1,0:T(8,128)S(1)}, bf16[22,512,128]{2,1,0:T(8,128)(2,1)}, bf16[8,512,256]{2,1,0:T(8,128)(2,1)S(1)}, bf16[8,128,512]{2,1,0:T(8,128)(2,1)S(1)}) custom-call(s32[128]{0:T(128)S(1)} %copy-done.8, s32[8,128]{1,0:T(8,128)S(1)} %copy-done.7, bf16[64,512,128]{2,1,0:T(8,128)(2,1)} %bitcast.2, f32[8,128]{1,0:T(8,128)S(1)} %copy-done.6, ...), custom_call_target="tpu_custom_call" | custom-call | tf_op jit(solution)/shard_map/spread/pallas_call | solution.py:272
  38.3 0.0 copy-done.9
  38.3 39.0 %coarse.1 = (bf16[8,8,64,128]{3,2,1,0:T(8,128)(2,1)S(1)}, bf16[22,128,128]{2,1,0:T(8,128)(2,1)S(1)}, s32[64]{0:T(128)S(1)}) custom-call(s32[128]{0:T(128)S(1)} %copy-done.8, s32[16,128]{1,0:T(8,128)S(1)} %get-tuple-element.16.plan_ref, bf16[64,512,128]{2,1,0:T(8,128)(2,1)} %bitcast.3, bf16[22,512,128]{2,1,0:T(8,128)(2,1)} %get-tuple-element.17.got_ref, ...), custom_call_target="tpu_custom_call" | custom-call | flops 16999999488 | bytes 8388608 | tf_op jit(solution)/shard_map/coarse/pallas_call | solution.py:433
  77.3 0.0 copy-start.2
  77.4 0.0 copy-start.3
  77.4 0.0 copy-start.5
  77.4 25.4 %rim.1.rim_ref = bf16[10,10,64,128]{3,2,1,0:T(8,128)(2,1)S(1)} custom-call(s32[64]{0:T(128)S(1)} %get-tuple-element.20.map_ref, bf16[8,8,64,128]{3,2,1,0:T(8,128)(2,1)S(1)} %get-tuple-element.21.grid_ref, bf16[22,128,128]{2,1,0:T(8,128)(2,1)S(1)} %get-tuple-element.22.back_ref), custom_call_target="tpu_custom_call" | custom-call | tf_op jit(solution)/shard_map/rim/pallas_call | solution.py:636
  102.7 0.0 copy-done.2
  102.8 0.0 copy-done.3
  102.8 0.0 copy-done.5
  102.8 14.8 %lift.1 = bf16[64,512,128]{2,1,0:T(8,128)(2,1)} custom-call(s32[2,2,16]{2,1,0:T(2,128)S(1)} %copy-done.5, bf16[10,10,64,128]{3,2,1,0:T(8,128)(2,1)S(1)} %rim.1.rim_ref, bf16[64,512,128]{2,1,0:T(8,128)(2,1)} %bitcast.4, bf16[3,3,3,128,128]{4,3,2,1,0:T(8,128)(2,1)S(1)} %copy-done.2, bf16[2,2,2,128,128]{4,3,2,1,0:T(8,128)(2,1)S(1)} %copy-done.3), custom_call_target="tpu_custom_call" | custom-call | flops 5000000000 | bytes 18874368 | tf_op jit(solution)/shard_map/lift/pallas_call | solution.py:527
Async XLA Ops:
  3.7 1.2 %copy-start = (bf16[8,128,512]{2,1,0:T(8,128)(2,1)S(1)}, bf16[8,128,512]{2,1,0:T(8,128)(2,1)}, u32[]{:S(2)}) copy-start(bf16[8,128,512]{2,1,0:T(8,128)(2,1)} %w_in_hbm.1) | copy-start | bytes 3145732
  4.9 1.2 %copy-start.1 = (bf16[8,512,128]{2,1,0:T(8,128)(2,1)S(1)}, bf16[8,512,128]{2,1,0:T(8,128)(2,1)}, u32[]{:S(2)}) copy-start(bf16[8,512,128]{2,1,0:T(8,128)(2,1)} %w_out_hbm.1) | copy-start | bytes 3145732
  6.1 0.7 copy-start.4
  6.9 0.7 copy-start.6
  7.5 0.7 copy-start.7
  8.2 0.6 copy-start.8
  8.8 29.5 %copy-start.9 = (bf16[2,2,2,128,128]{4,3,2,1,0:T(8,128)(2,1)S(1)}, bf16[2,2,2,128,128]{4,3,2,1,0:T(8,128)(2,1)}, u32[]{:S(2)}) copy-start(bf16[2,2,2,128,128]{4,3,2,1,0:T(8,128)(2,1)} %w_down_hbm.1) | copy-start | bytes 786436
  77.3 25.4 %copy-start.2 = (bf16[3,3,3,128,128]{4,3,2,1,0:T(8,128)(2,1)S(1)}, bf16[3,3,3,128,128]{4,3,2,1,0:T(8,128)(2,1)}, u32[]{:S(2)}) copy-start(bf16[3,3,3,128,128]{4,3,2,1,0:T(8,128)(2,1)} %w_conv_ref.1) | copy-start | bytes 2654212
  77.4 25.4 %copy-start.3 = (bf16[2,2,2,128,128]{4,3,2,1,0:T(8,128)(2,1)S(1)}, bf16[2,2,2,128,128]{4,3,2,1,0:T(8,128)(2,1)}, u32[]{:S(2)}) copy-start(bf16[2,2,2,128,128]{4,3,2,1,0:T(8,128)(2,1)} %w_up_ref.1) | copy-start | bytes 786436
  77.4 25.4 %copy-start.5 = (s32[2,2,16]{2,1,0:T(2,128)S(1)}, s32[2,2,16]{2,1,0:T(2,128)}, u32[]{:S(2)}) copy-start(s32[2,2,16]{2,1,0:T(2,128)} %owner_ref.3) | copy-start | bytes 772

commit v4 on v3

--- a/solution.py
+++ b/solution.py
@@ -9,7 +9,7 @@
 
 BF16 = jnp.bfloat16
 F32 = jnp.float32
-GROUP = 4
+GROUP = 3
 CHUNK = 512
 
 
@@ -22,8 +22,8 @@
     return (rows == lax.broadcasted_iota(jnp.int32, (n, n), 1)).astype(BF16)
 
 
-def prepare_weights(eye, gain_ref, shift_ref, w_in_ref, w_out_ref, wi_ref, wo_ref):
-    layers, chan, hid = w_in_ref.shape
+def prepare_weights(first, last, eye, gain_ref, shift_ref, w_in_ref, w_out_ref, wi_ref, wo_ref):
+    _, chan, hid = w_in_ref.shape
     row = lax.broadcasted_iota(jnp.int32, (chan, hid), 0)
 
     def one(l, _):
@@ -42,72 +42,71 @@
             wo_ref[l, :, cut] = transposed(eye, w_out[cut, :]).astype(BF16)
         return 0
 
-    lax.fori_loop(0, layers, one, 0)
-
-
-def feed_forward(s_ref, wi_ref, wo_ref):
+    lax.fori_loop(first, last, one, 0)
+
+
+def hidden_units(x, ones, wi):
+    scale = lax.rsqrt(jnp.mean(x * x, axis=0, keepdims=True) + 1e-06)
+    normed = jnp.concatenate([(x * scale).astype(BF16), ones], axis=0)
+    u = jnp.dot(wi, normed, preferred_element_type=F32)
+    return (u * jnp.tanh(u) + u).astype(BF16)
+
+
+def feed_forward(s_ref, wi_ref, wo_ref, unrolled):
     layers = wi_ref.shape[0]
     chan, width = s_ref.shape
     count = width // CHUNK
     ones = jnp.ones((chan, CHUNK), BF16)
 
-    def hidden(step):
-        l, c = divmod(step, count)
-        x = s_ref[:, c * CHUNK : (c + 1) * CHUNK]
-        scale = lax.rsqrt(jnp.mean(x * x, axis=0, keepdims=True) + 1e-06)
-        normed = jnp.concatenate([(x * scale).astype(BF16), ones], axis=0)
-        u = jnp.dot(wi_ref[l], normed, preferred_element_type=F32)
-        return (u * jnp.tanh(u) + u).astype(BF16)
-
-    def update(step, h):
-        l, c = divmod(step, count)
+    def hidden(l, c):
+        return hidden_units(s_ref[:, c * CHUNK : (c + 1) * CHUNK], ones, wi_ref[l])
+
+    def update(l, c, h):
         s_ref[:, c * CHUNK : (c + 1) * CHUNK] += jnp.dot(wo_ref[l], h, preferred_element_type=F32)
 
-    held = hidden(0)
-    for step in range(layers * count):
-        following = hidden(step + 1) if step + 1 < layers * count else None
-        update(step, held)
-        held = following
-
-
-def list_kernel(owner_ref, list_ref, count_ref):
-    cols_x, cols_y, zcap = owner_ref.shape
-    slots = cols_x * cols_y * zcap
-
-    def note(slot, n):
-        column, r = slot // zcap, lax.rem(slot, zcap)
-        alive = owner_ref[column // cols_y, lax.rem(column, cols_y), r] >= 0
-
-        @pl.when(alive)
-        def _():
-            list_ref[n] = slot
-
-        return n + alive.astype(jnp.int32)
-
-    def clear(k, _):
-        list_ref[k] = 0
-        return 0
-
-    lax.fori_loop(0, list_ref.shape[0], clear, 0)
-    total = lax.fori_loop(0, slots, note, 0)
-    list_ref[slots] = total
-    count_ref[...] = jnp.full(count_ref.shape, total, jnp.int32)
-
-
-def occupied(owner):
-    return pl.pallas_call(
-        list_kernel,
-        out_shape=(jax.ShapeDtypeStruct((128,), jnp.int32), jax.ShapeDtypeStruct((8, 128), jnp.int32)),
-        in_specs=[pl.BlockSpec(memory_space=pltpu.SMEM)],
-        out_specs=(pl.BlockSpec(memory_space=pltpu.SMEM), pl.BlockSpec(memory_space=pltpu.VMEM)),
-        name="occupied",
-    )(owner)
+    def run(steps):
+        held = hidden(*steps[0])
+        for k, step in enumerate(steps):
+            following = hidden(*steps[k + 1]) if k + 1 < len(steps) else None
+            update(*step, held)
+            held = following
+
+    if unrolled:
+        run([divmod(step, count) for step in range(layers * count)])
+    else:
+
+        def layer(l, _):
+            run([(l, c) for c in range(count)])
+            return 0
+
+        lax.fori_loop(0, layers, layer, 0)
+
+
+def reduced(t, eye, s_ref, t_ref, w_down_ref):
+    chan = s_ref.shape[0]
+    half = lax.broadcasted_iota(jnp.int32, (16, 8, 1), 1) // 4
+    for m in range(4):
+        block = s_ref[:, t * 512 + m * 128 : t * 512 + (m + 1) * 128].astype(BF16)
+        t_ref[t, m * 128 : (m + 1) * 128, :] = transposed(eye, block)
+    total = jnp.zeros((128, 2 * chan), F32)
+    for a in range(2):
+        for c in range(2):
+            rows = jnp.concatenate(
+                [t_ref[t, pl.ds(128 * i + 64 * a + c, 32, stride=2), :] for i in range(4)], axis=0
+            ).astype(BF16)
+            both_b = jnp.concatenate([w_down_ref[a, 0, c], w_down_ref[a, 1, c]], axis=1)
+            total += jnp.dot(rows, both_b, preferred_element_type=F32)
+    both = total.reshape(16, 8, 2 * chan)
+    own = jnp.where(half == 0, both[:, :, :chan], both[:, :, chan:])
+    down = own + jnp.concatenate([own[:, 4:, :], own[:, :4, :]], axis=1)
+    return down / (1.0 + jnp.exp(-down))
 
 
 PAIRS = ("x0", "y0", "z0", "x1", "y1", "z1", "c")
 CAPS = {"c": 4}
 NEAR = 3
 SWEEPS = 3
+FULL_VMEM = 127 * 2**19
 
 
 def cap_of(name):
@@ -177,25 +176,52 @@
 
 
 def spread_kernel(
-    list_ref, count_ref, features_hbm, gain_ref, shift_ref, w_in_hbm, w_out_hbm,
-    plan_ref, got_hbm, wi_hbm, wo_hbm,
-    bricks_ref, send_ref, first_ref, second_ref, own_ref, plan_smem, w_in_ref, w_out_ref, wi_ref, wo_ref,
+    owner_ref, features_hbm, gain_hbm, shift_hbm, w_in_hbm, w_out_hbm, w_down_hbm,
+    plan_ref, early_ref, got_hbm, wi_hbm, wo_hbm,
+    bricks_ref, send_ref, count_ref, first_ref, second_ref, own_ref, pick_ref, pick_smem,
+    gain_ref, shift_ref, w_in_ref, w_out_ref, w_down_ref, wi_ref, wo_ref, s_ref, t_ref,
     sems, count_send, count_recv, brick_send, brick_recv,
 ):
     gx, gy = lax.axis_index("gx"), lax.axis_index("gy")
+    cols_x, cols_y, zcap = owner_ref.shape
+    layers = w_in_ref.shape[0]
     eye = identity(w_out_ref.shape[2])
-    load_bricks = pltpu.make_async_copy(features_hbm, bricks_ref, sems.at[0])
-    load_in = pltpu.make_async_copy(w_in_hbm, w_in_ref, sems.at[1])
-    load_out = pltpu.make_async_copy(w_out_hbm, w_out_ref, sems.at[2])
-    load_in.start()
-    load_out.start()
-    load_bricks.start()
+    loads = [
+        pltpu.make_async_copy(src, dst, sems.at[n])
+        for n, (src, dst) in enumerate(
+            (
+                (gain_hbm, gain_ref),
+                (shift_hbm, shift_ref),
+                (w_in_hbm, w_in_ref),
+                (w_out_hbm, w_out_ref),
+                (w_down_hbm, w_down_ref),
+                (features_hbm, bricks_ref),
+            )
+        )
+    ]
+    for load in loads:
+        load.start()
 
     along_x = [(lax.rem(gx + k, 8), gy) for k in range(1, 8)]
     along_y = [(gx, lax.rem(gy + k, 16)) for k in range(1, 16)]
     barrier = pltpu.get_barrier_semaphore()
     for device in along_x + along_y:
         pl.semaphore_signal(barrier, inc=1, device_id=device, device_id_type=pl.DeviceIdType.MESH)
+
+    row = lax.broadcasted_iota(jnp.int32, count_ref.shape, 0)
+    lane = lax.broadcasted_iota(jnp.int32, count_ref.shape, 1)
+    alive = jnp.zeros_like(lane)
+    total = 0
+    for slot in range(cols_x * cols_y * zcap):
+        column, r = divmod(slot, zcap)
+        mark = (owner_ref[column // cols_y, column % cols_y, r] >= 0).astype(jnp.int32)
+        alive = jnp.where(lane == slot, mark, alive)
+        total = total + mark
+    order = alive
+    for by in (1, 2, 4, 8, 16, 32):
+        order = order + jnp.where(lane >= by, pltpu.roll(order, by, 1), 0)
+    order = order - alive
+    count_ref[...] = jnp.full(count_ref.shape, total, jnp.int32)
     pl.semaphore_wait(barrier, len(along_x) + len(along_y))
 
     def send(src, dst, send_sem, recv_sem, device):
@@ -209,12 +235,11 @@
     copies = [
         send(count_ref, first_ref.at[k], count_send.at[k], count_recv.at[k], along_x[k - 1]) for k in range(1, 8)
     ]
-    load_in.wait()
-    load_out.wait()
+    for load in loads[:5]:
+        load.wait()
+    prepare_weights(0, layers // 2, eye, gain_ref, shift_ref, w_in_ref, w_out_ref, wi_ref, wo_ref)
     for copy in copies:
         copy.wait()
-    row = lax.broadcasted_iota(jnp.int32, count_ref.shape, 0)
-    lane = lax.rem(lax.broadcasted_iota(jnp.int32, count_ref.shape, 1), 16)
     column = count_ref[...]
     for k in range(1, 8):
         column = jnp.where(row == 8 - k, first_ref[k], column)
@@ -223,48 +248,67 @@
         send(own_ref, second_ref.at[k], count_send.at[7 + k], count_recv.at[7 + k], along_y[k - 1])
         for k in range(1, 16)
     ]
-    prepare_weights(eye, gain_ref, shift_ref, w_in_ref, w_out_ref, wi_ref, wo_ref)
-    store_wi = pltpu.make_async_copy(wi_ref, wi_hbm, sems.at[1])
-    store_wo = pltpu.make_async_copy(wo_ref, wo_hbm, sems.at[2])
-    store_wi.start()
-    store_wo.start()
+    prepare_weights(layers // 2, layers, eye, gain_ref, shift_ref, w_in_ref, w_out_ref, wi_ref, wo_ref)
+    stores = [
+        pltpu.make_async_copy(wi_ref, wi_hbm, sems.at[2]),
+        pltpu.make_async_copy(wo_ref, wo_hbm, sems.at[3]),
+    ]
+    for store in stores:
+        store.start()
     for copy in copies:
         copy.wait()
     counts = column
     for k in range(1, 16):
-        counts = jnp.where(lane == 16 - k, second_ref[k], counts)
-
-    flow = make_plan(counts)
+        counts = jnp.where(lax.rem(lane, 16) == 16 - k, second_ref[k], counts)
+
+    flow = make_plan(jnp.maximum(counts - GROUP, 0))
     sent = jnp.zeros_like(counts)
     got = jnp.zeros_like(counts)
+    places = lax.broadcasted_iota(jnp.int32, pick_ref.shape, 0)
+    want = places - PLACES
+    left = jnp.full((1, 1), total, jnp.int32)
     for k, name in enumerate(PAIRS):
-        sent = jnp.where(row == k, pltpu.roll(jnp.maximum(flow[name], 0), k, 0), sent)
+        leaving = jnp.maximum(flow[name], 0)
+        sent = jnp.where(row == k, pltpu.roll(leaving, k, 0), sent)
         got = jnp.where(row == k, pltpu.roll(jnp.maximum(-flow[name], 0), k, 0), got)
+        base = BASES[name]
+        here = (places >= base) & (places < base + cap_of(name))
+        want = jnp.where(here, jnp.broadcast_to(left - 1, want.shape) - (places - base), want)
+        left = left - leaving[0:1, 0:1]
     plan_ref[0:8, :] = sent
     plan_ref[8:16, :] = got
-    to_smem = pltpu.make_async_copy(plan_ref, plan_smem, sems.at[3])
+    repeat = pick_ref.shape[0] // 8
+    hit = (jnp.concatenate([order] * repeat, axis=0) == want) & (jnp.concatenate([alive] * repeat, axis=0) > 0)
+    pick = jnp.where(hit, jnp.concatenate([lane] * repeat, axis=0), 0)
+    for by in (1, 2, 4, 8, 16, 32, 64):
+        pick = pick + pltpu.roll(pick, by, 1)
+    pick_ref[...] = pick
+    to_smem = pltpu.make_async_copy(pick_ref, pick_smem, sems.at[0])
     to_smem.start()
-    load_bricks.wait()
+    loads[5].wait()
     to_smem.wait()
 
-    last = list_ref[64] - 1
     copies = []
     for k, name in enumerate(PAIRS):
         for t in range(cap_of(name)):
-            slot = list_ref[jnp.clip(last - t, 0, 63)]
-            send_ref[BASES[name] + t] = bricks_ref[slot]
-        last = last - plan_smem[k, 0]
-        places = pl.ds(BASES[name], cap_of(name))
+            send_ref[BASES[name] + t] = bricks_ref[pick_smem[BASES[name] + t, 0]]
+        part = pl.ds(BASES[name], cap_of(name))
         copies.append(
-            send(send_ref.at[places], got_hbm.at[places], brick_send.at[k], brick_recv.at[k], partner_device(name))
+            send(send_ref.at[part], got_hbm.at[part], brick_send.at[k], brick_recv.at[k], partner_device(name))
         )
+    for t in range(GROUP):
+        s_ref[:, t * 512 : (t + 1) * 512] = transposed(eye, bricks_ref[pick_smem[PLACES + t, 0]])
+    feed_forward(s_ref, wi_ref, wo_ref, False)
+    for t in range(GROUP):
+        made = reduced(t, eye, s_ref, t_ref, w_down_ref)
+        early_ref[t] = made.reshape(early_ref.shape[1:]).astype(BF16)
     for copy in copies:
         copy.wait()
-    store_wi.wait()
-    store_wo.wait()
-
-
-def spread(listed, count, features, gain, shift, w_in, w_out):
+    for store in stores:
+        store.wait()
+
+
+def spread(owner, features, gain, shift, w_in, w_out, w_down):
     slots, voxels, chan = features.shape
     layers, _, hid = w_in.shape
     vmem = pl.BlockSpec(memory_space=pltpu.VMEM)
@@ -273,42 +317,51 @@
         spread_kernel,
         out_shape=(
             jax.ShapeDtypeStruct((16, 128), jnp.int32),
+            jax.ShapeDtypeStruct((GROUP, 128, chan), BF16),
             jax.ShapeDtypeStruct((PLACES, voxels, chan), BF16),
             jax.ShapeDtypeStruct((layers, hid, 2 * chan), BF16),
             jax.ShapeDtypeStruct((layers, chan, hid), BF16),
         ),
-        in_specs=[pl.BlockSpec(memory_space=pltpu.SMEM), vmem, hbm, vmem, vmem, hbm, hbm],
-        out_specs=(vmem, hbm, hbm, hbm),
+        in_specs=[pl.BlockSpec(memory_space=pltpu.SMEM)] + [hbm] * 6,
+        out_specs=(vmem, vmem, hbm, hbm, hbm),
         scratch_shapes=[
             pltpu.VMEM(features.shape, BF16),
             pltpu.VMEM((PLACES, voxels, chan), BF16),
+            pltpu.VMEM((8, 128), jnp.int32),
             pltpu.VMEM((8, 8, 128), jnp.int32),
             pltpu.VMEM((16, 8, 128), jnp.int32),
             pltpu.VMEM((8, 128), jnp.int32),
-            pltpu.SMEM((16, 128), jnp.int32),
+            pltpu.VMEM((32, 128), jnp.int32),
+            pltpu.SMEM((32, 128), jnp.int32),
+            pltpu.VMEM(gain.shape, F32),
+            pltpu.VMEM(shift.shape, F32),
             pltpu.VMEM(w_in.shape, BF16),
             pltpu.VMEM(w_out.shape, BF16),
+            pltpu.VMEM(w_down.shape, BF16),
             pltpu.VMEM((layers, hid, 2 * chan), BF16),
             pltpu.VMEM((layers, chan, hid), BF16),
-            pltpu.SemaphoreType.DMA((4,)),
+            pltpu.VMEM((chan, GROUP * voxels), F32),
+            pltpu.VMEM((GROUP, voxels, chan), F32),
+            pltpu.SemaphoreType.DMA((6,)),
             pltpu.SemaphoreType.DMA((23,)),
             pltpu.SemaphoreType.DMA((23,)),
             pltpu.SemaphoreType.DMA((7,)),
             pltpu.SemaphoreType.DMA((7,)),
         ],
         compiler_params=pltpu.CompilerParams(
-            collective_id=0, has_side_effects=True, vmem_limit_bytes=48 * 2**20
+            collective_id=0, has_side_effects=True, vmem_limit_bytes=FULL_VMEM
         ),
         name="spread",
-    )(listed, count, features, gain, shift, w_in, w_out)
+    )(owner, features, gain, shift, w_in, w_out, w_down)
 
 
 def coarse_kernel(
-    list_ref, plan_ref, features_ref, got_ref, wi_hbm, wo_hbm, w_down_hbm,
+    owner_ref, plan_ref, early_ref, features_ref, got_ref, wi_hbm, wo_hbm, w_down_hbm,
     out_ref, back_ref, map_ref,
-    place_ref, buf_ref, s_ref, t_ref, grid_ref, wi_ref, wo_ref, w_down_ref, sems, w_sems,
+    list_ref, place_ref, buf_ref, s_ref, t_ref, grid_ref, wi_ref, wo_ref, w_down_ref, sems, w_sems,
 ):
-    zcap = 16
+    cols_x, cols_y, zcap = owner_ref.shape
+    slots = cols_x * cols_y * zcap
     chan = s_ref.shape[0]
     eye = identity(chan)
     weights = [
@@ -318,12 +371,13 @@
     for w in weights:
         w.start()
 
-    def clear(k, _):
-        map_ref[k] = -1
-        return 0
-
-    lax.fori_loop(0, map_ref.shape[0], clear, 0)
-    kept, others = list_ref[64], 0
+    total = 0
+    for slot in range(slots):
+        column, r = divmod(slot, zcap)
+        map_ref[slot] = -1
+        list_ref[total] = slot
+        total = total + (owner_ref[column // cols_y, column % cols_y, r] >= 0).astype(jnp.int32)
+    kept, others = total, 0
     for k, name in enumerate(PAIRS):
         sent, came = plan_ref[k, 0], plan_ref[8 + k, 0]
         for t in range(cap_of(name)):
@@ -337,38 +391,48 @@
                 place_ref[others + t] = BASES[name] + t
 
         kept, others = kept - sent, others + came
-    total = kept + others
-    groups = (total + GROUP - 1) // GROUP
-
-    def copies(g, t):
-        k = jnp.minimum(g * GROUP + t, total - 1)
+    ours = jnp.maximum(kept - GROUP, 0)
+    work = ours + others
+    groups = (work + GROUP - 1) // GROUP
+
+    def fetch(g):
         half = lax.rem(g, 2)
-        own = pltpu.make_async_copy(features_ref.at[list_ref[jnp.clip(k, 0, 63)]], buf_ref.at[half, t], sems.at[half, t])
-        other = pltpu.make_async_copy(
-            got_ref.at[place_ref[jnp.clip(k - kept, 0, PLACES - 1)]], buf_ref.at[half, t], sems.at[half, t]
-        )
-        return k, own, other
-
-    def fetch(g):
         for t in range(GROUP):
-            k, own, other = copies(g, t)
-
-            @pl.when(k < kept)
+            k = jnp.minimum(g * GROUP + t, work - 1)
+
+            @pl.when(k < ours)
             def _():
-                own.start()
-
-            @pl.when(k >= kept)
+                slot = list_ref[GROUP + k]
+                pltpu.make_async_copy(features_ref.at[slot], buf_ref.at[half, t], sems.at[half, t]).start()
+
+            @pl.when(k >= ours)
             def _():
-                other.start()
+                place = place_ref[k - ours]
+                pltpu.make_async_copy(got_ref.at[place], buf_ref.at[half, t], sems.at[half, t]).start()
 
     @pl.when(groups > 0)
     def _():
         fetch(0)
 
     grid_ref[...] = jnp.zeros_like(grid_ref)
+    side = lax.broadcasted_iota(jnp.int32, (8, 1), 0) // 4
+
+    def put(slot, made):
+        column, r = slot // zcap, lax.rem(slot, zcap)
+        x0, y0, zpair, odd = (column // 2) * 4, lax.rem(column, 2) * 4, r // 2, lax.rem(r, 2)
+        for i in range(4):
+            for j in range(4):
+                old = grid_ref[x0 + i, y0 + j, zpair]
+                grid_ref[x0 + i, y0 + j, zpair] = jnp.where(side == odd, made[4 * i + j], old)
+
+    for t in range(GROUP):
+
+        @pl.when(t < total)
+        def _():
+            put(list_ref[t], early_ref[t].astype(F32).reshape(16, 8, chan))
+
     for w in weights:
         w.wait()
-    half = lax.broadcasted_iota(jnp.int32, (16, 8, 1), 1) // 4
 
     def body(g, _):
         @pl.when(g + 1 < groups)
@@ -379,40 +443,18 @@
             pltpu.make_async_copy(features_ref.at[0], buf_ref.at[lax.rem(g, 2), t], sems.at[lax.rem(g, 2), t]).wait()
         for t in range(GROUP):
             s_ref[:, t * 512 : (t + 1) * 512] = transposed(eye, buf_ref[lax.rem(g, 2), t])
-        feed_forward(s_ref, wi_ref, wo_ref)
+        feed_forward(s_ref, wi_ref, wo_ref, True)
         for t in range(GROUP):
-            for m in range(4):
-                block = s_ref[:, t * 512 + m * 128 : t * 512 + (m + 1) * 128].astype(BF16)
-                t_ref[t, m * 128 : (m + 1) * 128, :] = transposed(eye, block)
-        for t in range(GROUP):
-            total_down = jnp.zeros((128, 2 * chan), F32)
-            for a in range(2):
-                for c in range(2):
-                    rows = jnp.concatenate(
-                        [t_ref[t, pl.ds(128 * i + 64 * a + c, 32, stride=2), :] for i in range(4)], axis=0
-                    ).astype(BF16)
-                    both_b = jnp.concatenate([w_down_ref[a, 0, c], w_down_ref[a, 1, c]], axis=1)
-                    total_down += jnp.dot(rows, both_b, preferred_element_type=F32)
-            both = total_down.reshape(16, 8, 2 * chan)
-            own = jnp.where(half == 0, both[:, :, :chan], both[:, :, chan:])
-            down = own + jnp.concatenate([own[:, 4:, :], own[:, :4, :]], axis=1)
-            made = down / (1.0 + jnp.exp(-down))
+            made = reduced(t, eye, s_ref, t_ref, w_down_ref)
             k = g * GROUP + t
 
-            @pl.when(k < kept)
+            @pl.when(k < ours)
             def _():
-                slot = list_ref[jnp.minimum(k, 63)]
-                column, r = slot // zcap, lax.rem(slot, zcap)
-                x0, y0, zpair, odd = (column // 2) * 4, lax.rem(column, 2) * 4, r // 2, lax.rem(r, 2)
-                for i in range(4):
-                    for j in range(4):
-                        old = grid_ref[x0 + i, y0 + j, zpair]
-                        grid_ref[x0 + i, y0 + j, zpair] = jnp.where(half[0] == odd, made[4 * i + j], old)
-
-            @pl.when((k >= kept) & (k < total))
+                put(list_ref[GROUP + k], made)
+
+            @pl.when((k >= ours) & (k < work))
             def _():
-                place = place_ref[jnp.clip(k - kept, 0, PLACES - 1)]
-                back_ref[place] = made.reshape(128, chan).astype(BF16)
+                back_ref[place_ref[k - ours]] = made.reshape(128, chan).astype(BF16)
 
         return 0
 
@@ -425,7 +467,7 @@
     lax.fori_loop(0, out_ref.shape[0], finish, 0)
 
 
-def coarse_grid(listed, plan, features, got, wi, wo, w_down):
+def coarse_grid(owner, plan, early, features, got, wi, wo, w_down):
     slots, voxels, chan = features.shape
     vmem = pl.BlockSpec(memory_space=pltpu.VMEM)
     hbm = pl.BlockSpec(memory_space=pltpu.HBM)
@@ -437,9 +479,10 @@
             jax.ShapeDtypeStruct((PLACES, 128, chan), BF16),
             jax.ShapeDtypeStruct((slots,), jnp.int32),
         ),
-        in_specs=[smem, smem, hbm, hbm, hbm, hbm, hbm],
+        in_specs=[smem, smem, vmem, hbm, hbm, hbm, hbm, hbm],
         out_specs=(vmem, vmem, smem),
         scratch_shapes=[
+            pltpu.SMEM((2 * slots,), jnp.int32),
             pltpu.SMEM((PLACES,), jnp.int32),
             pltpu.VMEM((2, GROUP, voxels, chan), BF16),
             pltpu.VMEM((chan, GROUP * voxels), F32),
@@ -451,10 +494,10 @@
             pltpu.SemaphoreType.DMA((2, GROUP)),
             pltpu.SemaphoreType.DMA((3,)),
         ],
-        compiler_params=pltpu.CompilerParams(vmem_limit_bytes=48 * 2**20),
+        compiler_params=pltpu.CompilerParams(vmem_limit_bytes=62 * 2**20),
         cost_estimate=pl.CostEstimate(flops=17 * 10**9, bytes_accessed=8 * 2**20, transcendentals=10**8),
         name="coarse",
-    )(listed, plan, features, got, wi, wo, w_down)
+    )(owner, plan, early, features, got, wi, wo, w_down)
 
 
 def lift_kernel(
@@ -654,9 +697,8 @@
 def local(features, owner, norm_gain, time_shift, w_in, w_out, w_down, w_conv, w_up):
     cols_x, cols_y, zcap, voxels, chan = features.shape
     flat = features.reshape(cols_x * cols_y * zcap, voxels, chan)
-    listed, count = occupied(owner)
-    plan, got, wi, wo = spread(listed, count, flat, norm_gain, time_shift, w_in, w_out)
-    grid, back, where = coarse_grid(listed, plan, flat, got, wi, wo, w_down)
+    plan, early, got, wi, wo = spread(owner, flat, norm_gain, time_shift, w_in, w_out, w_down)
+    grid, back, where = coarse_grid(owner, plan, early, flat, got, wi, wo, w_down)
     result = lift(owner, with_rim(where, grid, back), flat, w_conv, w_up)
     return result.reshape(features.shape)
 

time: 118 us -> 107 us (0.907)
  Pallas kernels: 112 us -> 104 us
  local copies, waits for them, and re-layouts: 5.17 us -> 3.02 us
    pallas_call x1, Pallas kernels: 39 us -> 33.6 us  [coarse_grid(): pl.pallas_call(coarse_kernel, out_shape=(jax.ShapeDtypeStruct((8, 8, slot...]
    pallas_call x1 -> x0, Pallas kernels: 3.68 us -> none  [occupied(): pl.pallas_call(list_kernel, out_shape=(jax.ShapeDtypeStruct((128,), jnp.i...]
    unnamed x20 -> x12, local copies, waits for them, and re-layouts: 5.17 us -> 3.02 us
    pallas_call x1, Pallas kernels: 29.5 us -> 30.8 us  [spread(): pl.pallas_call(spread_kernel, out_shape=(jax.ShapeDtypeStruct((16, 128),...]
where the time goes in v4:
time: 107 us
  Pallas kernels  104 us (97%)
  local copies, waits for them, and re-layouts  3.02 us (3%)
    pallas_call x1, Pallas kernels, coarse_grid(): pl.pallas_call(coarse_kernel, out_shape=(jax.ShapeDtypeStruct((8, 8, slot...  33.6 us
    pallas_call x1, Pallas kernels, spread(): pl.pallas_call(spread_kernel, out_shape=(jax.ShapeDtypeStruct((16, 128),...  30.8 us
    pallas_call x1, Pallas kernels, with_rim(): pl.pallas_call(rim_kernel, out_shape=jax.ShapeDtypeStruct((gsx + 2, gsy +...  24.5 us
    pallas_call x1, Pallas kernels, lift(): pl.pallas_call(lift_kernel, grid=(columns,), out_shape=jax.ShapeDtypeStru...  14.7 us
    unnamed x12, local copies, waits for them, and re-layouts  3.02 us

profile of v4, /device:TPU:1, one launch (start us, length us, event | category | flops | bytes accessed | tf_op | source)
XLA Modules:
  0.0 106.7 jit_solution(5618424040798922027)
XLA Ops:
  0.0 30.8 %spread.1 = (s32[16,128]{1,0:T(8,128)}, bf16[3,128,128]{2,1,0:T(8,128)(2,1)}, bf16[22,512,128]{2,1,0:T(8,128)(2,1)}, bf16[8,512,256]{2,1,0:T(8,128)(2,1)}, bf16[8,128,512]{2,1,0:T(8,128)(2,1)}) custom-call(s32[2,2,16]{2,1,0:T(2,128)} %owner_ref.5, bf16[64,512,128]{2,1,0:T(8,128)(2,1)} %bitcast.2, f32[8,128]{1,0:T(8,128)} %gain_hbm.1, f32[8,512]{1,0:T(8,128)} %shift_hbm.1, ...), custom_call_target="tpu_custom_call" | custom-call | tf_op jit(solution)/shard_map/spread/pallas_call | solution.py:316
  30.8 0.0 copy-start.1
  30.8 0.0 copy-start.3
  30.8 33.6 %coarse.1 = (bf16[8,8,64,128]{3,2,1,0:T(8,128)(2,1)}, bf16[22,128,128]{2,1,0:T(8,128)(2,1)}, s32[64]{0:T(128)}) custom-call(s32[2,2,16]{2,1,0:T(2,128)} %owner_ref.5, s32[16,128]{1,0:T(8,128)} %get-tuple-element.13.plan_ref, bf16[3,128,128]{2,1,0:T(8,128)(2,1)} %get-tuple-element.14.early_ref, bf16[64,512,128]{2,1,0:T(8,128)(2,1)} %bitcast.3, ...), custom_call_target="tpu_custom_call" | custom-call | flops 16999999488 | bytes 8388608 | tf_op jit(solution)/shard_map/coarse/pallas_call | solution.py:475
  64.4 0.0 copy-start.4
  64.4 0.0 copy-start
  64.5 1.2 %copy-done = bf16[8,8,64,128]{3,2,1,0:T(8,128)(2,1)S(1)} copy-done((bf16[8,8,64,128]{3,2,1,0:T(8,128)(2,1)S(1)}, bf16[8,8,64,128]{3,2,1,0:T(8,128)(2,1)}, u32[]{:S(2)}) %copy-start) | copy-done | bytes 1048600
  65.7 0.0 copy-start.2
  65.7 1.1 %copy-done.2 = bf16[22,128,128]{2,1,0:T(8,128)(2,1)S(1)} copy-done((bf16[22,128,128]{2,1,0:T(8,128)(2,1)S(1)}, bf16[22,128,128]{2,1,0:T(8,128)(2,1)}, u32[]{:S(2)}) %copy-start.2) | copy-done | bytes 720920
  66.8 0.0 copy-start.5
  66.8 0.7 copy-done.5
  67.5 24.5 %rim.1.rim_ref = bf16[10,10,64,128]{3,2,1,0:T(8,128)(2,1)S(1)} custom-call(s32[64]{0:T(128)S(1)} %copy-done.5, bf16[8,8,64,128]{3,2,1,0:T(8,128)(2,1)S(1)} %copy-done, bf16[22,128,128]{2,1,0:T(8,128)(2,1)S(1)} %copy-done.2), custom_call_target="tpu_custom_call" | custom-call | tf_op jit(solution)/shard_map/rim/pallas_call | solution.py:679
  92.0 0.0 copy-done.1
  92.0 0.0 copy-done.3
  92.0 0.0 copy-done.4
  92.0 14.7 %lift.1 = bf16[64,512,128]{2,1,0:T(8,128)(2,1)} custom-call(s32[2,2,16]{2,1,0:T(2,128)S(1)} %copy-done.4, bf16[10,10,64,128]{3,2,1,0:T(8,128)(2,1)S(1)} %rim.1.rim_ref, bf16[64,512,128]{2,1,0:T(8,128)(2,1)} %bitcast.4, bf16[3,3,3,128,128]{4,3,2,1,0:T(8,128)(2,1)S(1)} %copy-done.1, bf16[2,2,2,128,128]{4,3,2,1,0:T(8,128)(2,1)S(1)} %copy-done.3), custom_call_target="tpu_custom_call" | custom-call | flops 5000000000 | bytes 18874368 | tf_op jit(solution)/shard_map/lift/pallas_call | solution.py:570
Async XLA Ops:
  30.8 61.2 %copy-start.1 = (bf16[3,3,3,128,128]{4,3,2,1,0:T(8,128)(2,1)S(1)}, bf16[3,3,3,128,128]{4,3,2,1,0:T(8,128)(2,1)}, u32[]{:S(2)}) copy-start(bf16[3,3,3,128,128]{4,3,2,1,0:T(8,128)(2,1)} %w_conv_ref.1) | copy-start | bytes 2654212
  30.8 61.2 %copy-start.3 = (bf16[2,2,2,128,128]{4,3,2,1,0:T(8,128)(2,1)S(1)}, bf16[2,2,2,128,128]{4,3,2,1,0:T(8,128)(2,1)}, u32[]{:S(2)}) copy-start(bf16[2,2,2,128,128]{4,3,2,1,0:T(8,128)(2,1)} %w_up_ref.1) | copy-start | bytes 786436
  64.4 27.6 %copy-start.4 = (s32[2,2,16]{2,1,0:T(2,128)S(1)}, s32[2,2,16]{2,1,0:T(2,128)}, u32[]{:S(2)}) copy-start(s32[2,2,16]{2,1,0:T(2,128)} %owner_ref.5) | copy-start | bytes 772
  64.4 1.2 %copy-start = (bf16[8,8,64,128]{3,2,1,0:T(8,128)(2,1)S(1)}, bf16[8,8,64,128]{3,2,1,0:T(8,128)(2,1)}, u32[]{:S(2)}) copy-start(bf16[8,8,64,128]{3,2,1,0:T(8,128)(2,1)} %get-tuple-element.19.grid_ref) | copy-start | bytes 3145732
  65.7 1.1 %copy-start.2 = (bf16[22,128,128]{2,1,0:T(8,128)(2,1)S(1)}, bf16[22,128,128]{2,1,0:T(8,128)(2,1)}, u32[]{:S(2)}) copy-start(bf16[22,128,128]{2,1,0:T(8,128)(2,1)} %get-tuple-element.20.back_ref) | copy-start | bytes 2162692
  66.8 0.7 copy-start.5

commit v5 on v4

--- a/solution.py
+++ b/solution.py
@@ -10,6 +10,7 @@
 BF16 = jnp.bfloat16
 F32 = jnp.float32
 GROUP = 3
+EARLY = 2 * GROUP
 CHUNK = 512
 
 
@@ -22,7 +23,7 @@
     return (rows == lax.broadcasted_iota(jnp.int32, (n, n), 1)).astype(BF16)
 
 
-def prepare_weights(first, last, eye, gain_ref, shift_ref, w_in_ref, w_out_ref, wi_ref, wo_ref):
+def prepare_weights(first, last, eye, gain_ref, shift_ref, w_in_ref, w_out_ref, w_ref):
     _, chan, hid = w_in_ref.shape
     row = lax.broadcasted_iota(jnp.int32, (chan, hid), 0)
 
@@ -37,9 +38,10 @@
         w_out = w_out_ref[l]
         for m in range(hid // chan):
             cut = slice(m * chan, (m + 1) * chan)
-            wi_ref[l, cut, :chan] = (transposed(eye, w_in[:, cut]) * gain).astype(BF16)
-            wi_ref[l, cut, chan:] = transposed(eye, parts[:, cut]).astype(BF16)
-            wo_ref[l, :, cut] = transposed(eye, w_out[cut, :]).astype(BF16)
+            w_ref[l, cut, :chan] = (transposed(eye, w_in[:, cut]) * gain).astype(BF16)
+            w_ref[l, cut, chan:] = transposed(eye, parts[:, cut]).astype(BF16)
+            rows = slice(hid + (m // 2) * chan, hid + (m // 2 + 1) * chan)
+            w_ref[l, rows, (m % 2) * chan : (m % 2 + 1) * chan] = transposed(eye, w_out[cut, :]).astype(BF16)
         return 0
 
     lax.fori_loop(first, last, one, 0)
@@ -52,41 +54,45 @@
     return (u * jnp.tanh(u) + u).astype(BF16)
 
 
-def feed_forward(s_ref, wi_ref, wo_ref, unrolled):
-    layers = wi_ref.shape[0]
+def feed_forward(s_ref, w_ref, first, last, between=None):
+    _, rows, _ = w_ref.shape
     chan, width = s_ref.shape
+    hid = rows - 2 * chan
     count = width // CHUNK
     ones = jnp.ones((chan, CHUNK), BF16)
 
     def hidden(l, c):
-        return hidden_units(s_ref[:, c * CHUNK : (c + 1) * CHUNK], ones, wi_ref[l])
+        return hidden_units(s_ref[:, c * CHUNK : (c + 1) * CHUNK], ones, w_ref[l, :hid, :])
 
     def update(l, c, h):
-        s_ref[:, c * CHUNK : (c + 1) * CHUNK] += jnp.dot(wo_ref[l], h, preferred_element_type=F32)
+        w_out = jnp.concatenate([w_ref[l, hid : hid + chan, :], w_ref[l, hid + chan :, :]], axis=1)
+        s_ref[:, c * CHUNK : (c + 1) * CHUNK] += jnp.dot(w_out, h, preferred_element_type=F32)
 
     def run(steps):
         held = hidden(*steps[0])
         for k, step in enumerate(steps):
             following = hidden(*steps[k + 1]) if k + 1 < len(steps) else None
+            if between is not None:
+                between(k)
             update(*step, held)
             held = following
 
-    if unrolled:
-        run([divmod(step, count) for step in range(layers * count)])
+    if between is not None:
+        run([divmod(step, count) for step in range(first * count, last * count)])
     else:
 
         def layer(l, _):
             run([(l, c) for c in range(count)])
             return 0
 
-        lax.fori_loop(0, layers, layer, 0)
-
-
-def reduced(t, eye, s_ref, t_ref, w_down_ref):
-    chan = s_ref.shape[0]
+        lax.fori_loop(first, last, layer, 0, unroll=2)
+
+
+def reduced(t, eye, last_ref, t_ref, w_down_ref):
+    chan = last_ref.shape[0]
     half = lax.broadcasted_iota(jnp.int32, (16, 8, 1), 1) // 4
     for m in range(4):
-        block = s_ref[:, t * 512 + m * 128 : t * 512 + (m + 1) * 128].astype(BF16)
+        block = last_ref[:, t * 512 + m * 128 : t * 512 + (m + 1) * 128]
         t_ref[t, m * 128 : (m + 1) * 128, :] = transposed(eye, block)
     total = jnp.zeros((128, 2 * chan), F32)
     for a in range(2):
@@ -107,6 +113,9 @@
 NEAR = 3
 SWEEPS = 3
 FULL_VMEM = 127 * 2**19
+COARSE_VMEM = 61 * 2**20
+RIM_VMEM = 484 * 2**17
+LIFT_VMEM = 62 * 2**20
 
 
 def cap_of(name):
@@ -177,9 +186,9 @@
 
 def spread_kernel(
     owner_ref, features_hbm, gain_hbm, shift_hbm, w_in_hbm, w_out_hbm, w_down_hbm,
-    plan_ref, early_ref, got_hbm, wi_hbm, wo_hbm,
-    bricks_ref, send_ref, count_ref, first_ref, second_ref, own_ref, pick_ref, pick_smem,
-    gain_ref, shift_ref, w_in_ref, w_out_ref, w_down_ref, wi_ref, wo_ref, s_ref, t_ref,
+    plan_ref, early_ref, got_hbm, w_hbm,
+    bricks_ref, send_ref, count_ref, first_ref, second_ref, own_ref, pick_ref, pick_smem, head_ref, head_smem,
+    gain_ref, shift_ref, w_in_ref, w_out_ref, w_down_ref, w_ref, s_ref, last_ref, t_ref,
     sems, count_send, count_recv, brick_send, brick_recv,
 ):
     gx, gy = lax.axis_index("gx"), lax.axis_index("gy")
@@ -222,6 +231,18 @@
         order = order + jnp.where(lane >= by, pltpu.roll(order, by, 1), 0)
     order = order - alive
     count_ref[...] = jnp.full(count_ref.shape, total, jnp.int32)
+
+    def slots_of(wanted):
+        repeat = wanted.shape[0] // 8
+        hit = (jnp.concatenate([order] * repeat, axis=0) == wanted) & (jnp.concatenate([alive] * repeat, axis=0) > 0)
+        slot = jnp.where(hit, jnp.concatenate([lane] * repeat, axis=0), 0)
+        for by in (1, 2, 4, 8, 16, 32, 64):
+            slot = slot + pltpu.roll(slot, by, 1)
+        return slot
+
+    head_ref[...] = slots_of(row)
+    head_to_smem = pltpu.make_async_copy(head_ref, head_smem, sems.at[6])
+    head_to_smem.start()
     pl.semaphore_wait(barrier, len(along_x) + len(along_y))
 
     def send(src, dst, send_sem, recv_sem, device):
@@ -237,7 +258,9 @@
     ]
     for load in loads[:5]:
         load.wait()
-    prepare_weights(0, layers // 2, eye, gain_ref, shift_ref, w_in_ref, w_out_ref, wi_ref, wo_ref)
+    prepare_weights(0, layers, eye, gain_ref, shift_ref, w_in_ref, w_out_ref, w_ref)
+    store = pltpu.make_async_copy(w_ref, w_hbm, sems.at[2])
+    store.start()
     for copy in copies:
         copy.wait()
     column = count_ref[...]
@@ -248,24 +271,33 @@
         send(own_ref, second_ref.at[k], count_send.at[7 + k], count_recv.at[7 + k], along_y[k - 1])
         for k in range(1, 16)
     ]
-    prepare_weights(layers // 2, layers, eye, gain_ref, shift_ref, w_in_ref, w_out_ref, wi_ref, wo_ref)
-    stores = [
-        pltpu.make_async_copy(wi_ref, wi_hbm, sems.at[2]),
-        pltpu.make_async_copy(wo_ref, wo_hbm, sems.at[3]),
-    ]
-    for store in stores:
-        store.start()
+    loads[5].wait()
+    head_to_smem.wait()
+
+    def begin(group):
+        for t in range(GROUP):
+            brick = bricks_ref[head_smem[group * GROUP + t, 0]]
+            s_ref[:, t * 512 : (t + 1) * 512] = transposed(eye, brick)
+
+    def end(group):
+        last_ref[...] = s_ref[...].astype(BF16)
+        for t in range(GROUP):
+            made = reduced(t, eye, last_ref, t_ref, w_down_ref)
+            early_ref[group * GROUP + t] = made.reshape(early_ref.shape[1:]).astype(BF16)
+
+    begin(0)
+    feed_forward(s_ref, w_ref, 0, layers // 2)
     for copy in copies:
         copy.wait()
     counts = column
     for k in range(1, 16):
         counts = jnp.where(lax.rem(lane, 16) == 16 - k, second_ref[k], counts)
 
-    flow = make_plan(jnp.maximum(counts - GROUP, 0))
+    flow = make_plan(jnp.maximum(counts - EARLY, 0))
     sent = jnp.zeros_like(counts)
     got = jnp.zeros_like(counts)
     places = lax.broadcasted_iota(jnp.int32, pick_ref.shape, 0)
-    want = places - PLACES
+    want = jnp.full_like(places, -1)
     left = jnp.full((1, 1), total, jnp.int32)
     for k, name in enumerate(PAIRS):
         leaving = jnp.maximum(flow[name], 0)
@@ -277,15 +309,9 @@
         left = left - leaving[0:1, 0:1]
     plan_ref[0:8, :] = sent
     plan_ref[8:16, :] = got
-    repeat = pick_ref.shape[0] // 8
-    hit = (jnp.concatenate([order] * repeat, axis=0) == want) & (jnp.concatenate([alive] * repeat, axis=0) > 0)
-    pick = jnp.where(hit, jnp.concatenate([lane] * repeat, axis=0), 0)
-    for by in (1, 2, 4, 8, 16, 32, 64):
-        pick = pick + pltpu.roll(pick, by, 1)
-    pick_ref[...] = pick
+    pick_ref[...] = slots_of(want)
     to_smem = pltpu.make_async_copy(pick_ref, pick_smem, sems.at[0])
     to_smem.start()
-    loads[5].wait()
     to_smem.wait()
 
     copies = []
@@ -296,16 +322,14 @@
         copies.append(
             send(send_ref.at[part], got_hbm.at[part], brick_send.at[k], brick_recv.at[k], partner_device(name))
         )
-    for t in range(GROUP):
-        s_ref[:, t * 512 : (t + 1) * 512] = transposed(eye, bricks_ref[pick_smem[PLACES + t, 0]])
-    feed_forward(s_ref, wi_ref, wo_ref, False)
-    for t in range(GROUP):
-        made = reduced(t, eye, s_ref, t_ref, w_down_ref)
-        early_ref[t] = made.reshape(early_ref.shape[1:]).astype(BF16)
+    feed_forward(s_ref, w_ref, layers // 2, layers)
+    end(0)
+    begin(1)
+    feed_forward(s_ref, w_ref, 0, layers)
+    end(1)
     for copy in copies:
         copy.wait()
-    for store in stores:
-        store.wait()
+    store.wait()
 
 
 def spread(owner, features, gain, shift, w_in, w_out, w_down):
@@ -317,13 +341,12 @@
         spread_kernel,
         out_shape=(
             jax.ShapeDtypeStruct((16, 128), jnp.int32),
-            jax.ShapeDtypeStruct((GROUP, 128, chan), BF16),
+            jax.ShapeDtypeStruct((EARLY, 128, chan), BF16),
             jax.ShapeDtypeStruct((PLACES, voxels, chan), BF16),
-            jax.ShapeDtypeStruct((layers, hid, 2 * chan), BF16),
-            jax.ShapeDtypeStruct((layers, chan, hid), BF16),
+            jax.ShapeDtypeStruct((layers, hid + 2 * chan, 2 * chan), BF16),
         ),
         in_specs=[pl.BlockSpec(memory_space=pltpu.SMEM)] + [hbm] * 6,
-        out_specs=(vmem, vmem, hbm, hbm, hbm),
+        out_specs=(vmem, vmem, hbm, hbm),
         scratch_shapes=[
             pltpu.VMEM(features.shape, BF16),
             pltpu.VMEM((PLACES, voxels, chan), BF16),
@@ -331,18 +354,20 @@
             pltpu.VMEM((8, 8, 128), jnp.int32),
             pltpu.VMEM((16, 8, 128), jnp.int32),
             pltpu.VMEM((8, 128), jnp.int32),
-            pltpu.VMEM((32, 128), jnp.int32),
-            pltpu.SMEM((32, 128), jnp.int32),
+            pltpu.VMEM((24, 128), jnp.int32),
+            pltpu.SMEM((24, 128), jnp.int32),
+            pltpu.VMEM((8, 128), jnp.int32),
+            pltpu.SMEM((8, 128), jnp.int32),
             pltpu.VMEM(gain.shape, F32),
             pltpu.VMEM(shift.shape, F32),
             pltpu.VMEM(w_in.shape, BF16),
             pltpu.VMEM(w_out.shape, BF16),
             pltpu.VMEM(w_down.shape, BF16),
-            pltpu.VMEM((layers, hid, 2 * chan), BF16),
-            pltpu.VMEM((layers, chan, hid), BF16),
+            pltpu.VMEM((layers, hid + 2 * chan, 2 * chan), BF16),
             pltpu.VMEM((chan, GROUP * voxels), F32),
+            pltpu.VMEM((chan, GROUP * voxels), BF16),
             pltpu.VMEM((GROUP, voxels, chan), F32),
-            pltpu.SemaphoreType.DMA((6,)),
+            pltpu.SemaphoreType.DMA((7,)),
             pltpu.SemaphoreType.DMA((23,)),
             pltpu.SemaphoreType.DMA((23,)),
             pltpu.SemaphoreType.DMA((7,)),
@@ -356,9 +381,9 @@
 
 
 def coarse_kernel(
-    owner_ref, plan_ref, early_ref, features_ref, got_ref, wi_hbm, wo_hbm, w_down_hbm,
+    owner_ref, plan_ref, early_ref, features_ref, got_ref, w_hbm, w_down_hbm,
     out_ref, back_ref, map_ref,
-    list_ref, place_ref, buf_ref, s_ref, t_ref, grid_ref, wi_ref, wo_ref, w_down_ref, sems, w_sems,
+    list_ref, place_ref, buf_ref, s_ref, last_ref, t_ref, made_ref, grid_ref, w_ref, w_down_ref, sems, w_sems,
 ):
     cols_x, cols_y, zcap = owner_ref.shape
     slots = cols_x * cols_y * zcap
@@ -366,7 +391,7 @@
     eye = identity(chan)
     weights = [
         pltpu.make_async_copy(src, dst, w_sems.at[n])
-        for n, (src, dst) in enumerate(((wi_hbm, wi_ref), (wo_hbm, wo_ref), (w_down_hbm, w_down_ref)))
+        for n, (src, dst) in enumerate(((w_hbm, w_ref), (w_down_hbm, w_down_ref)))
     ]
     for w in weights:
         w.start()
@@ -391,7 +416,7 @@
                 place_ref[others + t] = BASES[name] + t
 
         kept, others = kept - sent, others + came
-    ours = jnp.maximum(kept - GROUP, 0)
+    ours = jnp.maximum(kept - EARLY, 0)
     work = ours + others
     groups = (work + GROUP - 1) // GROUP
 
@@ -402,7 +427,7 @@
 
             @pl.when(k < ours)
             def _():
-                slot = list_ref[GROUP + k]
+                slot = list_ref[EARLY + k]
                 pltpu.make_async_copy(features_ref.at[slot], buf_ref.at[half, t], sems.at[half, t]).start()
 
             @pl.when(k >= ours)
@@ -425,7 +450,7 @@
                 old = grid_ref[x0 + i, y0 + j, zpair]
                 grid_ref[x0 + i, y0 + j, zpair] = jnp.where(side == odd, made[4 * i + j], old)
 
-    for t in range(GROUP):
+    for t in range(EARLY):
 
         @pl.when(t < total)
         def _():
@@ -433,6 +458,23 @@
 
     for w in weights:
         w.wait()
+
+    def reduce(t):
+        made_ref[t] = reduced(t, eye, last_ref, t_ref, w_down_ref)
+
+    def place_results(g):
+        for t in range(GROUP):
+            k = g * GROUP + t
+
+            @pl.when((k >= 0) & (k < ours))
+            def _():
+                put(list_ref[EARLY + k], made_ref[t])
+
+            @pl.when((k >= ours) & (k >= 0) & (k < work))
+            def _():
+                pair = made_ref[t].reshape(8, 2, 8, chan)
+                packed = jnp.where(side == 0, pair[:, 0], pair[:, 1])
+                back_ref[place_ref[k - ours]] = packed.reshape(64, chan).astype(BF16)
 
     def body(g, _):
         @pl.when(g + 1 < groups)
@@ -443,22 +485,23 @@
             pltpu.make_async_copy(features_ref.at[0], buf_ref.at[lax.rem(g, 2), t], sems.at[lax.rem(g, 2), t]).wait()
         for t in range(GROUP):
             s_ref[:, t * 512 : (t + 1) * 512] = transposed(eye, buf_ref[lax.rem(g, 2), t])
-        feed_forward(s_ref, wi_ref, wo_ref, True)
+
+        def between(step):
+            if step % 6 == 1 and step // 6 < GROUP:
+                reduce(step // 6)
+
+        feed_forward(s_ref, w_ref, 0, w_ref.shape[0], between)
+        last_ref[...] = s_ref[...].astype(BF16)
+        place_results(g - 1)
+        return 0
+
+    lax.fori_loop(0, groups, body, 0)
+
+    @pl.when(groups > 0)
+    def _():
         for t in range(GROUP):
-            made = reduced(t, eye, s_ref, t_ref, w_down_ref)
-            k = g * GROUP + t
-
-            @pl.when(k < ours)
-            def _():
-                put(list_ref[GROUP + k], made)
-
-            @pl.when((k >= ours) & (k < work))
-            def _():
-                back_ref[place_ref[k - ours]] = made.reshape(128, chan).astype(BF16)
-
-        return 0
-
-    lax.fori_loop(0, groups, body, 0)
+            reduce(t)
+        place_results(groups - 1)
 
     def finish(x, _):
         out_ref[x] = grid_ref[x].reshape(out_ref.shape[1:]).astype(BF16)
@@ -467,7 +510,7 @@
     lax.fori_loop(0, out_ref.shape[0], finish, 0)
 
 
-def coarse_grid(owner, plan, early, features, got, wi, wo, w_down):
+def coarse_grid(owner, plan, early, features, got, weights, w_down):
     slots, voxels, chan = features.shape
     vmem = pl.BlockSpec(memory_space=pltpu.VMEM)
     hbm = pl.BlockSpec(memory_space=pltpu.HBM)
@@ -476,28 +519,29 @@
         coarse_kernel,
         out_shape=(
             jax.ShapeDtypeStruct((8, 8, slots, chan), BF16),
-            jax.ShapeDtypeStruct((PLACES, 128, chan), BF16),
+            jax.ShapeDtypeStruct((PLACES, 64, chan), BF16),
             jax.ShapeDtypeStruct((slots,), jnp.int32),
         ),
-        in_specs=[smem, smem, vmem, hbm, hbm, hbm, hbm, hbm],
+        in_specs=[smem, smem, vmem, hbm, hbm, hbm, hbm],
         out_specs=(vmem, vmem, smem),
         scratch_shapes=[
             pltpu.SMEM((2 * slots,), jnp.int32),
             pltpu.SMEM((PLACES,), jnp.int32),
             pltpu.VMEM((2, GROUP, voxels, chan), BF16),
             pltpu.VMEM((chan, GROUP * voxels), F32),
+            pltpu.VMEM((chan, GROUP * voxels), BF16),
             pltpu.VMEM((GROUP, voxels, chan), F32),
+            pltpu.VMEM((GROUP, 16, 8, chan), F32),
             pltpu.VMEM((8, 8, slots // 8, 8, chan), F32),
-            pltpu.VMEM(wi.shape, BF16),
-            pltpu.VMEM(wo.shape, BF16),
+            pltpu.VMEM(weights.shape, BF16),
             pltpu.VMEM(w_down.shape, BF16),
             pltpu.SemaphoreType.DMA((2, GROUP)),
-            pltpu.SemaphoreType.DMA((3,)),
+            pltpu.SemaphoreType.DMA((2,)),
         ],
-        compiler_params=pltpu.CompilerParams(vmem_limit_bytes=62 * 2**20),
+        compiler_params=pltpu.CompilerParams(vmem_limit_bytes=COARSE_VMEM),
         cost_estimate=pl.CostEstimate(flops=17 * 10**9, bytes_accessed=8 * 2**20, transcendentals=10**8),
         name="coarse",
-    )(owner, plan, early, features, got, wi, wo, w_down)
+    )(owner, plan, early, features, got, weights, w_down)
 
 
 def lift_kernel(
@@ -525,13 +569,13 @@
                         )
         a_ref[...] = jnp.zeros_like(a_ref)
 
-    x0, y0 = p * 4, q * 4
     live = jnp.concatenate(
         [jnp.full((1, 16, chan), (owner_ref[p, q, r] >= 0).astype(F32)) for r in range(zcap)], axis=0
     )
     z = lax.rem(lax.broadcasted_iota(jnp.int32, (4 * gsz, 2 * chan), 0), gsz)
-    for pair in range(2):
-        y = y0 + 2 * pair
+
+    def mix(column, pair):
+        x0, y = (column // 2) * 4, lax.rem(column, 2) * 4 + 2 * pair
         total = jnp.zeros((4 * gsz, 6 * chan), F32)
         for d in range(3):
             rows = jnp.concatenate(
@@ -544,21 +588,32 @@
         for o in range(2):
             own = rim_ref[pl.ds(x0 + 1, 4), y + o + 1].reshape(4 * gsz, chan).astype(F32)
             mixed = summed[:, o * chan : (o + 1) * chan] + own
-            j = 2 * pair + o
-            a_ref[j, 0, pl.ds(0, 4 * gsz, stride=2), :] = mixed
-            a_ref[j, 1, pl.ds(1, 4 * gsz, stride=2), :] = mixed
-            spread = jnp.concatenate([a_ref[j, 0], a_ref[j, 1]], axis=1).astype(BF16)
+            a_ref[2 * pair + o, 0, pl.ds(0, 4 * gsz, stride=2), :] = mixed
+            a_ref[2 * pair + o, 1, pl.ds(1, 4 * gsz, stride=2), :] = mixed
+
+    def raise_up(pair):
+        for j in (2 * pair, 2 * pair + 1):
+            spread_out = jnp.concatenate([a_ref[j, 0], a_ref[j, 1]], axis=1).astype(BF16)
             for a in range(2):
                 weights = jnp.concatenate(
                     [jnp.concatenate([w_up_ref[a, b, c] for b in range(2)], axis=1) for c in range(2)], axis=0
                 )
-                upward = jnp.dot(spread, weights, preferred_element_type=F32)
+                upward = jnp.dot(spread_out, weights, preferred_element_type=F32)
                 for i in range(4):
                     part = upward[2 * gsz * i : 2 * gsz * (i + 1)].reshape(gsz // 4, 8, 2 * chan)
                     part = jnp.concatenate([part[:, :, :chan], part[:, :, chan:]], axis=1)
                     base = 128 * i + 64 * a + 16 * j
                     given = features_ref[:, base : base + 16, :].astype(F32)
                     out_ref[:, base : base + 16, :] = ((given + part) * live).astype(BF16)
+
+    @pl.when(step == 0)
+    def _():
+        mix(step, 0)
+
+    mix(step, 1)
+    raise_up(0)
+    mix(jnp.minimum(step + 1, pl.num_programs(0) - 1), 0)
+    raise_up(1)
 
 
 def lift(owner, rim, features, w_conv, w_up):
@@ -577,18 +632,20 @@
             pltpu.VMEM((3, 4 * chan, 6 * chan), BF16),
             pltpu.VMEM((4, 2, 8 * gsz, chan), F32),
         ],
-        compiler_params=pltpu.CompilerParams(vmem_limit_bytes=48 * 2**20),
+        compiler_params=pltpu.CompilerParams(vmem_limit_bytes=LIFT_VMEM),
         cost_estimate=pl.CostEstimate(flops=5 * 10**9, bytes_accessed=18 * 2**20, transcendentals=0),
         name="lift",
     )(owner, rim, features, w_conv, w_up)
 
 
 def rim_kernel(
-    map_ref, grid_ref, back_ref,
+    map_ref, grid_hbm, back_hbm,
     out_ref,
-    whole_ref, home_ref, send_sems, recv_sems,
+    grid_ref, whole_ref, home_ref, send_sems, recv_sems, load_sem,
 ):
     gsx, gsy, gsz, chan = grid_ref.shape
+    load = pltpu.make_async_copy(grid_hbm, grid_ref, load_sem)
+    load.start()
     gx, gy = lax.axis_index("gx"), lax.axis_index("gy")
     nx, ny = lax.axis_size("gx"), lax.axis_size("gy")
     sides = [(dx, dy) for dx in (-1, 0, 1) for dy in (-1, 0, 1) if (dx, dy) != (0, 0)]
@@ -611,27 +668,30 @@
     copies = []
     for k, name in enumerate(PAIRS):
         places = pl.ds(BASES[name], cap_of(name))
-        copies.append(send(len(sides) + k, back_ref.at[places], home_ref.at[places], partners[k]))
+        copies.append(send(len(sides) + k, back_hbm.at[places], home_ref.at[places], partners[k]))
+    load.wait()
     for copy in copies:
         copy.wait()
 
-    odd = lax.broadcasted_iota(jnp.int32, (16, 8, chan), 1) // 4
+    half = lax.broadcasted_iota(jnp.int32, (1, 8, chan), 1) // 4
     for column in range(4):
         x0, y0 = (column // 2) * 4, (column % 2) * 4
 
         def merge(m, _):
             zs = pl.ds(pl.multiple_of(m * 16, 16), 16)
-            old = grid_ref[x0 : x0 + 4, y0 : y0 + 4, zs, :].astype(F32).reshape(16, 16, chan)
+            old = grid_ref[x0 : x0 + 4, y0 : y0 + 4, zs, :].astype(F32).reshape(8, 2, 16, chan)
             new = []
             for pair in range(2):
-                value = old[:, 8 * pair : 8 * pair + 8, :]
+                first, second = old[:, 0, 8 * pair : 8 * pair + 8, :], old[:, 1, 8 * pair : 8 * pair + 8, :]
                 for side in range(2):
                     place = map_ref[column * 16 + m * 4 + 2 * pair + side]
-                    brick = home_ref[jnp.maximum(place, 0)].astype(F32).reshape(16, 8, chan)
-                    taken = jnp.full((16, 8, chan), place, jnp.int32) >= 0
-                    value = jnp.where(taken & (odd == side), brick, value)
-                new.append(value)
-            merged = jnp.concatenate(new, axis=1).reshape(4, 4, 16, chan).astype(BF16)
+                    brick = home_ref[jnp.maximum(place, 0)].astype(F32).reshape(8, 8, chan)
+                    other = jnp.concatenate([brick[:, 4:, :], brick[:, :4, :]], axis=1)
+                    taken = (jnp.full((1, 8, chan), place, jnp.int32) >= 0) & (half == side)
+                    first = jnp.where(taken, brick if side == 0 else other, first)
+                    second = jnp.where(taken, other if side == 0 else brick, second)
+                new.append(jnp.stack([first, second], axis=1))
+            merged = jnp.concatenate(new, axis=2).reshape(4, 4, 16, chan).astype(BF16)
             whole_ref[x0 : x0 + 4, y0 : y0 + 4, zs, :] = merged
             return 0
 
@@ -676,19 +736,22 @@
 def with_rim(where, grid, back):
     gsx, gsy, gsz, chan = grid.shape
     vmem = pl.BlockSpec(memory_space=pltpu.VMEM)
+    hbm = pl.BlockSpec(memory_space=pltpu.HBM)
     return pl.pallas_call(
         rim_kernel,
         out_shape=jax.ShapeDtypeStruct((gsx + 2, gsy + 2, gsz, chan), BF16),
-        in_specs=[pl.BlockSpec(memory_space=pltpu.SMEM), vmem, vmem],
+        in_specs=[pl.BlockSpec(memory_space=pltpu.SMEM), hbm, hbm],
         out_specs=vmem,
         scratch_shapes=[
+            pltpu.VMEM(grid.shape, BF16),
             pltpu.VMEM(grid.shape, BF16),
             pltpu.VMEM(back.shape, BF16),
             pltpu.SemaphoreType.DMA((15,)),
             pltpu.SemaphoreType.DMA((15,)),
+            pltpu.SemaphoreType.DMA,
         ],
         compiler_params=pltpu.CompilerParams(
-            collective_id=1, has_side_effects=True, vmem_limit_bytes=32 * 2**20
+            collective_id=1, has_side_effects=True, vmem_limit_bytes=RIM_VMEM
         ),
         name="rim",
     )(where, grid, back)
@@ -697,8 +760,8 @@
 def local(features, owner, norm_gain, time_shift, w_in, w_out, w_down, w_conv, w_up):
     cols_x, cols_y, zcap, voxels, chan = features.shape
     flat = features.reshape(cols_x * cols_y * zcap, voxels, chan)
-    plan, early, got, wi, wo = spread(owner, flat, norm_gain, time_shift, w_in, w_out, w_down)
-    grid, back, where = coarse_grid(owner, plan, early, flat, got, wi, wo, w_down)
+    plan, early, got, weights = spread(owner, flat, norm_gain, time_shift, w_in, w_out, w_down)
+    grid, back, where = coarse_grid(owner, plan, early, flat, got, weights, w_down)
     result = lift(owner, with_rim(where, grid, back), flat, w_conv, w_up)
     return result.reshape(features.shape)
 

time: 107 us -> 95.2 us (0.89)
  Pallas kernels: 104 us -> 95 us
  local copies, waits for them, and re-layouts: 3.02 us -> 0 us
    pallas_call x1, Pallas kernels: 24.5 us -> 16.9 us  [with_rim(): pl.pallas_call(rim_kernel, out_shape=jax.ShapeDtypeStruct((gsx + 2, gsy +...]
    unnamed x12 -> x0, local copies, waits for them, and re-layouts: 3.02 us -> none
    pallas_call x1, Pallas kernels: 30.8 us -> 33.4 us  [spread(): pl.pallas_call(spread_kernel, out_shape=(jax.ShapeDtypeStruct((16, 128),...]
    pallas_call x1, Pallas kernels: 33.6 us -> 31.3 us  [coarse_grid(): pl.pallas_call(coarse_kernel, out_shape=(jax.ShapeDtypeStruct((8, 8, slot...]
    pallas_call x1, Pallas kernels: 14.7 us -> 13.4 us  [lift(): pl.pallas_call(lift_kernel, grid=(columns,), out_shape=jax.ShapeDtypeStru...]
where the time goes in v5:
time: 95.2 us; the launch traced here: 95 us
  Pallas kernels  95 us (100%)
    pallas_call x1, Pallas kernels, spread(): pl.pallas_call(spread_kernel, out_shape=(jax.ShapeDtypeStruct((16, 128),...  33.4 us
    pallas_call x1, Pallas kernels, coarse_grid(): pl.pallas_call(coarse_kernel, out_shape=(jax.ShapeDtypeStruct((8, 8, slot...  31.3 us
    pallas_call x1, Pallas kernels, with_rim(): pl.pallas_call(rim_kernel, out_shape=jax.ShapeDtypeStruct((gsx + 2, gsy +...  16.9 us
    pallas_call x1, Pallas kernels, lift(): pl.pallas_call(lift_kernel, grid=(columns,), out_shape=jax.ShapeDtypeStru...  13.4 us

profile of v5, /device:TPU:1, one launch (start us, length us, event | category | flops | bytes accessed | tf_op | source)
XLA Modules:
  0.0 95.0 jit_solution(9826962202054552531)
XLA Ops:
  0.0 33.4 %spread.1 = (s32[16,128]{1,0:T(8,128)}, bf16[6,128,128]{2,1,0:T(8,128)(2,1)}, bf16[22,512,128]{2,1,0:T(8,128)(2,1)}, bf16[8,768,256]{2,1,0:T(8,128)(2,1)}) custom-call(s32[2,2,16]{2,1,0:T(2,128)} %owner_ref.5, bf16[64,512,128]{2,1,0:T(8,128)(2,1)} %bitcast.2, f32[8,128]{1,0:T(8,128)} %gain_hbm.1, f32[8,512]{1,0:T(8,128)} %shift_hbm.1, ...), custom_call_target="tpu_custom_call" | custom-call | tf_op jit(solution)/shard_map/spread/pallas_call | solution.py:340
  33.4 31.3 %coarse.1 = (bf16[8,8,64,128]{3,2,1,0:T(8,128)(2,1)}, bf16[22,64,128]{2,1,0:T(8,128)(2,1)}, s32[64]{0:T(128)}) custom-call(s32[2,2,16]{2,1,0:T(2,128)} %owner_ref.5, s32[16,128]{1,0:T(8,128)} %get-tuple-element.12.plan_ref, bf16[6,128,128]{2,1,0:T(8,128)(2,1)} %get-tuple-element.13.early_ref, bf16[64,512,128]{2,1,0:T(8,128)(2,1)} %bitcast.3, ...), custom_call_target="tpu_custom_call" | custom-call | flops 16999999488 | bytes 8388608 | tf_op jit(solution)/shard_map/coarse/pallas_call | solution.py:518
  64.7 16.9 %rim.1.rim_ref = bf16[10,10,64,128]{3,2,1,0:T(8,128)(2,1)} custom-call(s32[64]{0:T(128)} %get-tuple-element.16.map_ref, bf16[8,8,64,128]{3,2,1,0:T(8,128)(2,1)} %get-tuple-element.17.grid_hbm, bf16[22,64,128]{2,1,0:T(8,128)(2,1)} %get-tuple-element.18.back_hbm), custom_call_target="tpu_custom_call" | custom-call | tf_op jit(solution)/shard_map/rim/pallas_call | solution.py:740
  81.6 13.4 %lift.1 = bf16[64,512,128]{2,1,0:T(8,128)(2,1)} custom-call(s32[2,2,16]{2,1,0:T(2,128)} %owner_ref.5, bf16[10,10,64,128]{3,2,1,0:T(8,128)(2,1)} %rim.1.rim_ref, bf16[64,512,128]{2,1,0:T(8,128)(2,1)} %bitcast.4, bf16[3,3,3,128,128]{4,3,2,1,0:T(8,128)(2,1)} %w_conv_ref.1, bf16[2,2,2,128,128]{4,3,2,1,0:T(8,128)(2,1)} %w_up_ref.1), custom_call_target="tpu_custom_call" | custom-call | flops 5000000000 | bytes 18874368 | tf_op jit(solution)/shard_map/lift/pallas_call | solution.py:625

commit v6 on v5

--- a/solution.py
+++ b/solution.py
@@ -23,46 +23,52 @@
     return (rows == lax.broadcasted_iota(jnp.int32, (n, n), 1)).astype(BF16)
 
 
-def prepare_weights(first, last, eye, gain_ref, shift_ref, w_in_ref, w_out_ref, w_ref):
-    _, chan, hid = w_in_ref.shape
-    row = lax.broadcasted_iota(jnp.int32, (chan, hid), 0)
+def shift_parts(shift):
+    high = shift.astype(BF16).astype(F32)
+    mid = (shift - high).astype(BF16).astype(F32)
+    low = shift - high - mid
+    rest = jnp.zeros((128 - 3 * shift.shape[0], shift.shape[1]), F32)
+    return jnp.concatenate([high, mid, low, rest], axis=0).astype(BF16)
+
+
+def prepare_weights(eye, gain_ref, shift_ref, w_in_ref, w_out_ref, w_ref):
+    layers, chan, hid = w_in_ref.shape
+    parts = shift_parts(shift_ref[...] * 0.5)
+    columns = [transposed(eye, parts[:, m * chan : (m + 1) * chan]).astype(BF16) for m in range(hid // chan)]
 
     def one(l, _):
         gain = gain_ref[pl.ds(l, 1), :] * 0.5
-        shift = shift_ref[pl.ds(l, 1), :] * 0.5
-        high = shift.astype(BF16).astype(F32)
-        mid = (shift - high).astype(BF16).astype(F32)
-        low = shift - high - mid
-        parts = jnp.where(row == 0, high, jnp.where(row == 1, mid, jnp.where(row == 2, low, 0.0))).astype(BF16)
         w_in = w_in_ref[l]
-        w_out = w_out_ref[l]
+        w_out = transposed(eye, w_out_ref[l]).astype(BF16)
         for m in range(hid // chan):
             cut = slice(m * chan, (m + 1) * chan)
             w_ref[l, cut, :chan] = (transposed(eye, w_in[:, cut]) * gain).astype(BF16)
-            w_ref[l, cut, chan:] = transposed(eye, parts[:, cut]).astype(BF16)
-            rows = slice(hid + (m // 2) * chan, hid + (m // 2 + 1) * chan)
-            w_ref[l, rows, (m % 2) * chan : (m % 2 + 1) * chan] = transposed(eye, w_out[cut, :]).astype(BF16)
+            w_ref[l, cut, chan:] = columns[m]
+        w_ref[l, hid : hid + chan, :] = w_out[:, : 2 * chan]
+        w_ref[l, hid + chan :, :] = w_out[:, 2 * chan :]
         return 0
 
-    lax.fori_loop(first, last, one, 0)
-
-
-def hidden_units(x, ones, wi):
+    lax.fori_loop(0, layers, one, 0, unroll=2)
+
+
+def hidden_units(x, chosen, wi):
     scale = lax.rsqrt(jnp.mean(x * x, axis=0, keepdims=True) + 1e-06)
-    normed = jnp.concatenate([(x * scale).astype(BF16), ones], axis=0)
+    normed = jnp.concatenate([(x * scale).astype(BF16), chosen], axis=0)
     u = jnp.dot(wi, normed, preferred_element_type=F32)
     return (u * jnp.tanh(u) + u).astype(BF16)
 
 
 def feed_forward(s_ref, w_ref, first, last, between=None):
-    _, rows, _ = w_ref.shape
+    layers, rows, _ = w_ref.shape
     chan, width = s_ref.shape
     hid = rows - 2 * chan
     count = width // CHUNK
-    ones = jnp.ones((chan, CHUNK), BF16)
+    row = lax.broadcasted_iota(jnp.int32, (chan, 128), 0)
 
     def hidden(l, c):
-        return hidden_units(s_ref[:, c * CHUNK : (c + 1) * CHUNK], ones, w_ref[l, :hid, :])
+        chosen = ((lax.rem(row, layers) == l) & (row < 3 * layers)).astype(F32).astype(BF16)
+        chosen = jnp.concatenate([chosen] * (CHUNK // 128), axis=1)
+        return hidden_units(s_ref[:, c * CHUNK : (c + 1) * CHUNK], chosen, w_ref[l, :hid, :])
 
     def update(l, c, h):
         w_out = jnp.concatenate([w_ref[l, hid : hid + chan, :], w_ref[l, hid + chan :, :]], axis=1)
@@ -85,7 +91,7 @@
             run([(l, c) for c in range(count)])
             return 0
 
-        lax.fori_loop(first, last, layer, 0, unroll=2)
+        lax.fori_loop(first, last, layer, 0, unroll=8)
 
 
 def reduced(t, eye, last_ref, t_ref, w_down_ref):
@@ -116,6 +122,7 @@
 COARSE_VMEM = 61 * 2**20
 RIM_VMEM = 484 * 2**17
 LIFT_VMEM = 62 * 2**20
+FIRST_CUT, SECOND_CUT = 2, 6
 
 
 def cap_of(name):
@@ -258,9 +265,23 @@
     ]
     for load in loads[:5]:
         load.wait()
-    prepare_weights(0, layers, eye, gain_ref, shift_ref, w_in_ref, w_out_ref, w_ref)
+    prepare_weights(eye, gain_ref, shift_ref, w_in_ref, w_out_ref, w_ref)
     store = pltpu.make_async_copy(w_ref, w_hbm, sems.at[2])
     store.start()
+    loads[5].wait()
+    head_to_smem.wait()
+
+    def begin(group):
+        for t in range(GROUP):
+            brick = bricks_ref[head_smem[group * GROUP + t, 0]]
+            s_ref[:, t * 512 : (t + 1) * 512] = transposed(eye, brick)
+
+    def end(group, t):
+        made = reduced(t, eye, last_ref, t_ref, w_down_ref)
+        early_ref[group * GROUP + t] = made.reshape(early_ref.shape[1:]).astype(BF16)
+
+    begin(0)
+    feed_forward(s_ref, w_ref, 0, FIRST_CUT)
     for copy in copies:
         copy.wait()
     column = count_ref[...]
@@ -271,22 +292,7 @@
         send(own_ref, second_ref.at[k], count_send.at[7 + k], count_recv.at[7 + k], along_y[k - 1])
         for k in range(1, 16)
     ]
-    loads[5].wait()
-    head_to_smem.wait()
-
-    def begin(group):
-        for t in range(GROUP):
-            brick = bricks_ref[head_smem[group * GROUP + t, 0]]
-            s_ref[:, t * 512 : (t + 1) * 512] = transposed(eye, brick)
-
-    def end(group):
-        last_ref[...] = s_ref[...].astype(BF16)
-        for t in range(GROUP):
-            made = reduced(t, eye, last_ref, t_ref, w_down_ref)
-            early_ref[group * GROUP + t] = made.reshape(early_ref.shape[1:]).astype(BF16)
-
-    begin(0)
-    feed_forward(s_ref, w_ref, 0, layers // 2)
+    feed_forward(s_ref, w_ref, FIRST_CUT, SECOND_CUT)
     for copy in copies:
         copy.wait()
     counts = column
@@ -322,11 +328,15 @@
         copies.append(
             send(send_ref.at[part], got_hbm.at[part], brick_send.at[k], brick_recv.at[k], partner_device(name))
         )
-    feed_forward(s_ref, w_ref, layers // 2, layers)
-    end(0)
+    feed_forward(s_ref, w_ref, SECOND_CUT, layers)
+    last_ref[...] = s_ref[...].astype(BF16)
+    for t in range(GROUP):
+        end(0, t)
     begin(1)
     feed_forward(s_ref, w_ref, 0, layers)
-    end(1)
+    last_ref[...] = s_ref[...].astype(BF16)
+    for t in range(GROUP):
+        end(1, t)
     for copy in copies:
         copy.wait()
     store.wait()
@@ -406,14 +416,9 @@
     for k, name in enumerate(PAIRS):
         sent, came = plan_ref[k, 0], plan_ref[8 + k, 0]
         for t in range(cap_of(name)):
-
-            @pl.when(t < sent)
-            def _():
-                map_ref[list_ref[kept - 1 - t]] = BASES[name] + t
-
-            @pl.when(t < came)
-            def _():
-                place_ref[others + t] = BASES[name] + t
+            slot = list_ref[jnp.maximum(kept - 1 - t, 0)]
+            map_ref[jnp.where(t < sent, slot, slots)] = BASES[name] + t
+            place_ref[others + t] = BASES[name] + t
 
         kept, others = kept - sent, others + came
     ours = jnp.maximum(kept - EARLY, 0)
@@ -520,13 +525,13 @@
         out_shape=(
             jax.ShapeDtypeStruct((8, 8, slots, chan), BF16),
             jax.ShapeDtypeStruct((PLACES, 64, chan), BF16),
-            jax.ShapeDtypeStruct((slots,), jnp.int32),
+            jax.ShapeDtypeStruct((2 * slots,), jnp.int32),
         ),
         in_specs=[smem, smem, vmem, hbm, hbm, hbm, hbm],
         out_specs=(vmem, vmem, smem),
         scratch_shapes=[
             pltpu.SMEM((2 * slots,), jnp.int32),
-            pltpu.SMEM((PLACES,), jnp.int32),
+            pltpu.SMEM((2 * PLACES,), jnp.int32),
             pltpu.VMEM((2, GROUP, voxels, chan), BF16),
             pltpu.VMEM((chan, GROUP * voxels), F32),
             pltpu.VMEM((chan, GROUP * voxels), BF16),
@@ -695,7 +700,7 @@
             whole_ref[x0 : x0 + 4, y0 : y0 + 4, zs, :] = merged
             return 0
 
-        lax.fori_loop(0, gsz // 16, merge, 0)
+        lax.fori_loop(0, gsz // 16, merge, 0, unroll=True)
 
     def cut(side, size):
         return {-1: pl.ds(0, 1), 0: pl.ds(0, size), 1: pl.ds(size - 1, 1)}[side]

time: 95.2 us -> 93.5 us (0.982)
  Pallas kernels: 95 us -> 93.3 us
    pallas_call x1, Pallas kernels: 33.4 us -> 30.7 us  [spread(): pl.pallas_call(spread_kernel, out_shape=(jax.ShapeDtypeStruct((16, 128),...]
    pallas_call x1, Pallas kernels: 16.9 us -> 18.1 us  [with_rim(): pl.pallas_call(rim_kernel, out_shape=jax.ShapeDtypeStruct((gsx + 2, gsy +...]
where the time goes in v6:
time: 93.5 us; the launch traced here: 93.3 us
  Pallas kernels  93.3 us (100%)
    pallas_call x1, Pallas kernels, coarse_grid(): pl.pallas_call(coarse_kernel, out_shape=(jax.ShapeDtypeStruct((8, 8, slot...  31.1 us
    pallas_call x1, Pallas kernels, spread(): pl.pallas_call(spread_kernel, out_shape=(jax.ShapeDtypeStruct((16, 128),...  30.7 us
    pallas_call x1, Pallas kernels, with_rim(): pl.pallas_call(rim_kernel, out_shape=jax.ShapeDtypeStruct((gsx + 2, gsy +...  18.1 us
    pallas_call x1, Pallas kernels, lift(): pl.pallas_call(lift_kernel, grid=(columns,), out_shape=jax.ShapeDtypeStru...  13.4 us

profile of v6, /device:TPU:1, one launch (start us, length us, event | category | flops | bytes accessed | tf_op | source)
XLA Modules:
  0.0 93.3 jit_solution(11308056002574653870)
XLA Ops:
  0.0 30.7 %spread.1 = (s32[16,128]{1,0:T(8,128)}, bf16[6,128,128]{2,1,0:T(8,128)(2,1)}, bf16[22,512,128]{2,1,0:T(8,128)(2,1)}, bf16[8,768,256]{2,1,0:T(8,128)(2,1)}) custom-call(s32[2,2,16]{2,1,0:T(2,128)} %owner_ref.5, bf16[64,512,128]{2,1,0:T(8,128)(2,1)} %bitcast.2, f32[8,128]{1,0:T(8,128)} %gain_hbm.1, f32[8,512]{1,0:T(8,128)} %shift_hbm.1, ...), custom_call_target="tpu_custom_call" | custom-call | tf_op jit(solution)/shard_map/spread/pallas_call | solution.py:350
  30.7 31.1 %coarse.1 = (bf16[8,8,64,128]{3,2,1,0:T(8,128)(2,1)}, bf16[22,64,128]{2,1,0:T(8,128)(2,1)}, s32[128]{0:T(128)}) custom-call(s32[2,2,16]{2,1,0:T(2,128)} %owner_ref.5, s32[16,128]{1,0:T(8,128)} %get-tuple-element.12.plan_ref, bf16[6,128,128]{2,1,0:T(8,128)(2,1)} %get-tuple-element.13.early_ref, bf16[64,512,128]{2,1,0:T(8,128)(2,1)} %bitcast.3, ...), custom_call_target="tpu_custom_call" | custom-call | flops 16999999488 | bytes 8388608 | tf_op jit(solution)/shard_map/coarse/pallas_call | solution.py:523
  61.8 18.1 %rim.1.rim_ref = bf16[10,10,64,128]{3,2,1,0:T(8,128)(2,1)} custom-call(s32[128]{0:T(128)} %get-tuple-element.16.map_ref, bf16[8,8,64,128]{3,2,1,0:T(8,128)(2,1)} %get-tuple-element.17.grid_hbm, bf16[22,64,128]{2,1,0:T(8,128)(2,1)} %get-tuple-element.18.back_hbm), custom_call_target="tpu_custom_call" | custom-call | tf_op jit(solution)/shard_map/rim/pallas_call | solution.py:745
  79.9 13.4 %lift.1 = bf16[64,512,128]{2,1,0:T(8,128)(2,1)} custom-call(s32[2,2,16]{2,1,0:T(2,128)} %owner_ref.5, bf16[10,10,64,128]{3,2,1,0:T(8,128)(2,1)} %rim.1.rim_ref, bf16[64,512,128]{2,1,0:T(8,128)(2,1)} %bitcast.4, bf16[3,3,3,128,128]{4,3,2,1,0:T(8,128)(2,1)} %w_conv_ref.1, bf16[2,2,2,128,128]{4,3,2,1,0:T(8,128)(2,1)} %w_up_ref.1), custom_call_target="tpu_custom_call" | custom-call | flops 5000000000 | bytes 18874368 | tf_op jit(solution)/shard_map/lift/pallas_call | solution.py:630

commit v7 on v6

--- a/solution.py
+++ b/solution.py
@@ -653,7 +653,7 @@
     load.start()
     gx, gy = lax.axis_index("gx"), lax.axis_index("gy")
     nx, ny = lax.axis_size("gx"), lax.axis_size("gy")
-    sides = [(dx, dy) for dx in (-1, 0, 1) for dy in (-1, 0, 1) if (dx, dy) != (0, 0)]
+    sides = [(0, -1), (0, 1), (-1, 0), (1, 0), (-1, -1), (-1, 1), (1, -1), (1, 1)]
     devices = [(lax.rem(gx + dx + nx, nx), lax.rem(gy + dy + ny, ny)) for dx, dy in sides]
     partners = [partner_device(name) for name in PAIRS]
 
@@ -678,8 +678,24 @@
     for copy in copies:
         copy.wait()
 
+    def cut(side, size):
+        return {-1: pl.ds(0, 1), 0: pl.ds(0, size), 1: pl.ds(size - 1, 1)}[side]
+
+    def place_of(side, size):
+        return {-1: pl.ds(size + 1, 1), 0: pl.ds(1, size), 1: pl.ds(0, 1)}[side]
+
+    def send_side(n):
+        dx, dy = sides[n]
+        return send(
+            n,
+            whole_ref.at[cut(dx, gsx), cut(dy, gsy)],
+            out_ref.at[place_of(dx, gsx), place_of(dy, gsy)],
+            devices[n],
+        )
+
     half = lax.broadcasted_iota(jnp.int32, (1, 8, chan), 1) // 4
-    for column in range(4):
+    copies = []
+    for column in (0, 2, 1, 3):
         x0, y0 = (column // 2) * 4, (column % 2) * 4
 
         def merge(m, _):
@@ -701,22 +717,10 @@
             return 0
 
         lax.fori_loop(0, gsz // 16, merge, 0, unroll=True)
-
-    def cut(side, size):
-        return {-1: pl.ds(0, 1), 0: pl.ds(0, size), 1: pl.ds(size - 1, 1)}[side]
-
-    def place_of(side, size):
-        return {-1: pl.ds(size + 1, 1), 0: pl.ds(1, size), 1: pl.ds(0, 1)}[side]
-
-    copies = [
-        send(
-            n,
-            whole_ref.at[cut(dx, gsx), cut(dy, gsy)],
-            out_ref.at[place_of(dx, gsx), place_of(dy, gsy)],
-            devices[n],
-        )
-        for n, (dx, dy) in enumerate(sides)
-    ]
+        if column == 2:
+            copies.append(send_side(0))
+
+    copies.extend(send_side(n) for n in range(1, len(sides)))
     out_ref[pl.ds(1, gsx), pl.ds(1, gsy)] = whole_ref[...]
     for copy in copies:
         copy.wait()

time: 93.5 us -> 93.4 us (level)
  no operation moved by 1% of the time
where the time goes in v7:
time: 93.4 us; the launch traced here: 93.1 us
  Pallas kernels  93.1 us (100%)
    pallas_call x1, Pallas kernels, coarse_grid(): pl.pallas_call(coarse_kernel, out_shape=(jax.ShapeDtypeStruct((8, 8, slot...  31.1 us
    pallas_call x1, Pallas kernels, spread(): pl.pallas_call(spread_kernel, out_shape=(jax.ShapeDtypeStruct((16, 128),...  30.7 us
    pallas_call x1, Pallas kernels, with_rim(): pl.pallas_call(rim_kernel, out_shape=jax.ShapeDtypeStruct((gsx + 2, gsy +...  17.9 us
    pallas_call x1, Pallas kernels, lift(): pl.pallas_call(lift_kernel, grid=(columns,), out_shape=jax.ShapeDtypeStru...  13.4 us

profile of v7, /device:TPU:1, one launch (start us, length us, event | category | flops | bytes accessed | tf_op | source)
XLA Modules:
  0.0 93.1 jit_solution(4688542793182891508)
XLA Ops:
  0.0 30.7 %spread.1 = (s32[16,128]{1,0:T(8,128)}, bf16[6,128,128]{2,1,0:T(8,128)(2,1)}, bf16[22,512,128]{2,1,0:T(8,128)(2,1)}, bf16[8,768,256]{2,1,0:T(8,128)(2,1)}) custom-call(s32[2,2,16]{2,1,0:T(2,128)} %owner_ref.5, bf16[64,512,128]{2,1,0:T(8,128)(2,1)} %bitcast.2, f32[8,128]{1,0:T(8,128)} %gain_hbm.1, f32[8,512]{1,0:T(8,128)} %shift_hbm.1, ...), custom_call_target="tpu_custom_call" | custom-call | tf_op jit(solution)/shard_map/spread/pallas_call | solution.py:350
  30.7 31.1 %coarse.1 = (bf16[8,8,64,128]{3,2,1,0:T(8,128)(2,1)}, bf16[22,64,128]{2,1,0:T(8,128)(2,1)}, s32[128]{0:T(128)}) custom-call(s32[2,2,16]{2,1,0:T(2,128)} %owner_ref.5, s32[16,128]{1,0:T(8,128)} %get-tuple-element.12.plan_ref, bf16[6,128,128]{2,1,0:T(8,128)(2,1)} %get-tuple-element.13.early_ref, bf16[64,512,128]{2,1,0:T(8,128)(2,1)} %bitcast.3, ...), custom_call_target="tpu_custom_call" | custom-call | flops 16999999488 | bytes 8388608 | tf_op jit(solution)/shard_map/coarse/pallas_call | solution.py:523
  61.8 17.9 %rim.1.rim_ref = bf16[10,10,64,128]{3,2,1,0:T(8,128)(2,1)} custom-call(s32[128]{0:T(128)} %get-tuple-element.16.map_ref, bf16[8,8,64,128]{3,2,1,0:T(8,128)(2,1)} %get-tuple-element.17.grid_hbm, bf16[22,64,128]{2,1,0:T(8,128)(2,1)} %get-tuple-element.18.back_hbm), custom_call_target="tpu_custom_call" | custom-call | tf_op jit(solution)/shard_map/rim/pallas_call | solution.py:749
  79.7 13.4 %lift.1 = bf16[64,512,128]{2,1,0:T(8,128)(2,1)} custom-call(s32[2,2,16]{2,1,0:T(2,128)} %owner_ref.5, bf16[10,10,64,128]{3,2,1,0:T(8,128)(2,1)} %rim.1.rim_ref, bf16[64,512,128]{2,1,0:T(8,128)(2,1)} %bitcast.4, bf16[3,3,3,128,128]{4,3,2,1,0:T(8,128)(2,1)} %w_conv_ref.1, bf16[2,2,2,128,128]{4,3,2,1,0:T(8,128)(2,1)} %w_up_ref.1), custom_call_target="tpu_custom_call" | custom-call | flops 5000000000 | bytes 18874368 | tf_op jit(solution)/shard_map/lift/pallas_call | solution.py:630
